TPU v7x, 512 devices: a whole 4x8x8 slice. The times are simulated.
512 devices in a mesh: gz: 64 (over x, z, core), gy: 8 (over y).
Axes of the slice: x: 4, y: 8, z: 8, core: 2. Of those that a mesh axis runs over, the one named last changes fastest.
Arguments:
- volume: bfloat16 [16, 512, 64, 128], P(None, 'gz', 'gy'), may hold values from -6 to 6
- kernel_full: bfloat16 [3, 3, 3, 16, 16], replicated, may hold values from -0.3125 to 0.3125
- kernel_half: bfloat16 [3, 3, 3, 16, 32], replicated, may hold values from -0.3125 to 0.3125
- kernel_quarter: bfloat16 [3, 3, 3, 32, 64], replicated, may hold values from -0.21875 to 0.21875
- kernel_eighth: bfloat16 [3, 3, 3, 64, 128], replicated, may hold values from -0.15625 to 0.15625
- skip_full: bfloat16 [16, 512, 64, 128], P(None, 'gz', 'gy'), may hold values from -0.03125 to 0.03125
- skip_half: bfloat16 [32, 256, 32, 64], P(None, 'gz', 'gy'), may hold values from -0.078125 to 0.078125
- skip_quarter: bfloat16 [64, 128, 16, 32], P(None, 'gz', 'gy'), may hold values from -0.25 to 0.25
- skip_eighth: bfloat16 [128, 64, 8, 16], P(None, 'gz', 'gy'), may hold values from -0.625 to 0.625
Outputs:
- grad_full: float32 [3, 3, 3, 16, 16], replicated
- grad_half: float32 [3, 3, 3, 16, 32], replicated
- grad_quarter: float32 [3, 3, 3, 32, 64], replicated
- grad_eighth: float32 [3, 3, 3, 64, 128], replicated
All inputs are finite; a program needn't handle non-finite values.
Results may differ from a plain program's by a relative error of at most 0.0041.
Values may be sent and summed in bfloat16 or wider, within the bound.
No kernel may reach another device: no remote copies, remote signals or barrier semaphores. Data moves between devices by JAX's collectives and lax.ppermute only.
A program may use at most 64 MiB of HBM per device.

v0:
```python
import jax
import jax.numpy as jnp
from jax import lax
from jax.sharding import PartitionSpec as P


def padded_2(array, sides, width):
    for axis, dim in sides:
        devices, length = (lax.axis_size(axis), array.shape[dim])
        up = [(i, (i + 1) % devices) for i in range(devices - 1)]
        down = [(j, i) for i, j in up]
        last = lax.slice_in_dim(array, length - width, length, axis=dim)
        initial = lax.slice_in_dim(array, 0, width, axis=dim)
        before = lax.ppermute(last, axis, up)
        after = lax.ppermute(initial, axis, down)
        array = jnp.concatenate([before, array, after], axis=dim)
    return array


def pad_columns(inputs):
    return jnp.pad(inputs, ((0, 0), (0, 0), (0, 0), (1, 1)))


def act_rims(inputs):
    return padded_2(pad_columns(inputs), (("gz", 1), ("gy", 2)), 1)


def grad_rims(inputs):
    return padded_2(pad_columns(inputs), (("gz", 1), ("gy", 2)), 1)


def convolve(padded, kernel):
    return lax.conv_general_dilated(
        padded[None],
        kernel,
        (1, 1, 1),
        "VALID",
        dimension_numbers=("NCDHW", "DHWIO", "NCDHW"),
        preferred_element_type=jnp.float32,
    )[0]


def transposed(padded_grad, kernel):
    return convolve(padded_grad, jnp.swapaxes(jnp.flip(kernel, (0, 1, 2)), 3, 4))


def weight_term(padded, gradient):
    product = lax.conv_general_dilated(
        padded[:, None],
        gradient[None],
        (1, 1, 1),
        "VALID",
        dimension_numbers=("NCDHW", "IODHW", "NCDHW"),
        preferred_element_type=jnp.float32,
    )
    return jnp.transpose(product, (2, 3, 4, 0, 1))


def shrink(preact):
    chans, depth, height, width = preact.shape
    blocks = jax.nn.silu(preact).reshape(chans, depth // 2, 2, height // 2, 2, width // 2, 2)
    return jnp.mean(blocks, axis=(2, 4, 6)).astype(jnp.bfloat16)


def spread_up(carried):
    chans, depth, height, width = carried.shape
    grown = jnp.broadcast_to(
        carried[:, :, None, :, None, :, None], (chans, depth, 2, height, 2, width, 2)
    )
    return grown.reshape(chans, 2 * depth, 2 * height, 2 * width) * 0.125


def slope(preact):
    sig = jax.nn.sigmoid(preact)
    return sig * (1.0 + preact * (1.0 - sig))


def on_device(
    volume,
    kernel_full,
    kernel_half,
    kernel_quarter,
    kernel_eighth,
    skip_full,
    skip_half,
    skip_quarter,
    skip_eighth,
):
    kernels = [kernel_full, kernel_half, kernel_quarter, kernel_eighth]
    skips = [skip_full, skip_half, skip_quarter, skip_eighth]
    inputs = volume
    paddings = []
    preacts = []
    spread_levels = 3
    for level_index in range(spread_levels):
        padded = act_rims(inputs)
        preact = convolve(padded, kernels[level_index])
        paddings.append(padded)
        preacts.append(preact)
        inputs = shrink(preact)
    terms = [None, None, None]
    padded = act_rims(inputs)
    preact = convolve(padded, kernel_eighth)
    gradient = (skip_eighth.astype(jnp.float32) * slope(preact)).astype(jnp.bfloat16)
    deep_term = weight_term(padded, gradient)
    carried = transposed(grad_rims(gradient), kernel_eighth)
    levels_left = (2, 1, 0)
    for level_index in levels_left:
        upstream = skips[level_index].astype(jnp.float32) + spread_up(carried)
        gradient = (upstream * slope(preacts[level_index])).astype(jnp.bfloat16)
        terms[level_index] = weight_term(paddings[level_index], gradient)
        if level_index > 0:
            carried = transposed(grad_rims(gradient), kernels[level_index])
    grad_zero, grad_one, grad_two, grad_three = lax.psum(
        (terms[0], terms[1], terms[2], deep_term), ("gz", "gy")
    )
    return (grad_zero, grad_one, grad_two, grad_three)


def solution(mesh):
    in_specs = (
        P(None, "gz", "gy", None),
        P(),
        P(),
        P(),
        P(),
        P(None, "gz", "gy", None),
        P(None, "gz", "gy", None),
        P(None, "gz", "gy", None),
        P(None, "gz", "gy", None),
    )
    out_specs = (P(), P(), P(), P())
    return jax.shard_map(
        on_device, mesh=mesh, in_specs=in_specs, out_specs=out_specs, check_vma=False
    )
```

profile of v0, /device:TPU:1, one launch (start us, length us, event | category | flops | bytes accessed | tf_op | source)
XLA Modules:
  0.0 850.5 jit_solution(15225772303860362800)
XLA Ops:
  8.5 5.4 collective-permute-start
  13.9 4.7 collective-permute-start.1
  19.5 3.2 collective-permute-start.2
  24.2 3.7 collective-permute-done.3
  28.3 3.5 reshape.102
  31.8 7.9 copy.259
  40.8 9.3 %broadcast_select_fusion = f32[8,8,8,17,16]{4,2,3,1,0:T(8,128)} fusion(pred[8,17]{0,1:T(8,128)(4,1)S(1)} %copy-done.13, bf16[3,3,3,16,16]{4,3,2,1,0:T(8,128)(2,1)S(1)} %copy-done.11, bf16[16,10,10,1,7,2]{0,4,5,2,1,3:T(8,128)(2,1)S(1)} %slice.95, bf16[16,10,10,1,8,17]{0,4,5,2,1,3:T(8,128)(2,1)} %copy.259), kind=kOutput, calls=%fused_computation.8 | convolution fusion | flops 121922560 | bytes 1051016 | tf_op jit(solution)/shard_map/conv_general_dilated | solution.py:33
  50.1 6.4 copy.260
  56.6 3.3 reshape.106
  62.6 5.2 copy.263
  68.5 3.3 collective-permute-start.4
  74.0 3.4 collective-permute-done.5
  77.6 3.2 collective-permute-start.6
  82.5 3.4 collective-permute-done.7
  101.3 3.1 collective-permute-done.9
  104.5 4.9 collective-permute-start.10
  110.6 3.7 collective-permute-done.11
  118.0 3.6 collective-permute-start.12
  123.7 4.0 collective-permute-start.14
  131.0 5.3 collective-permute-start.16
  138.4 4.6 collective-permute-start.18
  144.3 5.0 collective-permute-start.20
  154.5 3.9 collective-permute-start.22
  159.7 10.8 %copy.298 = bf16[16,1,10,10,130]{0,1,4,3,2:T(2,128)(2,1)} copy(bf16[16,1,10,10,130]{4,0,3,2,1:T(8,128)(2,1)S(1)} %get-tuple-element.9) | data formatting | bytes 832000 | tf_op jit(solution)/shard_map/broadcast_in_dim | solution.py:49
  175.3 3.8 collective-permute-start.24
  184.9 4.3 collective-permute-start.26
  190.6 8.2 fusion.117
  202.4 4.1 broadcast_in_dim.73
  209.8 7.2 copy.299
  217.1 51.0 %fusion.116 = f32[3,3,3,16,16]{4,3,2,1,0:T(8,128)} fusion(bf16[16,1,10,10,130]{0,1,4,3,2:T(2,128)(2,1)} %copy.298, bf16[1,16,8,8,128]{1,0,4,3,2:T(2,128)(2,1)} %copy.299), kind=kOutput, calls=%fused_computation.168 | convolution fusion | flops 113246208 | bytes 705792 | tf_op jit(solution)/shard_map/transpose | solution.py:56
  269.9 288.9 %all-reduce.12.cloned.1.call-done = (f32[3,3,3,16,16]{4,3,2,1,0:T(8,128)}, f32[3,3,3,16,32]{4,3,2,1,0:T(8,128)}) async-done(((f32[3,3,3,16,16]{4,3,2,1,0:T(8,128)}, f32[3,3,3,16,32]{4,3,2,1,0:T(8,128)}), (f32[3,3,3,16,16]{4,3,2,1,0:T(8,128)}, f32[3,3,3,16,32]{4,3,2,1,0:T(8,128)})) %all-reduce.12.cloned.1.call-update) | async-done | bytes 82960 | tf_op jit(solution)/shard_map/psum | solution.py:114
  558.8 277.4 %all-reduce.14.cloned.1.call-done = (f32[3,3,3,32,64]{4,3,2,1,0:T(8,128)}, f32[3,3,3,64,128]{4,3,2,1,0:T(8,128)}) async-done(((f32[3,3,3,32,64]{4,3,2,1,0:T(8,128)}, f32[3,3,3,64,128]{4,3,2,1,0:T(8,128)}), (f32[3,3,3,32,64]{4,3,2,1,0:T(8,128)}, f32[3,3,3,64,128]{4,3,2,1,0:T(8,128)})) %all-reduce.14.cloned.1.call-update) | async-done | bytes 1105936 | tf_op jit(solution)/shard_map/psum | solution.py:114
  (183 shorter events, 75.3 us)
Async XLA Ops:
  7.2 121.6 %copy-start = (bf16[3,3,3,64,128]{4,3,2,1,0:T(8,128)(2,1)S(1)}, bf16[3,3,3,64,128]{4,3,2,1,0:T(8,128)(2,1)}, u32[]{:S(2)}) copy-start(bf16[3,3,3,64,128]{4,3,2,1,0:T(8,128)(2,1)} %param.13) | copy-start | bytes 1327108
  7.2 551.6 %all-reduce.12.cloned.1.call-start = ((), (), s32[]{:S(2)}) async-start(), calls=%async_computation | async-start | bytes 884736 | tf_op jit(solution)/shard_map/psum | solution.py:114
  8.5 10.3 %collective-permute-start = (bf16[16,1,8,130]{3,0,2,1:T(8,128)(2,1)S(1)}, bf16[16,1,8,130]{3,0,2,1:T(8,128)(2,1)S(1)}, u32[]{:S(2)}, u32[]{:S(2)}) collective-permute-start(bf16[16,1,8,130]{3,0,2,1:T(8,128)(2,1)S(1)} %get-tuple-element.14), channel_id=1, source_target_pairs={{0,8},{8,16},{16,24},{24,32},{32,40},{40,48},{48,56},{56,64},{64,7... | collective-permute-start | bytes 99848 | tf_op jit(solution)/shard_map/ppermute | solution.py:14
  13.9 5.6 collective-permute-start.1
  19.5 4.7 collective-permute-start.2
  22.7 5.2 collective-permute-start.3
  68.5 5.5 collective-permute-start.4
  71.8 5.7 collective-permute-start.5
  77.6 5.0 collective-permute-start.6
  80.8 5.2 collective-permute-start.7
  96.3 5.0 collective-permute-start.8
  99.3 5.1 collective-permute-start.9
  104.5 6.2 collective-permute-start.10
  109.3 5.0 collective-permute-start.11
  116.1 5.6 collective-permute-start.13
  118.0 4.4 collective-permute-start.12
  122.4 5.3 collective-permute-start.15
  123.7 4.9 collective-permute-start.14
  129.1 7.3 collective-permute-start.17
  131.0 6.1 collective-permute-start.16
  137.1 5.9 collective-permute-start.19
  138.4 5.4 collective-permute-start.18
  144.3 7.0 collective-permute-start.20
  149.4 5.1 collective-permute-start.21
  154.5 18.5 %collective-permute-start.22 = (bf16[64,4,1,34]{0,3,2,1:T(8,128)(2,1)S(1)}, bf16[64,4,1,34]{0,3,2,1:T(8,128)(2,1)S(1)}, u32[]{:S(2)}, u32[]{:S(2)}) collective-permute-start(bf16[64,4,1,34]{0,3,2,1:T(8,128)(2,1)S(1)} %get-tuple-element.26), channel_id=1, source_target_pairs={{0,1},{1,2},{2,3},{3,4},{4,5},{5,6},{6,7},{8,9},{9,10},{10,11},{11... | collective-permute-start | bytes 52232 | tf_op jit(solution)/shard_map/ppermute | solution.py:14
  158.4 14.5 %collective-permute-start.23 = (bf16[64,4,1,34]{0,3,2,1:T(8,128)(2,1)S(1)}, bf16[64,4,1,34]{0,3,2,1:T(8,128)(2,1)S(1)}, u32[]{:S(2)}, u32[]{:S(2)}) collective-permute-start(bf16[64,4,1,34]{0,3,2,1:T(8,128)(2,1)S(1)} %get-tuple-element.27), channel_id=1, source_target_pairs={{1,0},{2,1},{3,2},{4,3},{5,4},{6,5},{7,6},{9,8},{10,9},{11,10},{12... | collective-permute-start | bytes 52232 | tf_op jit(solution)/shard_map/ppermute | solution.py:15
  175.3 7.5 collective-permute-start.24
  179.1 5.7 collective-permute-start.25
  184.9 13.9 %collective-permute-start.26 = (bf16[32,6,1,66]{3,0,2,1:T(8,128)(2,1)S(1)}, bf16[32,6,1,66]{3,0,2,1:T(8,128)(2,1)S(1)}, u32[]{:S(2)}, u32[]{:S(2)}) collective-permute-start(bf16[32,6,1,66]{3,0,2,1:T(8,128)(2,1)S(1)} %get-tuple-element.16), channel_id=1, source_target_pairs={{0,1},{1,2},{2,3},{3,4},{4,5},{5,6},{6,7},{8,9},{9,10},{10,11},{11... | collective-permute-start | bytes 76040 | tf_op jit(solution)/shard_map/ppermute | solution.py:14
  189.1 9.7 %collective-permute-start.27 = (bf16[32,6,1,66]{3,0,2,1:T(8,128)(2,1)S(1)}, bf16[32,6,1,66]{3,0,2,1:T(8,128)(2,1)S(1)}, u32[]{:S(2)}, u32[]{:S(2)}) collective-permute-start(bf16[32,6,1,66]{3,0,2,1:T(8,128)(2,1)S(1)} %get-tuple-element.17), channel_id=1, source_target_pairs={{1,0},{2,1},{3,2},{4,3},{5,4},{6,5},{7,6},{9,8},{10,9},{11,10},{12... | collective-permute-start | bytes 76040 | tf_op jit(solution)/shard_map/ppermute | solution.py:15
  268.1 568.1 %all-reduce.14.cloned.1.call-start = ((), (), s32[]{:S(2)}) async-start(), calls=%async_computation.1 | async-start | bytes 2654208 | tf_op jit(solution)/shard_map/psum | solution.py:114
  268.1 575.3 %copy-start.1 = (bf16[3,3,3,64,128]{4,3,2,1,0:T(8,128)(2,1)S(1)}, bf16[3,3,3,64,128]{4,3,2,1,0:T(8,128)(2,1)}, u32[]{:S(2)}) copy-start(bf16[3,3,3,64,128]{4,3,2,1,0:T(8,128)(2,1)} %param.13) | copy-start | bytes 1327108
  (15 other events, 331.6 us)
Sparse Core Ops, SparseCore 0:
  268.2 290.5 all-reduce.11
  565.2 270.9 all-reduce.13
where the time goes:
time: 860 us; the launch traced here: 850 us
  waiting for transfers between devices  593 us (69%)
  starting transfers between devices  83.4 us (10%)
  local copies, waits for them, and re-layouts  77.7 us (9%)
  matrix products  77.6 us (9%)
  between operations  15.4 us (2%)
    psum x2, waiting for transfers between devices, on_device(): lax.psum((terms[0], terms[1], terms[2], deep_term), ('gz', 'gy'))  566 us
    transpose x4, matrix products, weight_term(): return jnp.transpose(product, (2, 3, 4, 0, 1))  62.2 us
    ppermute x14, starting transfers between devices, padded_2(): before = lax.ppermute(last, axis, up)  57.4 us
    conv_general_dilated x29, local copies, waits for them, and re-layouts, convolve(): lax.conv_general_dilated(padded[None], kernel, (1, 1, 1), 'VALID', dimens...  31.1 us
    ppermute x14, starting transfers between devices, padded_2(): after = lax.ppermute(initial, axis, down)  25.9 us
    ppermute x14, waiting for transfers between devices, padded_2(): after = lax.ppermute(initial, axis, down)  23.2 us
  transfers between devices with their start and end apart: 30, of which 15 were waited for; matrix products, arithmetic and copies ran while one was open for 3% of the time, Pallas kernels for 0%

commit v1 on v0

v1 whole, which is shorter than its diff:
```python
import jax
import jax.numpy as jnp
from jax import lax
from jax.experimental import pallas as pl
from jax.experimental.pallas import tpu as pltpu
from jax.sharding import PartitionSpec as P

F32 = jnp.float32
BF16 = jnp.bfloat16
GZ = ("x", "z", "c")
VMEM_BYTES = 14 * 1024 * 1024
HALF = (256, 640)
NT = (((1,), (1,)), ((), ()))


def call(body, outs, scratch, flops, *args):
    return pl.pallas_call(
        body,
        out_shape=tuple(jax.ShapeDtypeStruct(shape, dtype) for shape, dtype in outs),
        in_specs=[pl.BlockSpec(memory_space=pltpu.VMEM) for _ in args],
        out_specs=tuple(pl.BlockSpec(memory_space=pltpu.VMEM) for _ in outs),
        scratch_shapes=[pltpu.VMEM(shape, dtype) for shape, dtype in scratch],
        compiler_params=pltpu.CompilerParams(vmem_limit_bytes=VMEM_BYTES),
        cost_estimate=pl.CostEstimate(flops=flops, bytes_accessed=1 << 20, transcendentals=0),
    )(*args)


def place_of():
    depth_at, row_at = lax.axis_index(GZ), lax.axis_index("gy")
    return (
        depth_at > 0,
        depth_at < lax.axis_size(GZ) - 1,
        row_at > 0,
        row_at < lax.axis_size("gy") - 1,
        lax.axis_index("c"),
        row_at,
    )


def lanes(shape):
    return lax.broadcasted_iota(jnp.int32, shape, 1)


def at_column(tile, step):
    if step == 0:
        return tile
    moved = pltpu.roll(tile.astype(F32), (-step) % 128, 1)
    edge = 127 if step > 0 else 0
    return jnp.where(lanes(tile.shape) == edge, 0.0, moved).astype(BF16)


def put_shifts(shifts, row, layer, tile):
    for step in range(3):
        shifts[step, row : row + tile.shape[0], layer * 128 : layer * 128 + 128] = at_column(
            tile, step - 1
        )


def convolved(weights, shifts, rows, depth):
    total = None
    for down in range(3):
        for step in range(3):
            window = shifts[step, rows[0] : rows[1], down * 128 : (down + depth) * 128]
            tap = weights[down * 3 + step]
            term = jnp.dot(
                tap[:, : rows[1] - rows[0]], window, preferred_element_type=F32
            )
            total = term if total is None else total + term
    return total


def sigmoid(values):
    return 1.0 / (1.0 + jnp.exp(-values))


def slope(values):
    sig = sigmoid(values)
    return sig * (1.0 + values * (1.0 - sig))


def exact_dot(values, picks):
    high = values.astype(BF16)
    rest = values - high.astype(F32)
    middle = rest.astype(BF16)
    low = (rest - middle.astype(F32)).astype(BF16)
    total = jnp.dot(low, picks, preferred_element_type=F32)
    total = total + jnp.dot(middle, picks, preferred_element_type=F32)
    return total + jnp.dot(high, picks, preferred_element_type=F32)


def pair_columns(down):
    rows = lax.broadcasted_iota(jnp.int32, (128, 128), 0)
    columns = lax.broadcasted_iota(jnp.int32, (128, 128), 1)
    hit = (rows // 2 == columns) if down else (columns // 2 == rows)
    return jnp.where(hit, 0.125, 0.0).astype(BF16)


def pooled(first, second, channels, width):
    both = first + second
    blocks = both.shape[0] // (2 * channels)
    rows = []
    for block in range(blocks):
        start = 2 * block * channels
        rows.append(
            both[start : start + channels] + both[start + channels : start + 2 * channels]
        )
    summed = rows[0] if blocks == 1 else jnp.concatenate(rows, axis=0)
    mean = exact_dot(summed, pair_columns(True))
    return jnp.where(lanes(mean.shape) < width // 2, mean, 0.0)


def silu(values):
    return values * sigmoid(values)


def prepare(kernels, dims):
    def body(*refs):
        ins, outs, wide = refs[:4], refs[4:11], refs[11]
        for level, (rows, chans, feats) in enumerate(dims):
            source, taps = ins[level][...], outs[level]
            picks = (
                lax.broadcasted_iota(jnp.int32, (feats, 128), 0)
                == lax.broadcasted_iota(jnp.int32, (feats, 128), 1) % feats
            )
            spread = jnp.dot(
                source, jnp.where(picks, 1.0, 0.0).astype(BF16), preferred_element_type=F32
            )
            size = taps.shape[2]
            place = lanes((chans, 128)) // feats
            for down in range(3):
                for step in range(3):
                    wide[...] = jnp.zeros_like(wide)
                    for row in range(rows + 2):
                        value = jnp.zeros((chans, 128), F32)
                        for across in range(3):
                            at = ((down * 3 + across) * 3 + step) * chans
                            value = jnp.where(
                                place == row - across, spread[at : at + chans], value
                            )
                        wide[row * chans : (row + 1) * chans, :] = value
                    taps[down * 3 + step] = wide[:size, :].T.astype(BF16)
        for level in range(1, 4):
            rows, chans, feats = dims[level]
            if level == 2:
                rows = 4
            source, taps = ins[level][...], outs[3 + level]
            size = (rows + 2) * feats
            picks = (
                lax.broadcasted_iota(jnp.int32, (feats, size), 0)
                == lax.broadcasted_iota(jnp.int32, (feats, size), 1) % feats
            )
            spread = jnp.dot(
                source, jnp.where(picks, 1.0, 0.0).astype(BF16), preferred_element_type=F32
            )
            place = lanes((chans, size)) // feats
            for down in range(3):
                for step in range(3):
                    for row in range(rows):
                        value = jnp.zeros((chans, size), F32)
                        for across in range(3):
                            at = (((2 - down) * 3 + 2 - across) * 3 + 2 - step) * chans
                            value = jnp.where(
                                place == row + across, spread[at : at + chans], value
                            )
                        taps[down * 3 + step, row * chans : (row + 1) * chans, :] = (
                            value.astype(BF16)
                        )

    shapes = [(9, 128, 256), (9, 128, 128), (9, 128, 128), (9, 128, 256)]
    shapes += [(9, 64, 192), (9, 128, 384), (9, 64, 384)]
    flat = [kernel.reshape(-1, kernel.shape[-1]) for kernel in kernels]
    return call(body, [(s, BF16) for s in shapes], [((256, 128), F32)], 1 << 27, *flat)


def forward_full(volume, halo_z, halo_y, weights):
    def body(own, before, after, above, below, taps, pre, act, shifts):
        for layer in range(10):
            middle = before if layer == 0 else after if layer == 9 else own
            at = 0 if layer in (0, 9) else layer - 1
            put_shifts(shifts, 0, layer, above[layer * 16 : layer * 16 + 16])
            put_shifts(shifts, 16, layer, middle[at, :128])
            put_shifts(shifts, 144, layer, below[layer * 16 : layer * 16 + 16])
        value = convolved(taps, shifts, (0, 160), 8)
        active = silu(value)
        for layer in range(8):
            pre[layer] = value[:, layer * 128 : layer * 128 + 128]
        for layer in range(4):
            at = layer * 256
            act[layer] = pooled(
                active[:, at : at + 128], active[:, at + 128 : at + 256], 16, 128
            ).astype(BF16)

    outs = [((8, 128, 128), F32), ((4, 64, 128), BF16), ((3, 160, 1280), BF16)]
    return call(body, outs, [], 1 << 29, volume, *halo_z, *halo_y, weights)


def forward_half(act, halo_z, halo_y, weights_half, weights_quarter):
    def body(
        own, before, after, above, below, taps, next_taps, pre, act, next_pre, deep, shifts, inner
    ):
        flags = place_of()
        for layer in range(10):
            if layer < 3:
                middle = before[layer]
            elif layer < 7:
                middle = own[layer - 3]
            else:
                middle = after[layer - 7]
            put_shifts(shifts, 0, layer, above[layer])
            put_shifts(shifts, 48, layer, middle)
            put_shifts(shifts, 112, layer, below[layer])
        for part in range(2):
            value = convolved(taps, shifts, (part * 64, part * 64 + 96), 8)
            for layer in range(8):
                pre[layer, part * 128 : part * 128 + 128, :] = value[
                    :, layer * 128 : layer * 128 + 128
                ]
        row = lax.broadcasted_iota(jnp.int32, (128, 128), 0) // 32
        inside = (row > 0) | (flags[2])
        inside = inside & ((row < 3) | (flags[3]))
        for layer in range(4):
            value = pooled(silu(pre[2 * layer]), silu(pre[2 * layer + 1]), 32, 64)
            keep = inside
            if layer == 0:
                keep = keep & (flags[0])
            if layer == 3:
                keep = keep & (flags[1])
            value = jnp.where(keep, value, 0.0).astype(BF16)
            act[layer] = value
            put_shifts(inner, 0, layer, value)
        value = convolved(next_taps, inner, (0, 128), 2)
        next_pre[0] = value[:, :128]
        next_pre[1] = value[:, 128:]
        coarse = pooled(silu(value[:, :128]), silu(value[:, 128:]), 64, 32)
        dense = coarse[:8].astype(BF16).astype(F32)
        for group in range(1, 8):
            part = coarse[group * 8 : group * 8 + 8].astype(BF16).astype(F32)
            dense = dense + pltpu.roll(part, group * 16, 1)
        deep[...] = dense

    outs = [
        ((8, 256, 128), F32),
        ((4, 128, 128), BF16),
        ((2, 128, 128), F32),
        ((8, 128), F32),
        ((3, 160, 1280), BF16),
    ]
    return call(
        body,
        outs,
        [((3, 128, 512), BF16)],
        1 << 29,
        act,
        *halo_z,
        *halo_y,
        weights_half,
        weights_quarter,
    )


def turned(tile, by):
    return tile if by % 128 == 0 else pltpu.roll(tile, by % 128, 1)


def near_cell(tile, layer_step, step):
    moved = turned(tile, -(16 * layer_step + step))
    column = lanes(tile.shape) % 16
    if step > 0:
        moved = jnp.where(column == 15, 0.0, moved)
    if step < 0:
        moved = jnp.where(column == 0, 0.0, moved)
    return moved.astype(BF16)


def columns_last(tile, start):
    width = tile.shape[0]
    column = lax.broadcasted_iota(jnp.int32, (width, 128), 0)
    picks = jnp.where(lanes((width, 128)) == column + start, 1.0, 0.0).astype(BF16)
    return lax.dot_general(tile, picks, (((0,), (0,)), ((), ())), preferred_element_type=F32)


def opened(dense, layer):
    parts = [turned(dense, 16 * layer - 16 * group) for group in range(8)]
    return jnp.concatenate(parts, axis=0)


def deepest(columns, before, acts, after, skip_deep, halo_z, halo_y, skip, pre, weights, weights_back):
    def body(
        before, acts, after, skip_own, skip_before, skip_after, skip_above, skip_below, skip, pre,
        taps, taps_back, dense_out, out, shifts, delta_own, deltas,
    ):
        flags = place_of()
        core, row_at = flags[4], flags[5]
        place = lanes((64, 128)) // 16

        def cells(position, row):
            source = (before, acts, after)[position // 2]
            return source[position % 2 * columns + row]

        for near in range(5):
            row = row_at + near - 2
            valid = (row >= 0) & (row < columns)
            row = jnp.clip(row, 0, columns - 1)
            value = jnp.zeros((64, 128), F32)
            for layer in range(5):
                dense = jnp.where(core == 0, cells(layer, row), cells(layer + 1, row))
                value = jnp.where(place == layer, opened(dense, layer), value)
            value = jnp.where(valid, value, 0.0)
            for down in range(3):
                for step in range(3):
                    shifts[down * 3 + step, near * 64 : near * 64 + 64, :] = near_cell(
                        value, down - 1, step - 1
                    )
        place = lanes((128, 128)) // 16
        for near in range(3):
            value = None
            for tap in range(9):
                window = shifts[tap, near * 64 : near * 64 + 192, :]
                term = jnp.dot(taps[tap][:, :192], window, preferred_element_type=F32)
                value = term if value is None else value + term
            upstream = jnp.zeros((128, 128), F32)
            for layer in range(3):
                if near != 1:
                    at = 352 + layer * 16
                    dense = (skip_above, skip_below)[near // 2][at : at + 16]
                elif layer == 1:
                    dense = skip_own[...]
                else:
                    dense = (skip_before, skip_after)[layer // 2][0, 256:]
                upstream = upstream + columns_last(dense, 16 * layer + 16)
            keep = (place == 2) | ((place == 1) & (flags[0])) | ((place == 3) & (flags[1]))
            if near != 1:
                keep = keep & (flags[2 + near // 2])
            change = jnp.where(keep, upstream * slope(value), 0.0).astype(BF16).astype(F32)
            if near == 1:
                delta_own[...] = jnp.where(place == 2, change, 0.0).astype(BF16)
            deltas[near * 128 : near * 128 + 128, :] = change
        carried = None
        for down in range(3):
            for step in range(3):
                window = near_cell(deltas[...], down - 1, step - 1)
                term = jnp.dot(
                    taps_back[down * 3 + step], window, preferred_element_type=F32
                )
                carried = term if carried is None else carried + term
        carried = exact_dot(turned(carried, -32), pair_columns(False))
        carried = jnp.concatenate([carried, carried], axis=0)
        dense = None
        for layer in range(2):
            wide = [columns_last(skip[layer, row], 0) for row in range(2)]
            change = (jnp.concatenate(wide, axis=0) + carried) * slope(pre[layer])
            change = jnp.where(lanes(change.shape) < 32, change, 0.0).astype(BF16)
            out[layer] = change
            change = change.astype(F32)
            dense = change if dense is None else dense + turned(change, 32)
        dense_out[0] = dense.astype(BF16)

    outs = [
        ((1, 128, 128), BF16),
        ((2, 128, 128), BF16),
        ((9, 320, 128), BF16),
        ((128, 128), BF16),
    ]
    scratch = [((384, 128), F32)]
    return call(
        body, outs, scratch, 1 << 28,
        before, acts, after, skip_deep, *halo_z, *halo_y, skip, pre, weights, weights_back,
    )


def grad_deepest(shifts, delta):
    def body(shifts, delta, grad):
        for tap in range(9):
            grad[tap * 192 : tap * 192 + 192, :] = lax.dot_general(
                shifts[tap, 64:256, :], delta[...], NT, preferred_element_type=F32
            )

    return call(body, [((1728, 128), F32)], [], 1 << 27, shifts, delta)[0]


def diagonal(product, rows, chans, feats):
    place = lanes((3 * chans, 128)) // feats
    value = product[: 3 * chans]
    for row in range(1, rows):
        value = jnp.where(place == row, product[row * chans : (row + 3) * chans], value)
    turn = 64
    while turn >= feats:
        value = value + pltpu.roll(value, turn, 1)
        turn //= 2
    return value


def packed(tall, groups):
    size = tall.shape[0] // groups
    place = lanes((size, 128)) // (128 // groups)
    value = tall[:size, :]
    for group in range(1, groups):
        value = jnp.where(place == group, tall[group * size : (group + 1) * size, :], value)
    return value


def put_grads(tall, shifts, rows, offset, depth, delta, dims):
    count, chans, feats = dims
    for down in range(3):
        for step in range(3):
            at = (offset + down) * 128
            product = lax.dot_general(
                shifts[step, rows[0] : rows[1], at : at + depth * 128],
                delta,
                NT,
                preferred_element_type=F32,
            )
            tap = (down * 3 + step) * 3 * chans
            tall[tap : tap + 3 * chans, :] = diagonal(product, count, chans, feats)


def grad_quarter_of(act, delta):
    def body(act, delta, grad, shifts, tall):
        for layer in range(4):
            put_shifts(shifts, 0, layer, act[layer])
        both = jnp.concatenate([delta[0], delta[1]], axis=1)
        put_grads(tall, shifts, (0, 128), 0, 2, both, (2, 32, 64))
        grad[...] = packed(tall, 2)

    scratch = [((3, 128, 512), BF16), ((864, 128), F32)]
    return call(body, [((432, 128), F32)], scratch, 1 << 28, act, delta)[0]


def back_rest(
    delta, halo_z, halo_y, skip_half, halo_zs, halo_ys, pre_half, skip_full, pre_full,
    weights_quarter, weights_half, shifts_half, shifts_full, deep_grad, quarter_grad,
):
    def body(
        own, before, after, above, below, skip1, before1, after1, above1, below1, pre1, skip0, pre0,
        taps2, taps1, shifts1, shifts0, grad3, grad2, mine, other, moved2, moved1, delta1, delta0, tall, flat,
    ):
        flags = place_of()
        for layer in range(6):
            middle = (before, own, after)[layer // 2][0]
            for part, tile in enumerate((above[layer // 2], middle, below[layer // 2])):
                tile = turned(tile.astype(F32), -32 * (layer % 2))
                tile = jnp.where(lanes(tile.shape) < 32, tile, 0.0).astype(BF16)
                put_shifts(moved2, part * 128, layer, tile)
        value = convolved(taps2, moved2, (0, 384), 4)
        picks = pair_columns(False)
        row = lax.broadcasted_iota(jnp.int32, (192, 128), 0) // 32
        inside = lanes((192, 128)) < 64
        inside = inside & ((row > 0) | (flags[2])) & ((row < 5) | (flags[3]))
        for layer in range(6):
            if layer % 2 == 1 or layer == 0:
                at = (layer + 1) // 2 * 128
                carried = exact_dot(value[:, at : at + 128], picks)
                parts = [carried[part * 32 : part * 32 + 32] for part in (0, 1, 1, 2, 2, 3)]
                carried = jnp.concatenate(parts, axis=0)
            if layer == 0:
                middle = before1[0, 128:256]
            elif layer == 5:
                middle = after1[0, 128:256]
            else:
                middle = skip1[layer - 1]
            edge = 160 + layer * 32
            skip = jnp.concatenate(
                [above1[edge : edge + 32], middle, below1[edge : edge + 32]], axis=0
            ).astype(F32)
            change = (skip + carried) * slope(pre1[layer + 1, 32:224])
            keep = inside
            if layer == 0:
                keep = keep & (flags[0])
            if layer == 5:
                keep = keep & (flags[1])
            change = jnp.where(keep, change, 0.0).astype(BF16)
            put_shifts(moved1, 0, layer, change)
            if 0 < layer < 5:
                delta1[:, (layer - 1) * 128 : layer * 128] = change[32:160]
        value = convolved(taps1, moved1, (0, 192), 4)
        for layer in range(8):
            if layer % 2 == 0:
                at = layer // 2 * 128
                carried = exact_dot(value[:, at : at + 128], picks)
                parts = [carried[part // 2 * 16 : part // 2 * 16 + 16] for part in range(8)]
                carried = jnp.concatenate(parts, axis=0)
            change = (skip0[layer].astype(F32) + carried) * slope(pre0[layer])
            delta0[:, layer * 128 : layer * 128 + 128] = change.astype(BF16)
        flat[:1728, :] = grad3[...]
        flat[1728:2160, :] = grad2[...]
        tall[...] = jnp.zeros_like(tall)
        put_grads(tall, shifts1, (32, 128), 2, 4, delta1[...], (4, 16, 32))
        flat[2160:2272, :] = packed(tall, 4)
        put_grads(tall, shifts0, (0, 160), 0, 8, delta0[...], (8, 16, 16))
        flat[2272:2328, :] = packed(tall, 8)
        flat[2328:, :] = jnp.zeros((2560 - 2328, 128), F32)
        core = flags[4]
        for part in range(5):
            block = slice(part * 128, part * 128 + 128)
            mine[:, block] = flat[pl.ds(pl.multiple_of(part * 512 + core * 256, 256), 256), :]
            other[:, block] = flat[
                pl.ds(pl.multiple_of(part * 512 + (1 - core) * 256, 256), 256), :
            ]

    scratch = [
        ((3, 384, 768), BF16),
        ((3, 192, 768), BF16),
        ((128, 512), BF16),
        ((128, 1024), BF16),
        ((448, 128), F32),
        ((2560, 128), F32),
    ]
    return call(
        body, [(HALF, F32), (HALF, F32)], scratch, 1 << 30,
        delta, *halo_z, *halo_y, skip_half, *halo_zs, *halo_ys, pre_half, skip_full, pre_full,
        weights_quarter, weights_half, shifts_half, shifts_full, deep_grad, quarter_grad,
    )


def unpack(mine, other):
    def body(mine, other, full, half, quarter, eighth, whole, tall):
        core = lax.axis_index("c")
        for part in range(5):
            block = slice(part * 128, part * 128 + 128)
            at = part * 512 + core * 256
            whole[pl.ds(pl.multiple_of(at, 256), 256), :] = mine[:, block].astype(F32)
            at = part * 512 + (1 - core) * 256
            whole[pl.ds(pl.multiple_of(at, 256), 256), :] = other[:, block].astype(F32)

        def spread(out, source, chans):
            for down in range(3):
                for across in range(3):
                    for step in range(3):
                        at = ((down * 3 + across) * 3 + step) * chans
                        start = ((down * 3 + step) * 3 + across) * chans
                        out[at : at + chans, :] = source[
                            start : start + chans, : out.shape[1]
                        ]

        spread(eighth, whole, 64)
        for out, start, size, groups, chans in (
            (quarter, 1728, 432, 2, 32),
            (half, 2160, 112, 4, 16),
            (full, 2272, 56, 8, 16),
        ):
            dense = whole[start : start + size, :]
            for group in range(groups):
                tall[group * size : (group + 1) * size, :] = (
                    dense if group == 0 else pltpu.roll(dense, 128 - group * (128 // groups), 1)
                )
            spread(out, tall, chans)

    outs = [((432, 16), F32), ((432, 32), F32), ((864, 64), F32), ((1728, 128), F32)]
    scratch = [((2560, 128), F32), ((864, 128), F32)]
    return call(body, outs, scratch, 1 << 20, mine, other)


def exchange(first, last, axis):
    size = lax.axis_size(axis)
    up = [(i, i + 1) for i in range(size - 1)]
    down = [(i + 1, i) for i in range(size - 1)]
    return lax.ppermute(last, axis, up), lax.ppermute(first, axis, down)


def rims(block, depth, rows):
    before, after = exchange(block[:depth], block[block.shape[0] - depth :], GZ)
    tall = block.shape[1]

    def edge(start):
        parts = [part[:, start : start + rows] for part in (before, block, after)]
        return jnp.concatenate(parts, axis=0)

    return (before, after), exchange(edge(0), edge(tall - rows), "gy")


def laid_out(array):
    chans, depth, height, width = array.shape
    rows = jnp.transpose(array, (1, 2, 0, 3)).reshape(depth, height * chans, width)
    return jnp.pad(rows, ((0, 0), (0, 0), (0, 128 - width)))


def summed(mine, other):
    swap = [(0, 1), (1, 0)]
    columns, planes = lax.axis_size("gy"), lax.axis_size(("x", "z"))
    rows, width = HALF[0] // columns, HALF[1]
    pair = (mine + lax.ppermute(other, "c", swap)).astype(BF16)
    pieces = lax.all_to_all(pair.reshape(columns, rows, width), "gy", 0, 0)
    column = jnp.sum(pieces.astype(F32), axis=0)
    chunk = rows // planes
    pieces = lax.all_to_all(column, ("x", "z"), 0, 0, tiled=True)
    done = jnp.sum(pieces.reshape(planes, chunk, width), axis=0)
    spread = jnp.broadcast_to(done[None], (planes, chunk, width)).reshape(rows, width)
    column = lax.all_to_all(lax.optimization_barrier(spread), ("x", "z"), 0, 0, tiled=True)
    column = column.astype(BF16)
    spread = lax.optimization_barrier(jnp.broadcast_to(column[None], (columns, rows, width)))
    half = lax.all_to_all(spread, "gy", 0, 0).reshape(HALF)
    return unpack(half, lax.ppermute(half, "c", swap))


def on_device(
    volume,
    kernel_full,
    kernel_half,
    kernel_quarter,
    kernel_eighth,
    skip_full,
    skip_half,
    skip_quarter,
    skip_eighth,
):
    kernels = (kernel_full, kernel_half, kernel_quarter, kernel_eighth)
    volume = laid_out(volume)
    skip1 = laid_out(skip_half)
    skip3 = jnp.transpose(skip_eighth, (1, 2, 3, 0)).reshape(1, 16, 128)
    skip2 = jnp.transpose(skip_quarter, (1, 2, 3, 0))
    first = jnp.concatenate([volume[:1], skip1[:1], skip3], axis=1)
    last = jnp.concatenate([volume[7:], skip1[3:], skip3], axis=1)
    before, after = exchange(first, last, GZ)
    before, after, skip0 = lax.optimization_barrier((before, after, laid_out(skip_full)))

    def edge(start, start1):
        parts = [
            part[:, start : start + 16].reshape(-1, 128)
            for part in (before[:, :128], volume, after[:, :128])
        ]
        parts += [
            part[:, start1 : start1 + 32].reshape(-1, 128)
            for part in (before[:, 128:256], skip1, after[:, 128:256])
        ]
        parts += [before[0, 256:], skip3[0], after[0, 256:]]
        return jnp.concatenate(parts, axis=0)

    above, below = exchange(edge(0, 0), edge(112, 96), "gy")
    halo_z0, halo_y0 = (before, after), (above, below)
    dims = ((8, 16, 16), (4, 16, 32), (2, 32, 64), (1, 64, 128))
    w0, w1, w2, w3, t1, t2, t3 = prepare(kernels, dims)
    pre0, act1, shifts0 = forward_full(volume, halo_z0, halo_y0, w0)
    halo_z, halo_y = rims(act1, 3, 48)
    pre1, act2, pre2, act3, shifts1 = forward_half(act1, halo_z, halo_y, w1, w2)
    columns = lax.axis_size("gy")
    many = (2 * columns,) + act3.shape
    acts = lax.all_to_all(
        lax.optimization_barrier(jnp.broadcast_to(act3[None], many)), ("c", "gy"), 0, 0
    )
    before, after = exchange(acts, acts, ("x", "z"))
    dense2, delta2, shifts3, delta3 = deepest(
        columns, before, acts, after, skip3[0], halo_z0, halo_y0, skip2, pre2, w3, t3
    )
    halo_z, halo_y = rims(dense2, 1, 128)
    grad3 = grad_deepest(shifts3, delta3)
    grad2 = grad_quarter_of(act2, delta2)
    mine, other = back_rest(
        dense2, halo_z, halo_y, skip1, halo_z0, halo_y0, pre1, skip0, pre0,
        t2, t1, shifts1, shifts0, grad3, grad2,
    )
    outs = summed(mine, other)
    return tuple(out.reshape(kernel.shape) for out, kernel in zip(outs, kernels))


def solution(mesh):
    fine = jax.sharding.Mesh(mesh.devices.reshape(4, 8, 2, 8), ("x", "z", "c", "gy"))
    return mapped(fine)


def mapped(fine):
    block = P(None, GZ, "gy", None)
    return jax.shard_map(
        on_device,
        mesh=fine,
        in_specs=(block, P(), P(), P(), P(), block, block, block, block),
        out_specs=(P(), P(), P(), P()),
        check_vma=False,
    )
```

time: 860 us -> 176 us (0.20)
  waiting for transfers between devices: 593 us -> 23.8 us
  blocking collectives: 0 us -> 78.9 us
  matrix products: 77.6 us -> 0 us
  local copies, waits for them, and re-layouts: 77.7 us -> 4.33 us
  starting transfers between devices: 83.4 us -> 52.3 us
  between operations: 15.4 us -> 1.15 us
  Pallas kernels: 0 us -> 12.7 us
    psum x2 -> x0, waiting for transfers between devices: 566 us -> none  [on_device(): lax.psum((terms[0], terms[1], terms[2], deep_term), ('gz', 'gy'))]
    all_to_all x0 -> x5, blocking collectives: none -> 78.9 us  [the longest x1 20.2 us: summed(): pieces = lax.all_to_all(column, ('x', 'z'), 0, 0, tiled=True)]
    transpose x4 -> x0, matrix products: 62.2 us -> none  [weight_term(): return jnp.transpose(product, (2, 3, 4, 0, 1))]
    conv_general_dilated x29 -> x0, local copies, waits for them, and re-layouts: 31.1 us -> none  [convolve(): lax.conv_general_dilated(padded[None], kernel, (1, 1, 1), 'VALID', dimens...]
    ppermute x28 -> x16, starting transfers between devices: 83.3 us -> 52.3 us  [the longest x14 43.8 us: exchange(): return (lax.ppermute(last, axis, up), lax.ppermute(first, axis, down))]
    broadcast_in_dim x14 -> x2, local copies, waits for them, and re-layouts: 26.2 us -> 0.04 us  [the longest x1 0.03 us: summed(): jnp.broadcast_to(column[None], (columns, rows, width))]
    conv_general_dilated x7 -> x0, matrix products: 15.4 us -> none  [convolve(): lax.conv_general_dilated(padded[None], kernel, (1, 1, 1), 'VALID', dimens...]
    pallas_call x0 -> x8, Pallas kernels: none -> 12.7 us  [call(): pl.pallas_call(body, out_shape=tuple((jax.ShapeDtypeStruct(shape, dtype)...]
  transfers between devices with their start and end apart: 30 -> 16, of which waited for: 15 -> 9; matrix products, arithmetic and copies ran while one was open for 3% -> 1% of each run, Pallas kernels for 0% -> 1%
where the time goes in v1:
time: 176 us; the launch traced here: 175 us
  blocking collectives  78.9 us (45%)
  starting transfers between devices  52.3 us (30%)
  waiting for transfers between devices  23.8 us (14%)
  Pallas kernels  12.7 us (7%)
  local copies, waits for them, and re-layouts  4.33 us (2%)
  other arithmetic  1.8 us (1%)
    ppermute x14, starting transfers between devices, exchange(): return (lax.ppermute(last, axis, up), lax.ppermute(first, axis, down))  43.8 us
    ppermute x14, waiting for transfers between devices, exchange(): return (lax.ppermute(last, axis, up), lax.ppermute(first, axis, down))  20.5 us
    all_to_all x1, blocking collectives, summed(): pieces = lax.all_to_all(column, ('x', 'z'), 0, 0, tiled=True)  20.2 us
    all_to_all x1, blocking collectives, on_device(): lax.all_to_all(lax.optimization_barrier(jnp.broadcast_to(act3[None], many...  18.4 us
    all_to_all x1, blocking collectives, summed(): pieces = lax.all_to_all(pair.reshape(columns, rows, width), 'gy', 0, 0)  15.8 us
    pallas_call x8, Pallas kernels, call(): pl.pallas_call(body, out_shape=tuple((jax.ShapeDtypeStruct(shape, dtype)...  12.7 us
    all_to_all x1, blocking collectives, summed(): half = lax.all_to_all(spread, 'gy', 0, 0).reshape(HALF)  12.5 us
    all_to_all x1, blocking collectives, summed(): lax.all_to_all(lax.optimization_barrier(spread), ('x', 'z'), 0, 0, tiled=...  12.1 us
  transfers between devices with their start and end apart: 16, of which 9 were waited for; matrix products, arithmetic and copies ran while one was open for 1% of the time, Pallas kernels for 1%

profile of v1, /device:TPU:1, one launch (start us, length us, event | category | flops | bytes accessed | tf_op | source)
XLA Modules:
  0.0 175.1 jit_solution(14279465021450483344)
XLA Ops:
  3.3 5.4 %collective-permute-start = (bf16[1,272,128]{2,1,0:T(8,128)(2,1)S(1)}, bf16[1,272,128]{2,1,0:T(8,128)(2,1)S(1)}, u32[]{:S(2)}, u32[]{:S(2)}) collective-permute-start(bf16[1,272,128]{2,1,0:T(8,128)(2,1)S(1)} %get-tuple-element.91), channel_id=1, source_target_pairs={{0,8},{8,16},{16,24},{24,32},{32,40},{40,48},{48,56},{56,64},{64,7... | collective-permute-start | bytes 208904 | tf_op jit(solution)/shard_map/ppermute | solution.py:557
  8.7 4.7 %collective-permute-start.1 = (bf16[1,272,128]{2,1,0:T(8,128)(2,1)S(1)}, bf16[1,272,128]{2,1,0:T(8,128)(2,1)S(1)}, u32[]{:S(2)}, u32[]{:S(2)}) collective-permute-start(bf16[1,272,128]{2,1,0:T(8,128)(2,1)S(1)} %get-tuple-element.90), channel_id=1, source_target_pairs={{8,0},{16,8},{24,16},{32,24},{40,32},{48,40},{56,48},{64,56},{72,6... | collective-permute-start | bytes 208904 | tf_op jit(solution)/shard_map/ppermute | solution.py:557
  14.9 2.7 %collective-permute-start.2 = (bf16[400,128]{1,0:T(8,128)(2,1)S(1)}, bf16[400,128]{1,0:T(8,128)(2,1)S(1)}, u32[]{:S(2)}, u32[]{:S(2)}) collective-permute-start(bf16[400,128]{1,0:T(8,128)(2,1)S(1)} %get-tuple-element.69), channel_id=1, source_target_pairs={{0,1},{1,2},{2,3},{3,4},{4,5},{5,6},{6,7},{8,9},{9,10},{10,11},{11... | collective-permute-start | bytes 307208 | tf_op jit(solution)/shard_map/ppermute | solution.py:557
  17.7 1.3 collective-permute-start.3
  19.0 1.4 shard_map.120
  20.4 2.6 %collective-permute-done.3.below.skip_below.below1 = bf16[400,128]{1,0:T(8,128)(2,1)S(1)} collective-permute-done((bf16[400,128]{1,0:T(8,128)(2,1)S(1)}, bf16[400,128]{1,0:T(8,128)(2,1)S(1)}, u32[]{:S(2)}, u32[]{:S(2)}) %collective-permute-start.3) | collective-permute-done | bytes 102432 | tf_op jit(solution)/shard_map/ppermute | solution.py:557
  24.3 3.3 %collective-permute-start.4 = (bf16[3,64,128]{2,1,0:T(8,128)(2,1)S(1)}, bf16[3,64,128]{2,1,0:T(8,128)(2,1)S(1)}, u32[]{:S(2)}, u32[]{:S(2)}) collective-permute-start(bf16[3,64,128]{2,1,0:T(8,128)(2,1)S(1)} %get-tuple-element.83), channel_id=1, source_target_pairs={{0,8},{8,16},{16,24},{24,32},{32,40},{40,48},{48,56},{56,64},{64,7... | collective-permute-start | bytes 147464 | tf_op jit(solution)/shard_map/ppermute | solution.py:557
  27.6 1.9 %collective-permute-start.5 = (bf16[3,64,128]{2,1,0:T(8,128)(2,1)S(1)}, bf16[3,64,128]{2,1,0:T(8,128)(2,1)S(1)}, u32[]{:S(2)}, u32[]{:S(2)}) collective-permute-start(bf16[3,64,128]{2,1,0:T(8,128)(2,1)S(1)} %get-tuple-element.82), channel_id=1, source_target_pairs={{8,0},{16,8},{24,16},{32,24},{40,32},{48,40},{56,48},{64,56},{72,6... | collective-permute-start | bytes 147464 | tf_op jit(solution)/shard_map/ppermute | solution.py:557
  29.6 3.5 %collective-permute-done.5.after = bf16[3,64,128]{2,1,0:T(8,128)(2,1)S(1)} collective-permute-done((bf16[3,64,128]{2,1,0:T(8,128)(2,1)S(1)}, bf16[3,64,128]{2,1,0:T(8,128)(2,1)S(1)}, u32[]{:S(2)}, u32[]{:S(2)}) %collective-permute-start.5) | collective-permute-done | bytes 49184 | tf_op jit(solution)/shard_map/ppermute | solution.py:557
  33.1 1.3 collective-permute-start.7
  34.4 4.0 %collective-permute-start.6 = (bf16[10,48,128]{2,1,0:T(8,128)(2,1)S(1)}, bf16[10,48,128]{2,1,0:T(8,128)(2,1)S(1)}, u32[]{:S(2)}, u32[]{:S(2)}) collective-permute-start(bf16[10,48,128]{2,1,0:T(8,128)(2,1)S(1)} %pad_maximum_fusion), channel_id=1, source_target_pairs={{0,1},{1,2},{2,3},{3,4},{4,5},{5,6},{6,7},{8,9},{9,10},{10,11},{11... | collective-permute-start | bytes 368648 | tf_op jit(solution)/shard_map/ppermute | solution.py:557
  38.7 1.5 collective-permute-done.6.above
  40.3 2.4 %shard_map.122 = (f32[8,256,128]{2,1,0:T(8,128)S(1)}, bf16[4,128,128]{2,1,0:T(8,128)(2,1)S(1)}, f32[2,128,128]{2,1,0:T(8,128)S(1)}, f32[8,128]{1,0:T(8,128)S(1)}, bf16[3,160,1280]{2,1,0:T(8,128)(2,1)S(1)}) custom-call(bf16[4,64,128]{2,1,0:T(8,128)(2,1)S(1)} %get-tuple-element.35.own, bf16[3,64,128]{2,1,0:T(8,128)(2,1)S(1)} %collective-permute-done.4.before, ...), custom_call_target="tpu_custom_call" | custom-call | flops 536870912 | bytes 1048576 | tf_op jit(solution)/shard_map/pallas_call | solution.py:17
  42.6 18.4 %all_to_all.33.acts = f32[16,8,128]{2,1,0:T(8,128)S(1)} all-to-all(f32[16,8,128]{2,1,0:T(8,128)S(1)} %broadcast_in_dim.4), channel_id=1, replica_groups=mesh['x'=4,'z'=8,'c'=2,'gy'=8] {'c','gy'}, dimensions={0} | all-to-all | bytes 131072 | tf_op jit(solution)/shard_map/all_to_all | solution.py:637
  61.0 4.0 %collective-permute-start.8 = (f32[16,8,128]{2,1,0:T(8,128)S(1)}, f32[16,8,128]{2,1,0:T(8,128)S(1)}, u32[]{:S(2)}, u32[]{:S(2)}) collective-permute-start(f32[16,8,128]{2,1,0:T(8,128)S(1)} %all_to_all.33.acts), channel_id=1, source_target_pairs={{0,16},{16,32},{32,48},{48,64},{64,80},{80,96},{96,112},{112,128},... | collective-permute-start | bytes 196616 | tf_op jit(solution)/shard_map/ppermute | solution.py:557
  65.1 1.3 collective-permute-start.9
  66.4 6.1 %collective-permute-done.9.after = f32[16,8,128]{2,1,0:T(8,128)S(1)} collective-permute-done((f32[16,8,128]{2,1,0:T(8,128)S(1)}, f32[16,8,128]{2,1,0:T(8,128)S(1)}, u32[]{:S(2)}, u32[]{:S(2)}) %collective-permute-start.9) | collective-permute-done | bytes 65568 | tf_op jit(solution)/shard_map/ppermute | solution.py:557
  72.5 1.8 %shard_map.123 = (bf16[1,128,128]{2,1,0:T(8,128)(2,1)S(1)}, bf16[2,128,128]{2,1,0:T(8,128)(2,1)S(1)}, bf16[9,320,128]{2,1,0:T(8,128)(2,1)S(1)}, bf16[128,128]{1,0:T(8,128)(2,1)S(1)}) custom-call(f32[16,8,128]{2,1,0:T(8,128)S(1)} %collective-permute-done.8.before, f32[16,8,128]{2,1,0:T(8,128)S(1)} %all_to_all.33.acts, ...), custom_call_target="tpu_custom_call" | custom-call | flops 268435456 | bytes 1048576 | tf_op jit(solution)/shard_map/pallas_call | solution.py:17
  74.3 8.1 %collective-permute-start.10 = (bf16[1,128,128]{2,1,0:T(8,128)(2,1)S(1)}, bf16[1,128,128]{2,1,0:T(8,128)(2,1)S(1)}, u32[]{:S(2)}, u32[]{:S(2)}) collective-permute-start(bf16[1,128,128]{2,1,0:T(8,128)(2,1)S(1)} %get-tuple-element.42.own), channel_id=1, source_target_pairs={{0,8},{8,16},{16,24},{24,32},{32,40},{40,48},{48,56},{56,64},{64,7... | collective-permute-start | bytes 98312 | tf_op jit(solution)/shard_map/ppermute | solution.py:557
  82.4 1.9 %collective-permute-start.11 = (bf16[1,128,128]{2,1,0:T(8,128)(2,1)S(1)}, bf16[1,128,128]{2,1,0:T(8,128)(2,1)S(1)}, u32[]{:S(2)}, u32[]{:S(2)}) collective-permute-start(bf16[1,128,128]{2,1,0:T(8,128)(2,1)S(1)} %get-tuple-element.42.own), channel_id=1, source_target_pairs={{8,0},{16,8},{24,16},{32,24},{40,32},{48,40},{56,48},{64,56},{72,6... | collective-permute-start | bytes 98312 | tf_op jit(solution)/shard_map/ppermute | solution.py:557
  84.3 3.3 %collective-permute-done.11.after = bf16[1,128,128]{2,1,0:T(8,128)(2,1)S(1)} collective-permute-done((bf16[1,128,128]{2,1,0:T(8,128)(2,1)S(1)}, bf16[1,128,128]{2,1,0:T(8,128)(2,1)S(1)}, u32[]{:S(2)}, u32[]{:S(2)}) %collective-permute-start.11) | collective-permute-done | bytes 32800 | tf_op jit(solution)/shard_map/ppermute | solution.py:557
  87.6 2.6 %collective-permute-start.12 = (bf16[3,128,128]{2,1,0:T(8,128)(2,1)S(1)}, bf16[3,128,128]{2,1,0:T(8,128)(2,1)S(1)}, u32[]{:S(2)}, u32[]{:S(2)}) collective-permute-start(bf16[3,128,128]{2,1,0:T(8,128)(2,1)S(1)} %constant_dynamic-update-slice_fusion.18), channel_id=1, source_target_pairs={{0,1},{1,2},{2,3},{3,4},{4,5},{5,6},{6,7},{8,9},{9,10},{10,11},{11... | collective-permute-start | bytes 294920 | tf_op jit(solution)/shard_map/ppermute | solution.py:557
  92.3 3.2 %collective-permute-done.13.below = bf16[3,128,128]{2,1,0:T(8,128)(2,1)S(1)} collective-permute-done((bf16[3,128,128]{2,1,0:T(8,128)(2,1)S(1)}, bf16[3,128,128]{2,1,0:T(8,128)(2,1)S(1)}, u32[]{:S(2)}, u32[]{:S(2)}) %collective-permute-start.13) | collective-permute-done | bytes 98336 | tf_op jit(solution)/shard_map/ppermute | solution.py:557
  95.6 3.7 %shard_map.126 = (f32[256,640]{1,0:T(8,128)S(1)}, f32[256,640]{1,0:T(8,128)S(1)}) custom-call(bf16[1,128,128]{2,1,0:T(8,128)(2,1)S(1)} %get-tuple-element.42.own, bf16[1,128,128]{2,1,0:T(8,128)(2,1)S(1)} %collective-permute-done.10.before, bf16[1,128,128]{2,1,0:T(8,128)(2,1)S(1)} %collective-permute-done.11.after, ...), custom_call_target="tpu_custom_call" | custom-call | flops 1073741824 | bytes 1048576 | tf_op jit(solution)/shard_map/pallas_call | solution.py:17
  99.3 1.9 %collective-permute-start.14 = (f32[256,640]{1,0:T(8,128)S(1)}, f32[256,640]{1,0:T(8,128)S(1)}, u32[]{:S(2)}, u32[]{:S(2)}) collective-permute-start(f32[256,640]{1,0:T(8,128)S(1)} %get-tuple-element.55), channel_id=1, source_target_pairs={{0,8},{8,0},{1,9},{9,1},{2,10},{10,2},{3,11},{11,3},{4,12},{12,4},... | collective-permute-start | bytes 1966088 | tf_op jit(solution)/shard_map/ppermute | solution.py:581
  101.2 2.1 %collective-permute-done.14 = f32[256,640]{1,0:T(8,128)S(1)} collective-permute-done((f32[256,640]{1,0:T(8,128)S(1)}, f32[256,640]{1,0:T(8,128)S(1)}, u32[]{:S(2)}, u32[]{:S(2)}) %collective-permute-start.14) | collective-permute-done | bytes 655392 | tf_op jit(solution)/shard_map/ppermute | solution.py:581
  103.3 15.8 %all_to_all.34 = bf16[8,32,640]{2,1,0:T(8,128)(2,1)S(1)} all-to-all(bf16[8,32,640]{2,1,0:T(8,128)(2,1)S(1)} %bitcast.70), channel_id=1, replica_groups=mesh['x'=4,'z'=8,'c'=2,'gy'=8] {'gy'}, dimensions={0} | all-to-all | bytes 655360 | tf_op jit(solution)/shard_map/all_to_all | solution.py:582
  119.2 20.2 %all_to_all.35 = f32[32,1,640]{2,1,0:T(1,128)S(1)} all-to-all(f32[32,1,640]{2,1,0:T(1,128)S(1)} %all_to_all.23), channel_id=1, replica_groups=mesh['x'=4,'z'=8,'c'=2,'gy'=8] {'x','z'}, dimensions={0} | all-to-all | bytes 163840 | tf_op jit(solution)/shard_map/all_to_all | solution.py:585
  141.1 12.1 %all_to_all.36 = bf16[32,2,320]{2,1,0:T(2,128)(2,1)S(1)} all-to-all(bf16[32,2,320]{2,1,0:T(2,128)(2,1)S(1)} %reshape.135), channel_id=1, replica_groups=mesh['x'=4,'z'=8,'c'=2,'gy'=8] {'x','z'}, dimensions={0} | all-to-all | bytes 81920 | tf_op jit(solution)/shard_map/all_to_all | solution.py:588
  153.3 12.5 %all_to_all.37 = bf16[8,32,640]{2,1,0:T(8,128)(2,1)S(1)} all-to-all(bf16[8,32,640]{2,1,0:T(8,128)(2,1)S(1)} %broadcast_in_dim.5), channel_id=1, replica_groups=mesh['x'=4,'z'=8,'c'=2,'gy'=8] {'gy'}, dimensions={0} | all-to-all | bytes 655360 | tf_op jit(solution)/shard_map/all_to_all | solution.py:591
  165.8 6.6 %collective-permute-start.15 = (bf16[256,640]{1,0:T(8,128)(2,1)S(1)}, bf16[256,640]{1,0:T(8,128)(2,1)S(1)}, u32[]{:S(2)}, u32[]{:S(2)}) collective-permute-start(bf16[256,640]{1,0:T(8,128)(2,1)S(1)} %bitcast.55), channel_id=1, source_target_pairs={{0,8},{8,0},{1,9},{9,1},{2,10},{10,2},{3,11},{11,3},{4,12},{12,4},... | collective-permute-start | bytes 983048 | tf_op jit(solution)/shard_map/ppermute | solution.py:592
  173.7 1.4 shard_map.127
  (70 shorter events, 10.9 us)
Async XLA Ops:
  0.6 13.9 %copy-start.6 = (bf16[16,8,8,128]{3,2,1,0:T(8,128)(2,1)S(1)}, bf16[16,8,8,128]{3,2,1,0:T(8,128)(2,1)}, u32[]{:S(2)}) copy-start(bf16[16,8,8,128]{3,2,1,0:T(8,128)(2,1)} %param.14) | copy-start | bytes 786436
  1.6 13.3 %copy-start.4 = (bf16[128,1,1,16]{0,3,2,1:T(8,128)(2,1)S(1)}, bf16[128,1,1,16]{0,3,2,1:T(8,128)(2,1)}, u32[]{:S(2)}) copy-start(bf16[128,1,1,16]{0,3,2,1:T(8,128)(2,1)} %param.17) | copy-start | bytes 12292
  1.7 17.3 %copy-start = (bf16[3,3,3,64,128]{4,3,2,1,0:T(8,128)(2,1)S(1)}, bf16[3,3,3,64,128]{4,3,2,1,0:T(8,128)(2,1)}, u32[]{:S(2)}) copy-start(bf16[3,3,3,64,128]{4,3,2,1,0:T(8,128)(2,1)} %param.13) | copy-start | bytes 1327108
  1.7 17.3 %copy-start.1 = (bf16[3,3,3,32,64]{4,3,2,1,0:T(8,128)(2,1)S(1)}, bf16[3,3,3,32,64]{4,3,2,1,0:T(8,128)(2,1)}, u32[]{:S(2)}) copy-start(bf16[3,3,3,32,64]{4,3,2,1,0:T(8,128)(2,1)} %param.12) | copy-start | bytes 331780
  1.7 17.3 %copy-start.2 = (bf16[3,3,3,16,16]{4,3,2,1,0:T(8,128)(2,1)S(1)}, bf16[3,3,3,16,16]{4,3,2,1,0:T(8,128)(2,1)}, u32[]{:S(2)}) copy-start(bf16[3,3,3,16,16]{4,3,2,1,0:T(8,128)(2,1)} %param.10) | copy-start | bytes 41476
  1.7 17.3 %copy-start.3 = (bf16[3,3,3,16,32]{4,3,2,1,0:T(8,128)(2,1)S(1)}, bf16[3,3,3,16,32]{4,3,2,1,0:T(8,128)(2,1)}, u32[]{:S(2)}) copy-start(bf16[3,3,3,16,32]{4,3,2,1,0:T(8,128)(2,1)} %param.11) | copy-start | bytes 82948
  3.3 11.5 %collective-permute-start = (bf16[1,272,128]{2,1,0:T(8,128)(2,1)S(1)}, bf16[1,272,128]{2,1,0:T(8,128)(2,1)S(1)}, u32[]{:S(2)}, u32[]{:S(2)}) collective-permute-start(bf16[1,272,128]{2,1,0:T(8,128)(2,1)S(1)} %get-tuple-element.91), channel_id=1, source_target_pairs={{0,8},{8,16},{16,24},{24,32},{32,40},{40,48},{48,56},{56,64},{64,7... | collective-permute-start | bytes 208904 | tf_op jit(solution)/shard_map/ppermute | solution.py:557
  8.7 6.1 %collective-permute-start.1 = (bf16[1,272,128]{2,1,0:T(8,128)(2,1)S(1)}, bf16[1,272,128]{2,1,0:T(8,128)(2,1)S(1)}, u32[]{:S(2)}, u32[]{:S(2)}) collective-permute-start(bf16[1,272,128]{2,1,0:T(8,128)(2,1)S(1)} %get-tuple-element.90), channel_id=1, source_target_pairs={{8,0},{16,8},{24,16},{32,24},{40,32},{48,40},{56,48},{64,56},{72,6... | collective-permute-start | bytes 208904 | tf_op jit(solution)/shard_map/ppermute | solution.py:557
  14.9 5.5 %collective-permute-start.2 = (bf16[400,128]{1,0:T(8,128)(2,1)S(1)}, bf16[400,128]{1,0:T(8,128)(2,1)S(1)}, u32[]{:S(2)}, u32[]{:S(2)}) collective-permute-start(bf16[400,128]{1,0:T(8,128)(2,1)S(1)} %get-tuple-element.69), channel_id=1, source_target_pairs={{0,1},{1,2},{2,3},{3,4},{4,5},{5,6},{6,7},{8,9},{9,10},{10,11},{11... | collective-permute-start | bytes 307208 | tf_op jit(solution)/shard_map/ppermute | solution.py:557
  17.7 5.4 %collective-permute-start.3 = (bf16[400,128]{1,0:T(8,128)(2,1)S(1)}, bf16[400,128]{1,0:T(8,128)(2,1)S(1)}, u32[]{:S(2)}, u32[]{:S(2)}) collective-permute-start(bf16[400,128]{1,0:T(8,128)(2,1)S(1)} %get-tuple-element.68), channel_id=1, source_target_pairs={{1,0},{2,1},{3,2},{4,3},{5,4},{6,5},{7,6},{9,8},{10,9},{11,10},{12... | collective-permute-start | bytes 307208 | tf_op jit(solution)/shard_map/ppermute | solution.py:557
  24.3 5.3 %collective-permute-start.4 = (bf16[3,64,128]{2,1,0:T(8,128)(2,1)S(1)}, bf16[3,64,128]{2,1,0:T(8,128)(2,1)S(1)}, u32[]{:S(2)}, u32[]{:S(2)}) collective-permute-start(bf16[3,64,128]{2,1,0:T(8,128)(2,1)S(1)} %get-tuple-element.83), channel_id=1, source_target_pairs={{0,8},{8,16},{16,24},{24,32},{32,40},{40,48},{48,56},{56,64},{64,7... | collective-permute-start | bytes 147464 | tf_op jit(solution)/shard_map/ppermute | solution.py:557
  27.6 5.4 %collective-permute-start.5 = (bf16[3,64,128]{2,1,0:T(8,128)(2,1)S(1)}, bf16[3,64,128]{2,1,0:T(8,128)(2,1)S(1)}, u32[]{:S(2)}, u32[]{:S(2)}) collective-permute-start(bf16[3,64,128]{2,1,0:T(8,128)(2,1)S(1)} %get-tuple-element.82), channel_id=1, source_target_pairs={{8,0},{16,8},{24,16},{32,24},{40,32},{48,40},{56,48},{64,56},{72,6... | collective-permute-start | bytes 147464 | tf_op jit(solution)/shard_map/ppermute | solution.py:557
  33.1 39.4 %copy-start.5 = (bf16[64,2,2,32]{0,3,2,1:T(8,128)(2,1)S(1)}, bf16[64,2,2,32]{0,3,2,1:T(8,128)(2,1)}, u32[]{:S(2)}) copy-start(bf16[64,2,2,32]{0,3,2,1:T(8,128)(2,1)} %param.16) | copy-start | bytes 49156
  33.1 5.6 %collective-permute-start.7 = (bf16[10,48,128]{2,1,0:T(8,128)(2,1)S(1)}, bf16[10,48,128]{2,1,0:T(8,128)(2,1)S(1)}, u32[]{:S(2)}, u32[]{:S(2)}) collective-permute-start(bf16[10,48,128]{2,1,0:T(8,128)(2,1)S(1)} %pad_maximum_fusion.1), channel_id=1, source_target_pairs={{1,0},{2,1},{3,2},{4,3},{5,4},{6,5},{7,6},{9,8},{10,9},{11,10},{12... | collective-permute-start | bytes 368648 | tf_op jit(solution)/shard_map/ppermute | solution.py:557
  34.4 5.8 %collective-permute-start.6 = (bf16[10,48,128]{2,1,0:T(8,128)(2,1)S(1)}, bf16[10,48,128]{2,1,0:T(8,128)(2,1)S(1)}, u32[]{:S(2)}, u32[]{:S(2)}) collective-permute-start(bf16[10,48,128]{2,1,0:T(8,128)(2,1)S(1)} %pad_maximum_fusion), channel_id=1, source_target_pairs={{0,1},{1,2},{2,3},{3,4},{4,5},{5,6},{6,7},{8,9},{9,10},{10,11},{11... | collective-permute-start | bytes 368648 | tf_op jit(solution)/shard_map/ppermute | solution.py:557
  61.0 5.4 %collective-permute-start.8 = (f32[16,8,128]{2,1,0:T(8,128)S(1)}, f32[16,8,128]{2,1,0:T(8,128)S(1)}, u32[]{:S(2)}, u32[]{:S(2)}) collective-permute-start(f32[16,8,128]{2,1,0:T(8,128)S(1)} %all_to_all.33.acts), channel_id=1, source_target_pairs={{0,16},{16,32},{32,48},{48,64},{64,80},{80,96},{96,112},{112,128},... | collective-permute-start | bytes 196616 | tf_op jit(solution)/shard_map/ppermute | solution.py:557
  65.1 7.4 %collective-permute-start.9 = (f32[16,8,128]{2,1,0:T(8,128)S(1)}, f32[16,8,128]{2,1,0:T(8,128)S(1)}, u32[]{:S(2)}, u32[]{:S(2)}) collective-permute-start(f32[16,8,128]{2,1,0:T(8,128)S(1)} %all_to_all.33.acts), channel_id=1, source_target_pairs={{16,0},{32,16},{48,32},{64,48},{80,64},{96,80},{112,96},{128,112},... | collective-permute-start | bytes 196616 | tf_op jit(solution)/shard_map/ppermute | solution.py:557
  74.3 10.0 %collective-permute-start.10 = (bf16[1,128,128]{2,1,0:T(8,128)(2,1)S(1)}, bf16[1,128,128]{2,1,0:T(8,128)(2,1)S(1)}, u32[]{:S(2)}, u32[]{:S(2)}) collective-permute-start(bf16[1,128,128]{2,1,0:T(8,128)(2,1)S(1)} %get-tuple-element.42.own), channel_id=1, source_target_pairs={{0,8},{8,16},{16,24},{24,32},{32,40},{40,48},{48,56},{56,64},{64,7... | collective-permute-start | bytes 98312 | tf_op jit(solution)/shard_map/ppermute | solution.py:557
  82.4 5.2 %collective-permute-start.11 = (bf16[1,128,128]{2,1,0:T(8,128)(2,1)S(1)}, bf16[1,128,128]{2,1,0:T(8,128)(2,1)S(1)}, u32[]{:S(2)}, u32[]{:S(2)}) collective-permute-start(bf16[1,128,128]{2,1,0:T(8,128)(2,1)S(1)} %get-tuple-element.42.own), channel_id=1, source_target_pairs={{8,0},{16,8},{24,16},{32,24},{40,32},{48,40},{56,48},{64,56},{72,6... | collective-permute-start | bytes 98312 | tf_op jit(solution)/shard_map/ppermute | solution.py:557
  87.6 4.7 %collective-permute-start.12 = (bf16[3,128,128]{2,1,0:T(8,128)(2,1)S(1)}, bf16[3,128,128]{2,1,0:T(8,128)(2,1)S(1)}, u32[]{:S(2)}, u32[]{:S(2)}) collective-permute-start(bf16[3,128,128]{2,1,0:T(8,128)(2,1)S(1)} %constant_dynamic-update-slice_fusion.18), channel_id=1, source_target_pairs={{0,1},{1,2},{2,3},{3,4},{4,5},{5,6},{6,7},{8,9},{9,10},{10,11},{11... | collective-permute-start | bytes 294920 | tf_op jit(solution)/shard_map/ppermute | solution.py:557
  90.2 5.4 %collective-permute-start.13 = (bf16[3,128,128]{2,1,0:T(8,128)(2,1)S(1)}, bf16[3,128,128]{2,1,0:T(8,128)(2,1)S(1)}, u32[]{:S(2)}, u32[]{:S(2)}) collective-permute-start(bf16[3,128,128]{2,1,0:T(8,128)(2,1)S(1)} %constant_dynamic-update-slice_fusion.18), channel_id=1, source_target_pairs={{1,0},{2,1},{3,2},{4,3},{5,4},{6,5},{7,6},{9,8},{10,9},{11,10},{12... | collective-permute-start | bytes 294920 | tf_op jit(solution)/shard_map/ppermute | solution.py:557
  99.3 4.0 %collective-permute-start.14 = (f32[256,640]{1,0:T(8,128)S(1)}, f32[256,640]{1,0:T(8,128)S(1)}, u32[]{:S(2)}, u32[]{:S(2)}) collective-permute-start(f32[256,640]{1,0:T(8,128)S(1)} %get-tuple-element.55), channel_id=1, source_target_pairs={{0,8},{8,0},{1,9},{9,1},{2,10},{10,2},{3,11},{11,3},{4,12},{12,4},... | collective-permute-start | bytes 1966088 | tf_op jit(solution)/shard_map/ppermute | solution.py:581
  165.8 7.8 %collective-permute-start.15 = (bf16[256,640]{1,0:T(8,128)(2,1)S(1)}, bf16[256,640]{1,0:T(8,128)(2,1)S(1)}, u32[]{:S(2)}, u32[]{:S(2)}) collective-permute-start(bf16[256,640]{1,0:T(8,128)(2,1)S(1)} %bitcast.55), channel_id=1, source_target_pairs={{0,8},{8,0},{1,9},{9,1},{2,10},{10,2},{3,11},{11,3},{4,12},{12,4},... | collective-permute-start | bytes 983048 | tf_op jit(solution)/shard_map/ppermute | solution.py:592

commit v2 on v1

--- a/solution.py
+++ b/solution.py
@@ -172,14 +172,24 @@
     return call(body, [(s, BF16) for s in shapes], [((256, 128), F32)], 1 << 27, *flat)
 
 
-def forward_full(volume, halo_z, halo_y, weights):
-    def body(own, before, after, above, below, taps, pre, act, shifts):
+def forward_full(volume, halo_z, halo_y, weights, skip_half, skip_deep):
+    def body(own, one, two, above, below, taps, skip1, skip3, pre, act, shifts, to_one, to_two):
+        even = lax.axis_index("c") == 0
         for layer in range(10):
-            middle = before if layer == 0 else after if layer == 9 else own
-            at = 0 if layer in (0, 9) else layer - 1
-            put_shifts(shifts, 0, layer, above[layer * 16 : layer * 16 + 16])
-            put_shifts(shifts, 16, layer, middle[at, :128])
-            put_shifts(shifts, 144, layer, below[layer * 16 : layer * 16 + 16])
+            if 0 < layer < 9:
+                parts = [part[layer * 16 : layer * 16 + 16] for part in (above, below)]
+                parts.insert(1, own[layer - 1])
+            else:
+                near, far = (two, one) if layer == 0 else (one, two)
+                at = (144, 0) if layer == 0 else (0, 144)
+                parts = [
+                    jnp.where(even, part[at[0] : at[0] + 16], part[at[1] : at[1] + 16])
+                    for part in (above, below)
+                ]
+                parts.insert(1, jnp.where(even, near[0], far[0]))
+            put_shifts(shifts, 0, layer, parts[0])
+            put_shifts(shifts, 16, layer, parts[1])
+            put_shifts(shifts, 144, layer, parts[2])
         value = convolved(taps, shifts, (0, 160), 8)
         active = silu(value)
         for layer in range(8):
@@ -189,26 +199,46 @@
             act[layer] = pooled(
                 active[:, at : at + 128], active[:, at + 128 : at + 256], 16, 128
             ).astype(BF16)
+        for layer in range(3):
+            rows = slice(layer * 64, layer * 64 + 64)
+            to_one[rows] = jnp.where(even, act[layer + 1], act[layer])
+            to_two[rows] = jnp.where(even, act[layer], act[layer + 1])
+        to_one[192:320] = jnp.where(even, skip1[3], skip1[0])
+        to_two[192:320] = jnp.where(even, skip1[0], skip1[3])
+        to_one[320:] = skip3[...]
+        to_two[320:] = skip3[...]
 
     outs = [((8, 128, 128), F32), ((4, 64, 128), BF16), ((3, 160, 1280), BF16)]
-    return call(body, outs, [], 1 << 29, volume, *halo_z, *halo_y, weights)
+    outs += [((336, 128), BF16), ((336, 128), BF16)]
+    return call(
+        body, outs, [], 1 << 29, volume, *halo_z, *halo_y, weights, skip_half, skip_deep
+    )
 
 
 def forward_half(act, halo_z, halo_y, weights_half, weights_quarter):
     def body(
-        own, before, after, above, below, taps, next_taps, pre, act, next_pre, deep, shifts, inner
+        own, one, two, above, below, taps, next_taps, pre, act, next_pre, deep, shifts, inner
     ):
         flags = place_of()
+        even = flags[4] == 0
         for layer in range(10):
-            if layer < 3:
-                middle = before[layer]
-            elif layer < 7:
+            if 3 <= layer < 7:
+                at = layer * 48
                 middle = own[layer - 3]
+                edges = [part[at : at + 48] for part in (above, below)]
             else:
-                middle = after[layer - 7]
-            put_shifts(shifts, 0, layer, above[layer])
+                near, far = (two, one) if layer < 3 else (one, two)
+                at = layer % 7 * 64
+                middle = jnp.where(even, near[at : at + 64], far[at : at + 64])
+                at = layer % 7 * 48
+                at = (336 + at, at) if layer < 3 else (at, 336 + at)
+                edges = [
+                    jnp.where(even, part[at[0] : at[0] + 48], part[at[1] : at[1] + 48])
+                    for part in (above, below)
+                ]
+            put_shifts(shifts, 0, layer, edges[0])
             put_shifts(shifts, 48, layer, middle)
-            put_shifts(shifts, 112, layer, below[layer])
+            put_shifts(shifts, 112, layer, edges[1])
         for part in range(2):
             value = convolved(taps, shifts, (part * 64, part * 64 + 96), 8)
             for layer in range(8):
@@ -286,7 +316,7 @@
 
 def deepest(columns, before, acts, after, skip_deep, halo_z, halo_y, skip, pre, weights, weights_back):
     def body(
-        before, acts, after, skip_own, skip_before, skip_after, skip_above, skip_below, skip, pre,
+        before, acts, after, skip_own, skip_one, skip_two, skip_above, skip_below, skip, pre,
         taps, taps_back, dense_out, out, shifts, delta_own, deltas,
     ):
         flags = place_of()
@@ -321,12 +351,16 @@
             upstream = jnp.zeros((128, 128), F32)
             for layer in range(3):
                 if near != 1:
-                    at = 352 + layer * 16
-                    dense = (skip_above, skip_below)[near // 2][at : at + 16]
+                    edge = (skip_above, skip_below)[near // 2]
+                    at = 704 - layer * 16
+                    dense = jnp.where(
+                        core == 0, edge[at : at + 16], edge[1392 - at - 16 : 1392 - at]
+                    )
                 elif layer == 1:
                     dense = skip_own[...]
                 else:
-                    dense = (skip_before, skip_after)[layer // 2][0, 256:]
+                    ends = (skip_two, skip_one) if layer == 0 else (skip_one, skip_two)
+                    dense = jnp.where(core == 0, ends[0][320:], ends[1][320:])
                 upstream = upstream + columns_last(dense, 16 * layer + 16)
             keep = (place == 2) | ((place == 1) & (flags[0])) | ((place == 3) & (flags[1]))
             if near != 1:
@@ -431,13 +465,23 @@
     weights_quarter, weights_half, shifts_half, shifts_full, deep_grad, quarter_grad,
 ):
     def body(
-        own, before, after, above, below, skip1, before1, after1, above1, below1, pre1, skip0, pre0,
+        own, one, two, above, below, skip1, one1, two1, above1, below1, pre1, skip0, pre0,
         taps2, taps1, shifts1, shifts0, grad3, grad2, mine, other, moved2, moved1, delta1, delta0, tall, flat,
     ):
         flags = place_of()
+        even = flags[4] == 0
         for layer in range(6):
-            middle = (before, own, after)[layer // 2][0]
-            for part, tile in enumerate((above[layer // 2], middle, below[layer // 2])):
+            block = layer // 2
+            if block == 1:
+                tiles = (above[1], own[0], below[1])
+            else:
+                near, far = (two, one) if block == 0 else (one, two)
+                tiles = (
+                    jnp.where(even, above[2 - block], above[block]),
+                    jnp.where(even, near[0], far[0]),
+                    jnp.where(even, below[2 - block], below[block]),
+                )
+            for part, tile in enumerate(tiles):
                 tile = turned(tile.astype(F32), -32 * (layer % 2))
                 tile = jnp.where(lanes(tile.shape) < 32, tile, 0.0).astype(BF16)
                 put_shifts(moved2, part * 128, layer, tile)
@@ -452,16 +496,18 @@
                 carried = exact_dot(value[:, at : at + 128], picks)
                 parts = [carried[part * 32 : part * 32 + 32] for part in (0, 1, 1, 2, 2, 3)]
                 carried = jnp.concatenate(parts, axis=0)
-            if layer == 0:
-                middle = before1[0, 128:256]
-            elif layer == 5:
-                middle = after1[0, 128:256]
+            if 0 < layer < 5:
+                at = 480 + layer * 32
+                parts = [above1[at : at + 32], skip1[layer - 1], below1[at : at + 32]]
             else:
-                middle = skip1[layer - 1]
-            edge = 160 + layer * 32
-            skip = jnp.concatenate(
-                [above1[edge : edge + 32], middle, below1[edge : edge + 32]], axis=0
-            ).astype(F32)
+                near, far = (two1, one1) if layer == 0 else (one1, two1)
+                at = (640, 480) if layer == 0 else (480, 640)
+                parts = [
+                    jnp.where(even, above1[at[0] : at[0] + 32], above1[at[1] : at[1] + 32]),
+                    jnp.where(even, near[192:320], far[192:320]),
+                    jnp.where(even, below1[at[0] : at[0] + 32], below1[at[1] : at[1] + 32]),
+                ]
+            skip = jnp.concatenate(parts, axis=0).astype(F32)
             change = (skip + carried) * slope(pre1[layer + 1, 32:224])
             keep = inside
             if layer == 0:
@@ -557,15 +603,12 @@
     return lax.ppermute(last, axis, up), lax.ppermute(first, axis, down)
 
 
-def rims(block, depth, rows):
-    before, after = exchange(block[:depth], block[block.shape[0] - depth :], GZ)
-    tall = block.shape[1]
-
-    def edge(start):
-        parts = [part[:, start : start + rows] for part in (before, block, after)]
-        return jnp.concatenate(parts, axis=0)
-
-    return (before, after), exchange(edge(0), edge(tall - rows), "gy")
+def swaps(to_one, to_two):
+    size = lax.axis_size(GZ)
+    on_chip = [(i, i ^ 1) for i in range(size)]
+    between = [(i, i + 1) for i in range(1, size - 1, 2)]
+    between += [(j, i) for i, j in between]
+    return lax.ppermute(to_one, GZ, on_chip), lax.ppermute(to_two, GZ, between)
 
 
 def laid_out(array):
@@ -576,19 +619,14 @@
 
 def summed(mine, other):
     swap = [(0, 1), (1, 0)]
-    columns, planes = lax.axis_size("gy"), lax.axis_size(("x", "z"))
-    rows, width = HALF[0] // columns, HALF[1]
     pair = (mine + lax.ppermute(other, "c", swap)).astype(BF16)
-    pieces = lax.all_to_all(pair.reshape(columns, rows, width), "gy", 0, 0)
-    column = jnp.sum(pieces.astype(F32), axis=0)
-    chunk = rows // planes
-    pieces = lax.all_to_all(column, ("x", "z"), 0, 0, tiled=True)
-    done = jnp.sum(pieces.reshape(planes, chunk, width), axis=0)
-    spread = jnp.broadcast_to(done[None], (planes, chunk, width)).reshape(rows, width)
-    column = lax.all_to_all(lax.optimization_barrier(spread), ("x", "z"), 0, 0, tiled=True)
-    column = column.astype(BF16)
-    spread = lax.optimization_barrier(jnp.broadcast_to(column[None], (columns, rows, width)))
-    half = lax.all_to_all(spread, "gy", 0, 0).reshape(HALF)
+    group = ("x", "z", "gy")
+    count = lax.axis_size(group)
+    chunk, width = HALF[0] // count, HALF[1]
+    pieces = lax.all_to_all(pair, group, 0, 0, tiled=True)
+    done = jnp.sum(pieces.reshape(count, chunk, width).astype(F32), axis=0).astype(BF16)
+    spread = jnp.broadcast_to(done[None], (count, chunk, width)).reshape(HALF)
+    half = lax.all_to_all(lax.optimization_barrier(spread), group, 0, 0, tiled=True)
     return unpack(half, lax.ppermute(half, "c", swap))
 
 
@@ -605,33 +643,40 @@
 ):
     kernels = (kernel_full, kernel_half, kernel_quarter, kernel_eighth)
     volume = laid_out(volume)
-    skip1 = laid_out(skip_half)
-    skip3 = jnp.transpose(skip_eighth, (1, 2, 3, 0)).reshape(1, 16, 128)
+    even = lax.axis_index("c") == 0
+    first, last = volume[:1], volume[7:]
+    one, two = swaps(jnp.where(even, last, first), jnp.where(even, first, last))
+    skip3 = jnp.transpose(skip_eighth, (1, 2, 3, 0)).reshape(16, 128)
     skip2 = jnp.transpose(skip_quarter, (1, 2, 3, 0))
-    first = jnp.concatenate([volume[:1], skip1[:1], skip3], axis=1)
-    last = jnp.concatenate([volume[7:], skip1[3:], skip3], axis=1)
-    before, after = exchange(first, last, GZ)
-    before, after, skip0 = lax.optimization_barrier((before, after, laid_out(skip_full)))
-
-    def edge(start, start1):
-        parts = [
-            part[:, start : start + 16].reshape(-1, 128)
-            for part in (before[:, :128], volume, after[:, :128])
-        ]
-        parts += [
-            part[:, start1 : start1 + 32].reshape(-1, 128)
-            for part in (before[:, 128:256], skip1, after[:, 128:256])
-        ]
-        parts += [before[0, 256:], skip3[0], after[0, 256:]]
-        return jnp.concatenate(parts, axis=0)
-
-    above, below = exchange(edge(0, 0), edge(112, 96), "gy")
-    halo_z0, halo_y0 = (before, after), (above, below)
+    one, two, skip0, skip1 = lax.optimization_barrier(
+        (one, two, laid_out(skip_full), laid_out(skip_half))
+    )
+
+    def flat(parts):
+        return jnp.concatenate([part.reshape(-1, 128) for part in parts], axis=0)
+
+    def edge(start):
+        return flat([part[:, start : start + 16] for part in (one, volume, two)])
+
+    halo_y = exchange(edge(0), edge(112), "gy")
     dims = ((8, 16, 16), (4, 16, 32), (2, 32, 64), (1, 64, 128))
     w0, w1, w2, w3, t1, t2, t3 = prepare(kernels, dims)
-    pre0, act1, shifts0 = forward_full(volume, halo_z0, halo_y0, w0)
-    halo_z, halo_y = rims(act1, 3, 48)
-    pre1, act2, pre2, act3, shifts1 = forward_half(act1, halo_z, halo_y, w1, w2)
+    pre0, act1, shifts0, to_one, to_two = forward_full(
+        volume, (one, two), halo_y, w0, skip1, skip3
+    )
+    halo_z1 = one, two = swaps(to_one, to_two)
+
+    def edge1(start, start1):
+        acts = [part[:192].reshape(3, 64, 128) for part in (one, two)]
+        acts.insert(1, act1)
+        rims = [part[192:320].reshape(1, 128, 128) for part in (one, two)]
+        rims.insert(1, skip1)
+        parts = [part[:, start : start + 48] for part in acts]
+        parts += [part[:, start1 : start1 + 32] for part in rims]
+        return flat(parts + [one[320:], skip3, two[320:]])
+
+    halo_y1 = exchange(edge1(0, 0), edge1(16, 96), "gy")
+    pre1, act2, pre2, act3, shifts1 = forward_half(act1, halo_z1, halo_y1, w1, w2)
     columns = lax.axis_size("gy")
     many = (2 * columns,) + act3.shape
     acts = lax.all_to_all(
@@ -639,13 +684,15 @@
     )
     before, after = exchange(acts, acts, ("x", "z"))
     dense2, delta2, shifts3, delta3 = deepest(
-        columns, before, acts, after, skip3[0], halo_z0, halo_y0, skip2, pre2, w3, t3
-    )
-    halo_z, halo_y = rims(dense2, 1, 128)
+        columns, before, acts, after, skip3, halo_z1, halo_y1, skip2, pre2, w3, t3
+    )
+    halo_z = one, two = swaps(dense2, dense2)
+    block = jnp.concatenate([one, dense2, two], axis=0)
+    halo_y = exchange(block, block, "gy")
     grad3 = grad_deepest(shifts3, delta3)
     grad2 = grad_quarter_of(act2, delta2)
     mine, other = back_rest(
-        dense2, halo_z, halo_y, skip1, halo_z0, halo_y0, pre1, skip0, pre0,
+        dense2, halo_z, halo_y, skip1, halo_z1, halo_y1, pre1, skip0, pre0,
         t2, t1, shifts1, shifts0, grad3, grad2,
     )
     outs = summed(mine, other)

time: 176 us -> 175 us (level)
  blocking collectives: 78.9 us -> 74.6 us
  starting transfers between devices: 52.3 us -> 56.5 us
  waiting for transfers between devices: 23.8 us -> 20.5 us
    ppermute x0 -> x6, starting transfers between devices: none -> 27 us  [the longest x3 14.7 us: swaps(): lax.ppermute(to_one, GZ, on_chip)]
    ppermute x14 -> x8, starting transfers between devices: 43.8 us -> 22.6 us  [exchange(): return (lax.ppermute(last, axis, up), lax.ppermute(first, axis, down))]
    all_to_all x1, blocking collectives: 18.4 us -> 11.2 us  [on_device(): lax.all_to_all(lax.optimization_barrier(jnp.broadcast_to(act3[None], many...]
    ppermute x14 -> x8, waiting for transfers between devices: 20.5 us -> 13.6 us  [exchange(): return (lax.ppermute(last, axis, up), lax.ppermute(first, axis, down))]
    ppermute x0 -> x6, waiting for transfers between devices: none -> 3.66 us  [the longest x3 3.65 us: swaps(): lax.ppermute(to_two, GZ, between)]
    all_to_all x4 -> x2, blocking collectives: 60.5 us -> 63.4 us  [the longest x1 38.1 us: summed(): pieces = lax.all_to_all(pair, group, 0, 0, tiled=True)]
where the time goes in v2:
time: 175 us; the launch traced here: 174 us
  blocking collectives  74.6 us (43%)
  starting transfers between devices  56.5 us (32%)
  waiting for transfers between devices  20.5 us (12%)
  Pallas kernels  12.8 us (7%)
  local copies, waits for them, and re-layouts  4.99 us (3%)
  other arithmetic  3.23 us (2%)
    all_to_all x1, blocking collectives, summed(): pieces = lax.all_to_all(pair, group, 0, 0, tiled=True)  38.1 us
    all_to_all x1, blocking collectives, summed(): lax.all_to_all(lax.optimization_barrier(spread), group, 0, 0, tiled=True)  25.3 us
    ppermute x8, starting transfers between devices, exchange(): return (lax.ppermute(last, axis, up), lax.ppermute(first, axis, down))  22.6 us
    ppermute x3, starting transfers between devices, swaps(): lax.ppermute(to_one, GZ, on_chip)  14.7 us
    ppermute x8, waiting for transfers between devices, exchange(): return (lax.ppermute(last, axis, up), lax.ppermute(first, axis, down))  13.6 us
    pallas_call x8, Pallas kernels, call(): pl.pallas_call(body, out_shape=tuple((jax.ShapeDtypeStruct(shape, dtype)...  12.8 us
    ppermute x3, starting transfers between devices, swaps(): lax.ppermute(to_two, GZ, between)  12.4 us
    all_to_all x1, blocking collectives, on_device(): lax.all_to_all(lax.optimization_barrier(jnp.broadcast_to(act3[None], many...  11.2 us
  transfers between devices with their start and end apart: 16, of which 9 were waited for; matrix products, arithmetic and copies ran while one was open for 1% of the time, Pallas kernels for 1%

profile of v2, /device:TPU:1, one launch (start us, length us, event | category | flops | bytes accessed | tf_op | source)
XLA Modules:
  0.0 173.8 jit_solution(11922416723349106475)
XLA Ops:
  1.6 8.8 %collective-permute-start = (bf16[1,128,128]{2,1,0:T(8,128)(2,1)S(1)}, bf16[1,128,128]{2,1,0:T(8,128)(2,1)S(1)}, u32[]{:S(2)}, u32[]{:S(2)}) collective-permute-start(bf16[1,128,128]{2,1,0:T(8,128)(2,1)S(1)} %bitcast.98), channel_id=1, source_target_pairs={{0,8},{8,0},{16,24},{24,16},{32,40},{40,32},{48,56},{56,48},{64,72... | collective-permute-start | bytes 98312 | tf_op jit(solution)/shard_map/ppermute | solution.py:611
  10.4 1.9 %collective-permute-start.1 = (bf16[1,128,128]{2,1,0:T(8,128)(2,1)S(1)}, bf16[1,128,128]{2,1,0:T(8,128)(2,1)S(1)}, u32[]{:S(2)}, u32[]{:S(2)}) collective-permute-start(bf16[1,128,128]{2,1,0:T(8,128)(2,1)S(1)} %bitcast.99), channel_id=1, source_target_pairs={{8,16},{24,32},{40,48},{56,64},{72,80},{88,96},{104,112},{120,128}... | collective-permute-start | bytes 98312 | tf_op jit(solution)/shard_map/ppermute | solution.py:611
  14.7 1.4 shard_map.120
  16.2 1.3 collective-permute-start.3
  17.5 4.0 %collective-permute-start.2 = (bf16[160,128]{1,0:T(8,128)(2,1)S(1)}, bf16[160,128]{1,0:T(8,128)(2,1)S(1)}, u32[]{:S(2)}, u32[]{:S(2)}) collective-permute-start(bf16[160,128]{1,0:T(8,128)(2,1)S(1)} %pad_maximum_fusion), channel_id=1, source_target_pairs={{0,1},{1,2},{2,3},{3,4},{4,5},{5,6},{6,7},{8,9},{9,10},{10,11},{11... | collective-permute-start | bytes 122888 | tf_op jit(solution)/shard_map/ppermute | solution.py:603
  22.6 1.2 shard_map.121
  23.8 1.9 %collective-permute-start.4 = (bf16[336,128]{1,0:T(8,128)(2,1)S(1)}, bf16[336,128]{1,0:T(8,128)(2,1)S(1)}, u32[]{:S(2)}, u32[]{:S(2)}) collective-permute-start(bf16[336,128]{1,0:T(8,128)(2,1)S(1)} %get-tuple-element.40), channel_id=1, source_target_pairs={{0,8},{8,0},{16,24},{24,16},{32,40},{40,32},{48,56},{56,48},{64,72... | collective-permute-start | bytes 258056 | tf_op jit(solution)/shard_map/ppermute | solution.py:611
  25.7 4.8 %collective-permute-start.5 = (bf16[336,128]{1,0:T(8,128)(2,1)S(1)}, bf16[336,128]{1,0:T(8,128)(2,1)S(1)}, u32[]{:S(2)}, u32[]{:S(2)}) collective-permute-start(bf16[336,128]{1,0:T(8,128)(2,1)S(1)} %get-tuple-element.41), channel_id=1, source_target_pairs={{8,16},{24,32},{40,48},{56,64},{72,80},{88,96},{104,112},{120,128}... | collective-permute-start | bytes 258056 | tf_op jit(solution)/shard_map/ppermute | solution.py:611
  30.6 2.1 %collective-permute-done.5.two.skip_two.two1 = bf16[336,128]{1,0:T(8,128)(2,1)S(1)} collective-permute-done((bf16[336,128]{1,0:T(8,128)(2,1)S(1)}, bf16[336,128]{1,0:T(8,128)(2,1)S(1)}, u32[]{:S(2)}, u32[]{:S(2)}) %collective-permute-start.5) | collective-permute-done | bytes 86048 | tf_op jit(solution)/shard_map/ppermute | solution.py:611
  32.9 4.3 %collective-permute-start.6 = (bf16[720,128]{1,0:T(8,128)(2,1)S(1)}, bf16[720,128]{1,0:T(8,128)(2,1)S(1)}, u32[]{:S(2)}, u32[]{:S(2)}) collective-permute-start(bf16[720,128]{1,0:T(8,128)(2,1)S(1)} %get-tuple-element.73), channel_id=1, source_target_pairs={{0,1},{1,2},{2,3},{3,4},{4,5},{5,6},{6,7},{8,9},{9,10},{10,11},{11... | collective-permute-start | bytes 552968 | tf_op jit(solution)/shard_map/ppermute | solution.py:603
  37.2 1.3 collective-permute-start.7
  39.6 3.8 %collective-permute-done.7.below.skip_below.below1 = bf16[720,128]{1,0:T(8,128)(2,1)S(1)} collective-permute-done((bf16[720,128]{1,0:T(8,128)(2,1)S(1)}, bf16[720,128]{1,0:T(8,128)(2,1)S(1)}, u32[]{:S(2)}, u32[]{:S(2)}) %collective-permute-start.7) | collective-permute-done | bytes 184352 | tf_op jit(solution)/shard_map/ppermute | solution.py:603
  43.4 2.4 %shard_map.122 = (f32[8,256,128]{2,1,0:T(8,128)S(1)}, bf16[4,128,128]{2,1,0:T(8,128)(2,1)S(1)}, f32[2,128,128]{2,1,0:T(8,128)S(1)}, f32[8,128]{1,0:T(8,128)S(1)}, bf16[3,160,1280]{2,1,0:T(8,128)(2,1)S(1)}) custom-call(bf16[4,64,128]{2,1,0:T(8,128)(2,1)S(1)} %get-tuple-element.39.own, bf16[336,128]{1,0:T(8,128)(2,1)S(1)} %collective-permute-done.4.one.skip_one.one1, ...), custom_call_target="tpu_custom_call" | custom-call | flops 536870912 | bytes 1048576 | tf_op jit(solution)/shard_map/pallas_call | solution.py:17
  45.8 11.2 %all_to_all.25.acts = f32[16,8,128]{2,1,0:T(8,128)S(1)} all-to-all(f32[16,8,128]{2,1,0:T(8,128)S(1)} %broadcast_in_dim.2), channel_id=1, replica_groups=mesh['x'=4,'z'=8,'c'=2,'gy'=8] {'c','gy'}, dimensions={0} | all-to-all | bytes 131072 | tf_op jit(solution)/shard_map/all_to_all | solution.py:682
  57.1 6.5 %collective-permute-start.8 = (f32[16,8,128]{2,1,0:T(8,128)S(1)}, f32[16,8,128]{2,1,0:T(8,128)S(1)}, u32[]{:S(2)}, u32[]{:S(2)}) collective-permute-start(f32[16,8,128]{2,1,0:T(8,128)S(1)} %all_to_all.25.acts), channel_id=1, source_target_pairs={{0,16},{16,32},{32,48},{48,64},{64,80},{80,96},{96,112},{112,128},... | collective-permute-start | bytes 196616 | tf_op jit(solution)/shard_map/ppermute | solution.py:603
  63.6 1.3 collective-permute-start.9
  64.9 4.3 %collective-permute-done.9.after = f32[16,8,128]{2,1,0:T(8,128)S(1)} collective-permute-done((f32[16,8,128]{2,1,0:T(8,128)S(1)}, f32[16,8,128]{2,1,0:T(8,128)S(1)}, u32[]{:S(2)}, u32[]{:S(2)}) %collective-permute-start.9) | collective-permute-done | bytes 65568 | tf_op jit(solution)/shard_map/ppermute | solution.py:603
  69.2 1.8 %shard_map.123 = (bf16[1,128,128]{2,1,0:T(8,128)(2,1)S(1)}, bf16[2,128,128]{2,1,0:T(8,128)(2,1)S(1)}, bf16[9,320,128]{2,1,0:T(8,128)(2,1)S(1)}, bf16[128,128]{1,0:T(8,128)(2,1)S(1)}) custom-call(f32[16,8,128]{2,1,0:T(8,128)S(1)} %collective-permute-done.8.before, f32[16,8,128]{2,1,0:T(8,128)S(1)} %all_to_all.25.acts, ...), custom_call_target="tpu_custom_call" | custom-call | flops 268435456 | bytes 1048576 | tf_op jit(solution)/shard_map/pallas_call | solution.py:17
  71.0 4.0 %collective-permute-start.10 = (bf16[1,128,128]{2,1,0:T(8,128)(2,1)S(1)}, bf16[1,128,128]{2,1,0:T(8,128)(2,1)S(1)}, u32[]{:S(2)}, u32[]{:S(2)}) collective-permute-start(bf16[1,128,128]{2,1,0:T(8,128)(2,1)S(1)} %get-tuple-element.48.own), channel_id=1, source_target_pairs={{0,8},{8,0},{16,24},{24,16},{32,40},{40,32},{48,56},{56,48},{64,72... | collective-permute-start | bytes 98312 | tf_op jit(solution)/shard_map/ppermute | solution.py:611
  75.0 5.7 %collective-permute-start.11 = (bf16[1,128,128]{2,1,0:T(8,128)(2,1)S(1)}, bf16[1,128,128]{2,1,0:T(8,128)(2,1)S(1)}, u32[]{:S(2)}, u32[]{:S(2)}) collective-permute-start(bf16[1,128,128]{2,1,0:T(8,128)(2,1)S(1)} %get-tuple-element.48.own), channel_id=1, source_target_pairs={{8,16},{24,32},{40,48},{56,64},{72,80},{88,96},{104,112},{120,128}... | collective-permute-start | bytes 98312 | tf_op jit(solution)/shard_map/ppermute | solution.py:611
  80.7 1.5 collective-permute-done.11.two
  82.2 2.7 %collective-permute-start.12 = (bf16[3,128,128]{2,1,0:T(8,128)(2,1)S(1)}, bf16[3,128,128]{2,1,0:T(8,128)(2,1)S(1)}, u32[]{:S(2)}, u32[]{:S(2)}) collective-permute-start(bf16[3,128,128]{2,1,0:T(8,128)(2,1)S(1)} %constant_dynamic-update-slice_fusion.18), channel_id=1, source_target_pairs={{0,1},{1,2},{2,3},{3,4},{4,5},{5,6},{6,7},{8,9},{9,10},{10,11},{11... | collective-permute-start | bytes 294920 | tf_op jit(solution)/shard_map/ppermute | solution.py:603
  84.9 1.3 collective-permute-start.13
  87.0 3.3 %collective-permute-done.13.below = bf16[3,128,128]{2,1,0:T(8,128)(2,1)S(1)} collective-permute-done((bf16[3,128,128]{2,1,0:T(8,128)(2,1)S(1)}, bf16[3,128,128]{2,1,0:T(8,128)(2,1)S(1)}, u32[]{:S(2)}, u32[]{:S(2)}) %collective-permute-start.13) | collective-permute-done | bytes 98336 | tf_op jit(solution)/shard_map/ppermute | solution.py:603
  90.3 3.8 %shard_map.126 = (f32[256,640]{1,0:T(8,128)S(1)}, f32[256,640]{1,0:T(8,128)S(1)}) custom-call(bf16[1,128,128]{2,1,0:T(8,128)(2,1)S(1)} %get-tuple-element.48.own, bf16[1,128,128]{2,1,0:T(8,128)(2,1)S(1)} %collective-permute-done.10.one, bf16[1,128,128]{2,1,0:T(8,128)(2,1)S(1)} %collective-permute-done.11.two, ...), custom_call_target="tpu_custom_call" | custom-call | flops 1073741824 | bytes 1048576 | tf_op jit(solution)/shard_map/pallas_call | solution.py:17
  94.0 1.9 %collective-permute-start.14 = (f32[256,640]{1,0:T(8,128)S(1)}, f32[256,640]{1,0:T(8,128)S(1)}, u32[]{:S(2)}, u32[]{:S(2)}) collective-permute-start(f32[256,640]{1,0:T(8,128)S(1)} %get-tuple-element.61), channel_id=1, source_target_pairs={{0,8},{8,0},{1,9},{9,1},{2,10},{10,2},{3,11},{11,3},{4,12},{12,4},... | collective-permute-start | bytes 1966088 | tf_op jit(solution)/shard_map/ppermute | solution.py:622
  96.0 2.1 %collective-permute-done.14 = f32[256,640]{1,0:T(8,128)S(1)} collective-permute-done((f32[256,640]{1,0:T(8,128)S(1)}, f32[256,640]{1,0:T(8,128)S(1)}, u32[]{:S(2)}, u32[]{:S(2)}) %collective-permute-start.14) | collective-permute-done | bytes 655392 | tf_op jit(solution)/shard_map/ppermute | solution.py:622
  99.8 38.1 %all_to_all.26 = bf16[256,2,320]{2,1,0:T(2,128)(2,1)S(1)} all-to-all(bf16[256,2,320]{2,1,0:T(2,128)(2,1)S(1)} %reshape.209), channel_id=1, replica_groups=mesh['x'=4,'z'=8,'c'=2,'gy'=8] {'x','z','gy'}, dimensions={0} | all-to-all | bytes 655360 | tf_op jit(solution)/shard_map/all_to_all | solution.py:626
  140.3 25.3 %all_to_all.27 = bf16[256,2,320]{2,1,0:T(2,128)(2,1)S(1)} all-to-all(bf16[256,2,320]{2,1,0:T(2,128)(2,1)S(1)} %reshape.211), channel_id=1, replica_groups=mesh['x'=4,'z'=8,'c'=2,'gy'=8] {'x','z','gy'}, dimensions={0} | all-to-all | bytes 655360 | tf_op jit(solution)/shard_map/all_to_all | solution.py:629
  166.2 4.9 %collective-permute-start.15 = (bf16[256,640]{1,0:T(8,128)(2,1)S(1)}, bf16[256,640]{1,0:T(8,128)(2,1)S(1)}, u32[]{:S(2)}, u32[]{:S(2)}) collective-permute-start(bf16[256,640]{1,0:T(8,128)(2,1)S(1)} %bitcast.68), channel_id=1, source_target_pairs={{0,8},{8,0},{1,9},{9,1},{2,10},{10,2},{3,11},{11,3},{4,12},{12,4},... | collective-permute-start | bytes 983048 | tf_op jit(solution)/shard_map/ppermute | solution.py:630
  171.1 1.2 collective-permute-done.15.other
  172.4 1.4 shard_map.127
  (72 shorter events, 11.2 us)
Async XLA Ops:
  0.6 14.0 %copy-start.6 = (bf16[32,4,4,64]{3,2,1,0:T(4,128)(2,1)S(1)}, bf16[32,4,4,64]{3,2,1,0:T(4,128)(2,1)}, u32[]{:S(2)}) copy-start(bf16[32,4,4,64]{3,2,1,0:T(4,128)(2,1)} %param.15) | copy-start | bytes 196612
  0.6 14.0 %copy-start.2 = (bf16[3,3,3,16,16]{4,3,2,1,0:T(8,128)(2,1)S(1)}, bf16[3,3,3,16,16]{4,3,2,1,0:T(8,128)(2,1)}, u32[]{:S(2)}) copy-start(bf16[3,3,3,16,16]{4,3,2,1,0:T(8,128)(2,1)} %param.10) | copy-start | bytes 41476
  0.7 14.0 %copy-start.3 = (bf16[3,3,3,16,32]{4,3,2,1,0:T(8,128)(2,1)S(1)}, bf16[3,3,3,16,32]{4,3,2,1,0:T(8,128)(2,1)}, u32[]{:S(2)}) copy-start(bf16[3,3,3,16,32]{4,3,2,1,0:T(8,128)(2,1)} %param.11) | copy-start | bytes 82948
  0.7 14.0 %copy-start.1 = (bf16[3,3,3,32,64]{4,3,2,1,0:T(8,128)(2,1)S(1)}, bf16[3,3,3,32,64]{4,3,2,1,0:T(8,128)(2,1)}, u32[]{:S(2)}) copy-start(bf16[3,3,3,32,64]{4,3,2,1,0:T(8,128)(2,1)} %param.12) | copy-start | bytes 331780
  0.7 14.0 %copy-start = (bf16[3,3,3,64,128]{4,3,2,1,0:T(8,128)(2,1)S(1)}, bf16[3,3,3,64,128]{4,3,2,1,0:T(8,128)(2,1)}, u32[]{:S(2)}) copy-start(bf16[3,3,3,64,128]{4,3,2,1,0:T(8,128)(2,1)} %param.13) | copy-start | bytes 1327108
  1.6 14.6 %collective-permute-start = (bf16[1,128,128]{2,1,0:T(8,128)(2,1)S(1)}, bf16[1,128,128]{2,1,0:T(8,128)(2,1)S(1)}, u32[]{:S(2)}, u32[]{:S(2)}) collective-permute-start(bf16[1,128,128]{2,1,0:T(8,128)(2,1)S(1)} %bitcast.98), channel_id=1, source_target_pairs={{0,8},{8,0},{16,24},{24,16},{32,40},{40,32},{48,56},{56,48},{64,72... | collective-permute-start | bytes 98312 | tf_op jit(solution)/shard_map/ppermute | solution.py:611
  10.4 5.8 %collective-permute-start.1 = (bf16[1,128,128]{2,1,0:T(8,128)(2,1)S(1)}, bf16[1,128,128]{2,1,0:T(8,128)(2,1)S(1)}, u32[]{:S(2)}, u32[]{:S(2)}) collective-permute-start(bf16[1,128,128]{2,1,0:T(8,128)(2,1)S(1)} %bitcast.99), channel_id=1, source_target_pairs={{8,16},{24,32},{40,48},{56,64},{72,80},{88,96},{104,112},{120,128}... | collective-permute-start | bytes 98312 | tf_op jit(solution)/shard_map/ppermute | solution.py:611
  13.4 9.1 %copy-start.5 = (bf16[128,1,1,16]{0,3,2,1:T(8,128)(2,1)S(1)}, bf16[128,1,1,16]{0,3,2,1:T(8,128)(2,1)}, u32[]{:S(2)}) copy-start(bf16[128,1,1,16]{0,3,2,1:T(8,128)(2,1)} %param.17) | copy-start | bytes 12292
  16.2 5.3 %collective-permute-start.3 = (bf16[160,128]{1,0:T(8,128)(2,1)S(1)}, bf16[160,128]{1,0:T(8,128)(2,1)S(1)}, u32[]{:S(2)}, u32[]{:S(2)}) collective-permute-start(bf16[160,128]{1,0:T(8,128)(2,1)S(1)} %pad_maximum_fusion.1), channel_id=1, source_target_pairs={{1,0},{2,1},{3,2},{4,3},{5,4},{6,5},{7,6},{9,8},{10,9},{11,10},{12... | collective-permute-start | bytes 122888 | tf_op jit(solution)/shard_map/ppermute | solution.py:603
  17.5 5.1 %collective-permute-start.2 = (bf16[160,128]{1,0:T(8,128)(2,1)S(1)}, bf16[160,128]{1,0:T(8,128)(2,1)S(1)}, u32[]{:S(2)}, u32[]{:S(2)}) collective-permute-start(bf16[160,128]{1,0:T(8,128)(2,1)S(1)} %pad_maximum_fusion), channel_id=1, source_target_pairs={{0,1},{1,2},{2,3},{3,4},{4,5},{5,6},{6,7},{8,9},{9,10},{10,11},{11... | collective-permute-start | bytes 122888 | tf_op jit(solution)/shard_map/ppermute | solution.py:603
  23.8 6.7 %collective-permute-start.4 = (bf16[336,128]{1,0:T(8,128)(2,1)S(1)}, bf16[336,128]{1,0:T(8,128)(2,1)S(1)}, u32[]{:S(2)}, u32[]{:S(2)}) collective-permute-start(bf16[336,128]{1,0:T(8,128)(2,1)S(1)} %get-tuple-element.40), channel_id=1, source_target_pairs={{0,8},{8,0},{16,24},{24,16},{32,40},{40,32},{48,56},{56,48},{64,72... | collective-permute-start | bytes 258056 | tf_op jit(solution)/shard_map/ppermute | solution.py:611
  25.7 6.9 %collective-permute-start.5 = (bf16[336,128]{1,0:T(8,128)(2,1)S(1)}, bf16[336,128]{1,0:T(8,128)(2,1)S(1)}, u32[]{:S(2)}, u32[]{:S(2)}) collective-permute-start(bf16[336,128]{1,0:T(8,128)(2,1)S(1)} %get-tuple-element.41), channel_id=1, source_target_pairs={{8,16},{24,32},{40,48},{56,64},{72,80},{88,96},{104,112},{120,128}... | collective-permute-start | bytes 258056 | tf_op jit(solution)/shard_map/ppermute | solution.py:611
  32.8 36.4 %copy-start.4 = (bf16[64,2,2,32]{0,3,2,1:T(8,128)(2,1)S(1)}, bf16[64,2,2,32]{0,3,2,1:T(8,128)(2,1)}, u32[]{:S(2)}) copy-start(bf16[64,2,2,32]{0,3,2,1:T(8,128)(2,1)} %param.16) | copy-start | bytes 49156
  32.9 6.7 %collective-permute-start.6 = (bf16[720,128]{1,0:T(8,128)(2,1)S(1)}, bf16[720,128]{1,0:T(8,128)(2,1)S(1)}, u32[]{:S(2)}, u32[]{:S(2)}) collective-permute-start(bf16[720,128]{1,0:T(8,128)(2,1)S(1)} %get-tuple-element.73), channel_id=1, source_target_pairs={{0,1},{1,2},{2,3},{3,4},{4,5},{5,6},{6,7},{8,9},{9,10},{10,11},{11... | collective-permute-start | bytes 552968 | tf_op jit(solution)/shard_map/ppermute | solution.py:603
  37.2 6.3 %collective-permute-start.7 = (bf16[720,128]{1,0:T(8,128)(2,1)S(1)}, bf16[720,128]{1,0:T(8,128)(2,1)S(1)}, u32[]{:S(2)}, u32[]{:S(2)}) collective-permute-start(bf16[720,128]{1,0:T(8,128)(2,1)S(1)} %get-tuple-element.72), channel_id=1, source_target_pairs={{1,0},{2,1},{3,2},{4,3},{5,4},{6,5},{7,6},{9,8},{10,9},{11,10},{12... | collective-permute-start | bytes 552968 | tf_op jit(solution)/shard_map/ppermute | solution.py:603
  57.1 7.9 %collective-permute-start.8 = (f32[16,8,128]{2,1,0:T(8,128)S(1)}, f32[16,8,128]{2,1,0:T(8,128)S(1)}, u32[]{:S(2)}, u32[]{:S(2)}) collective-permute-start(f32[16,8,128]{2,1,0:T(8,128)S(1)} %all_to_all.25.acts), channel_id=1, source_target_pairs={{0,16},{16,32},{32,48},{48,64},{64,80},{80,96},{96,112},{112,128},... | collective-permute-start | bytes 196616 | tf_op jit(solution)/shard_map/ppermute | solution.py:603
  63.6 5.6 %collective-permute-start.9 = (f32[16,8,128]{2,1,0:T(8,128)S(1)}, f32[16,8,128]{2,1,0:T(8,128)S(1)}, u32[]{:S(2)}, u32[]{:S(2)}) collective-permute-start(f32[16,8,128]{2,1,0:T(8,128)S(1)} %all_to_all.25.acts), channel_id=1, source_target_pairs={{16,0},{32,16},{48,32},{64,48},{80,64},{96,80},{112,96},{128,112},... | collective-permute-start | bytes 196616 | tf_op jit(solution)/shard_map/ppermute | solution.py:603
  71.0 9.6 %collective-permute-start.10 = (bf16[1,128,128]{2,1,0:T(8,128)(2,1)S(1)}, bf16[1,128,128]{2,1,0:T(8,128)(2,1)S(1)}, u32[]{:S(2)}, u32[]{:S(2)}) collective-permute-start(bf16[1,128,128]{2,1,0:T(8,128)(2,1)S(1)} %get-tuple-element.48.own), channel_id=1, source_target_pairs={{0,8},{8,0},{16,24},{24,16},{32,40},{40,32},{48,56},{56,48},{64,72... | collective-permute-start | bytes 98312 | tf_op jit(solution)/shard_map/ppermute | solution.py:611
  75.0 7.2 %collective-permute-start.11 = (bf16[1,128,128]{2,1,0:T(8,128)(2,1)S(1)}, bf16[1,128,128]{2,1,0:T(8,128)(2,1)S(1)}, u32[]{:S(2)}, u32[]{:S(2)}) collective-permute-start(bf16[1,128,128]{2,1,0:T(8,128)(2,1)S(1)} %get-tuple-element.48.own), channel_id=1, source_target_pairs={{8,16},{24,32},{40,48},{56,64},{72,80},{88,96},{104,112},{120,128}... | collective-permute-start | bytes 98312 | tf_op jit(solution)/shard_map/ppermute | solution.py:611
  82.2 4.7 %collective-permute-start.12 = (bf16[3,128,128]{2,1,0:T(8,128)(2,1)S(1)}, bf16[3,128,128]{2,1,0:T(8,128)(2,1)S(1)}, u32[]{:S(2)}, u32[]{:S(2)}) collective-permute-start(bf16[3,128,128]{2,1,0:T(8,128)(2,1)S(1)} %constant_dynamic-update-slice_fusion.18), channel_id=1, source_target_pairs={{0,1},{1,2},{2,3},{3,4},{4,5},{5,6},{6,7},{8,9},{9,10},{10,11},{11... | collective-permute-start | bytes 294920 | tf_op jit(solution)/shard_map/ppermute | solution.py:603
  84.9 5.4 %collective-permute-start.13 = (bf16[3,128,128]{2,1,0:T(8,128)(2,1)S(1)}, bf16[3,128,128]{2,1,0:T(8,128)(2,1)S(1)}, u32[]{:S(2)}, u32[]{:S(2)}) collective-permute-start(bf16[3,128,128]{2,1,0:T(8,128)(2,1)S(1)} %constant_dynamic-update-slice_fusion.18), channel_id=1, source_target_pairs={{1,0},{2,1},{3,2},{4,3},{5,4},{6,5},{7,6},{9,8},{10,9},{11,10},{12... | collective-permute-start | bytes 294920 | tf_op jit(solution)/shard_map/ppermute | solution.py:603
  94.0 4.0 %collective-permute-start.14 = (f32[256,640]{1,0:T(8,128)S(1)}, f32[256,640]{1,0:T(8,128)S(1)}, u32[]{:S(2)}, u32[]{:S(2)}) collective-permute-start(f32[256,640]{1,0:T(8,128)S(1)} %get-tuple-element.61), channel_id=1, source_target_pairs={{0,8},{8,0},{1,9},{9,1},{2,10},{10,2},{3,11},{11,3},{4,12},{12,4},... | collective-permute-start | bytes 1966088 | tf_op jit(solution)/shard_map/ppermute | solution.py:622
  166.2 6.2 %collective-permute-start.15 = (bf16[256,640]{1,0:T(8,128)(2,1)S(1)}, bf16[256,640]{1,0:T(8,128)(2,1)S(1)}, u32[]{:S(2)}, u32[]{:S(2)}) collective-permute-start(bf16[256,640]{1,0:T(8,128)(2,1)S(1)} %bitcast.68), channel_id=1, source_target_pairs={{0,8},{8,0},{1,9},{9,1},{2,10},{10,2},{3,11},{11,3},{4,12},{12,4},... | collective-permute-start | bytes 983048 | tf_op jit(solution)/shard_map/ppermute | solution.py:630

commit v3 on v2

--- a/solution.py
+++ b/solution.py
@@ -9,7 +9,6 @@
 BF16 = jnp.bfloat16
 GZ = ("x", "z", "c")
 VMEM_BYTES = 14 * 1024 * 1024
-HALF = (256, 640)
 NT = (((1,), (1,)), ((), ()))
 
 
@@ -314,9 +313,9 @@
     return jnp.concatenate(parts, axis=0)
 
 
-def deepest(columns, before, acts, after, skip_deep, halo_z, halo_y, skip, pre, weights, weights_back):
+def deepest(columns, acts, skip_deep, halo_z, halo_y, skip, pre, weights, weights_back):
     def body(
-        before, acts, after, skip_own, skip_one, skip_two, skip_above, skip_below, skip, pre,
+        acts, skip_own, skip_one, skip_two, skip_above, skip_below, skip, pre,
         taps, taps_back, dense_out, out, shifts, delta_own, deltas,
     ):
         flags = place_of()
@@ -324,8 +323,7 @@
         place = lanes((64, 128)) // 16
 
         def cells(position, row):
-            source = (before, acts, after)[position // 2]
-            return source[position % 2 * columns + row]
+            return acts[position % 2 * columns + row, position // 2]
 
         for near in range(5):
             row = row_at + near - 2
@@ -398,7 +396,7 @@
     scratch = [((384, 128), F32)]
     return call(
         body, outs, scratch, 1 << 28,
-        before, acts, after, skip_deep, *halo_z, *halo_y, skip, pre, weights, weights_back,
+        acts, skip_deep, *halo_z, *halo_y, skip, pre, weights, weights_back,
     )
 
 
@@ -466,7 +464,7 @@
 ):
     def body(
         own, one, two, above, below, skip1, one1, two1, above1, below1, pre1, skip0, pre0,
-        taps2, taps1, shifts1, shifts0, grad3, grad2, mine, other, moved2, moved1, delta1, delta0, tall, flat,
+        taps2, taps1, shifts1, shifts0, grad3, grad2, out, moved2, moved1, delta1, delta0, tall, flat,
     ):
         flags = place_of()
         even = flags[4] == 0
@@ -535,13 +533,9 @@
         put_grads(tall, shifts0, (0, 160), 0, 8, delta0[...], (8, 16, 16))
         flat[2272:2328, :] = packed(tall, 8)
         flat[2328:, :] = jnp.zeros((2560 - 2328, 128), F32)
-        core = flags[4]
         for part in range(5):
-            block = slice(part * 128, part * 128 + 128)
-            mine[:, block] = flat[pl.ds(pl.multiple_of(part * 512 + core * 256, 256), 256), :]
-            other[:, block] = flat[
-                pl.ds(pl.multiple_of(part * 512 + (1 - core) * 256, 256), 256), :
-            ]
+            at = part * 512
+            out[:, part * 128 : part * 128 + 128] = flat[at : at + 512, :].astype(BF16)
 
     scratch = [
         ((3, 384, 768), BF16),
@@ -552,21 +546,17 @@
         ((2560, 128), F32),
     ]
     return call(
-        body, [(HALF, F32), (HALF, F32)], scratch, 1 << 30,
+        body, [((512, 640), BF16)], scratch, 1 << 30,
         delta, *halo_z, *halo_y, skip_half, *halo_zs, *halo_ys, pre_half, skip_full, pre_full,
         weights_quarter, weights_half, shifts_half, shifts_full, deep_grad, quarter_grad,
-    )
-
-
-def unpack(mine, other):
-    def body(mine, other, full, half, quarter, eighth, whole, tall):
-        core = lax.axis_index("c")
+    )[0]
+
+
+def unpack(sums):
+    def body(sums, full, half, quarter, eighth, whole, tall):
         for part in range(5):
-            block = slice(part * 128, part * 128 + 128)
-            at = part * 512 + core * 256
-            whole[pl.ds(pl.multiple_of(at, 256), 256), :] = mine[:, block].astype(F32)
-            at = part * 512 + (1 - core) * 256
-            whole[pl.ds(pl.multiple_of(at, 256), 256), :] = other[:, block].astype(F32)
+            block = sums[:, part * 128 : part * 128 + 128]
+            whole[part * 512 : part * 512 + 512, :] = block.astype(F32)
 
         def spread(out, source, chans):
             for down in range(3):
@@ -593,7 +583,7 @@
 
     outs = [((432, 16), F32), ((432, 32), F32), ((864, 64), F32), ((1728, 128), F32)]
     scratch = [((2560, 128), F32), ((864, 128), F32)]
-    return call(body, outs, scratch, 1 << 20, mine, other)
+    return call(body, outs, scratch, 1 << 20, sums)
 
 
 def exchange(first, last, axis):
@@ -617,17 +607,26 @@
     return jnp.pad(rows, ((0, 0), (0, 0), (0, 128 - width)))
 
 
-def summed(mine, other):
-    swap = [(0, 1), (1, 0)]
-    pair = (mine + lax.ppermute(other, "c", swap)).astype(BF16)
-    group = ("x", "z", "gy")
-    count = lax.axis_size(group)
-    chunk, width = HALF[0] // count, HALF[1]
-    pieces = lax.all_to_all(pair, group, 0, 0, tiled=True)
-    done = jnp.sum(pieces.reshape(count, chunk, width).astype(F32), axis=0).astype(BF16)
-    spread = jnp.broadcast_to(done[None], (count, chunk, width)).reshape(HALF)
-    half = lax.all_to_all(lax.optimization_barrier(spread), group, 0, 0, tiled=True)
-    return unpack(half, lax.ppermute(half, "c", swap))
+def copies(part, count):
+    def body(part, out):
+        value = part[...].astype(BF16)
+        for copy in range(count):
+            out[copy] = value
+
+    return call(body, [((count,) + part.shape, BF16)], [], 1 << 20, part)[0]
+
+
+def summed(terms):
+    inner, outer = ("x", "c"), ("z", "gy")
+    first, second = lax.axis_size(inner), lax.axis_size(outer)
+    rows, width = terms.shape[0] // first, terms.shape[1]
+    pieces = lax.all_to_all(terms.reshape(first, rows, width), inner, 0, 0)
+    part = jnp.sum(pieces.astype(F32), axis=0)
+    pieces = lax.all_to_all(part, outer, 0, 0, tiled=True)
+    done = jnp.sum(pieces.reshape(second, -1, width), axis=0)
+    spread = jnp.broadcast_to(done[None], (second,) + done.shape).reshape(rows, width)
+    part = lax.all_to_all(lax.optimization_barrier(spread), outer, 0, 0, tiled=True)
+    return lax.all_to_all(copies(part, first), inner, 0, 0).reshape(terms.shape)
 
 
 def on_device(
@@ -648,8 +647,8 @@
     one, two = swaps(jnp.where(even, last, first), jnp.where(even, first, last))
     skip3 = jnp.transpose(skip_eighth, (1, 2, 3, 0)).reshape(16, 128)
     skip2 = jnp.transpose(skip_quarter, (1, 2, 3, 0))
-    one, two, skip0, skip1 = lax.optimization_barrier(
-        (one, two, laid_out(skip_full), laid_out(skip_half))
+    one, two, skip0, skip1, kernels = lax.optimization_barrier(
+        (one, two, laid_out(skip_full), laid_out(skip_half), kernels)
     )
 
     def flat(parts):
@@ -678,24 +677,25 @@
     halo_y1 = exchange(edge1(0, 0), edge1(16, 96), "gy")
     pre1, act2, pre2, act3, shifts1 = forward_half(act1, halo_z1, halo_y1, w1, w2)
     columns = lax.axis_size("gy")
-    many = (2 * columns,) + act3.shape
+    before, after = exchange(act3, act3, ("x", "z"))
+    chips = jnp.stack([before, act3, after])
+    many = (2 * columns,) + chips.shape
     acts = lax.all_to_all(
-        lax.optimization_barrier(jnp.broadcast_to(act3[None], many)), ("c", "gy"), 0, 0
-    )
-    before, after = exchange(acts, acts, ("x", "z"))
+        lax.optimization_barrier(jnp.broadcast_to(chips[None], many)), ("c", "gy"), 0, 0
+    )
     dense2, delta2, shifts3, delta3 = deepest(
-        columns, before, acts, after, skip3, halo_z1, halo_y1, skip2, pre2, w3, t3
+        columns, acts, skip3, halo_z1, halo_y1, skip2, pre2, w3, t3
     )
     halo_z = one, two = swaps(dense2, dense2)
     block = jnp.concatenate([one, dense2, two], axis=0)
     halo_y = exchange(block, block, "gy")
     grad3 = grad_deepest(shifts3, delta3)
     grad2 = grad_quarter_of(act2, delta2)
-    mine, other = back_rest(
+    terms = back_rest(
         dense2, halo_z, halo_y, skip1, halo_z1, halo_y1, pre1, skip0, pre0,
         t2, t1, shifts1, shifts0, grad3, grad2,
     )
-    outs = summed(mine, other)
+    outs = unpack(summed(terms))
     return tuple(out.reshape(kernel.shape) for out, kernel in zip(outs, kernels))
 
 

time: 175 us -> 175 us (level)
  blocking collectives: 74.6 us -> 102 us
  starting transfers between devices: 56.5 us -> 44 us
  waiting for transfers between devices: 20.5 us -> 10.6 us
  local copies, waits for them, and re-layouts: 4.99 us -> 2.81 us
  other arithmetic: 3.23 us -> 1.1 us
    all_to_all x3 -> x5, blocking collectives: 74.6 us -> 102 us  [the longest x1 29.4 us: summed(): pieces = lax.all_to_all(terms.reshape(first, rows, width), inner, 0, 0)]
    ppermute x8, waiting for transfers between devices: 13.6 us -> 6 us  [exchange(): return (lax.ppermute(last, axis, up), lax.ppermute(first, axis, down))]
    ppermute x2 -> x0, starting transfers between devices: 6.84 us -> none  [the longest x1 4.92 us: summed(): return unpack(half, lax.ppermute(half, 'c', swap))]
    ppermute x2 -> x0, waiting for transfers between devices: 3.3 us -> none  [the longest x1 2.06 us: summed(): pair = (mine + lax.ppermute(other, 'c', swap)).astype(BF16)]
    ppermute x3, starting transfers between devices: 12.4 us -> 9.67 us  [swaps(): lax.ppermute(to_two, GZ, between)]
    ppermute x8, starting transfers between devices: 22.6 us -> 20.7 us  [exchange(): return (lax.ppermute(last, axis, up), lax.ppermute(first, axis, down))]
    unnamed x33 -> x29, local copies, waits for them, and re-layouts: 2.01 us -> 0.17 us
    pallas_call x8 -> x9, Pallas kernels: 12.8 us -> 12.6 us  [call(): pl.pallas_call(body, out_shape=tuple((jax.ShapeDtypeStruct(shape, dtype)...]
  transfers between devices with their start and end apart: 16 -> 14, of which waited for: 9 -> 8; matrix products, arithmetic and copies ran while one was open for 1% -> 1% of each run, Pallas kernels for 1% -> 1%
where the time goes in v3:
time: 175 us
  blocking collectives  102 us (58%)
  starting transfers between devices  44 us (25%)
  Pallas kernels  12.6 us (7%)
  waiting for transfers between devices  10.6 us (6%)
  local copies, waits for them, and re-layouts  2.81 us (2%)
    all_to_all x1, blocking collectives, summed(): pieces = lax.all_to_all(terms.reshape(first, rows, width), inner, 0, 0)  29.4 us
    ppermute x8, starting transfers between devices, exchange(): return (lax.ppermute(last, axis, up), lax.ppermute(first, axis, down))  20.7 us
    all_to_all x1, blocking collectives, on_device(): lax.all_to_all(lax.optimization_barrier(jnp.broadcast_to(chips[None], man...  20.2 us
    all_to_all x1, blocking collectives, summed(): pieces = lax.all_to_all(part, outer, 0, 0, tiled=True)  20.1 us
    all_to_all x1, blocking collectives, summed(): return lax.all_to_all(copies(part, first), inner, 0, 0).reshape(terms.shape)  17 us
    all_to_all x1, blocking collectives, summed(): lax.all_to_all(lax.optimization_barrier(spread), outer, 0, 0, tiled=True)  15.6 us
    ppermute x3, starting transfers between devices, swaps(): lax.ppermute(to_one, GZ, on_chip)  13.6 us
    pallas_call x9, Pallas kernels, call(): pl.pallas_call(body, out_shape=tuple((jax.ShapeDtypeStruct(shape, dtype)...  12.6 us
  transfers between devices with their start and end apart: 14, of which 8 were waited for; matrix products, arithmetic and copies ran while one was open for 1% of the time, Pallas kernels for 1%

profile of v3, /device:TPU:1, one launch (start us, length us, event | category | flops | bytes accessed | tf_op | source)
XLA Modules:
  0.0 174.6 jit_solution(12705738599792788580)
XLA Ops:
  1.6 8.8 %collective-permute-start = (bf16[1,128,128]{2,1,0:T(8,128)(2,1)S(1)}, bf16[1,128,128]{2,1,0:T(8,128)(2,1)S(1)}, u32[]{:S(2)}, u32[]{:S(2)}) collective-permute-start(bf16[1,128,128]{2,1,0:T(8,128)(2,1)S(1)} %bitcast.101), channel_id=1, source_target_pairs={{0,8},{8,0},{16,24},{24,16},{32,40},{40,32},{48,56},{56,48},{64,72... | collective-permute-start | bytes 98312 | tf_op jit(solution)/shard_map/ppermute | solution.py:601
  10.4 1.9 %collective-permute-start.1 = (bf16[1,128,128]{2,1,0:T(8,128)(2,1)S(1)}, bf16[1,128,128]{2,1,0:T(8,128)(2,1)S(1)}, u32[]{:S(2)}, u32[]{:S(2)}) collective-permute-start(bf16[1,128,128]{2,1,0:T(8,128)(2,1)S(1)} %bitcast.102), channel_id=1, source_target_pairs={{8,16},{24,32},{40,48},{56,64},{72,80},{88,96},{104,112},{120,128}... | collective-permute-start | bytes 98312 | tf_op jit(solution)/shard_map/ppermute | solution.py:601
  12.3 1.1 copy.18
  14.6 1.0 collective-permute-done.1.two
  15.6 1.3 collective-permute-start.2
  16.9 1.3 collective-permute-start.3
  18.3 1.4 shard_map.120
  19.7 2.0 %collective-permute-done.3.below = bf16[160,128]{1,0:T(8,128)(2,1)S(1)} collective-permute-done((bf16[160,128]{1,0:T(8,128)(2,1)S(1)}, bf16[160,128]{1,0:T(8,128)(2,1)S(1)}, u32[]{:S(2)}, u32[]{:S(2)}) %collective-permute-start.3) | collective-permute-done | bytes 40992 | tf_op jit(solution)/shard_map/ppermute | solution.py:593
  21.7 1.2 shard_map.121
  22.9 1.9 %collective-permute-start.4 = (bf16[336,128]{1,0:T(8,128)(2,1)S(1)}, bf16[336,128]{1,0:T(8,128)(2,1)S(1)}, u32[]{:S(2)}, u32[]{:S(2)}) collective-permute-start(bf16[336,128]{1,0:T(8,128)(2,1)S(1)} %get-tuple-element.46), channel_id=1, source_target_pairs={{0,8},{8,0},{16,24},{24,16},{32,40},{40,32},{48,56},{56,48},{64,72... | collective-permute-start | bytes 258056 | tf_op jit(solution)/shard_map/ppermute | solution.py:601
  24.8 3.9 %collective-permute-start.5 = (bf16[336,128]{1,0:T(8,128)(2,1)S(1)}, bf16[336,128]{1,0:T(8,128)(2,1)S(1)}, u32[]{:S(2)}, u32[]{:S(2)}) collective-permute-start(bf16[336,128]{1,0:T(8,128)(2,1)S(1)} %get-tuple-element.47), channel_id=1, source_target_pairs={{8,16},{24,32},{40,48},{56,64},{72,80},{88,96},{104,112},{120,128}... | collective-permute-start | bytes 258056 | tf_op jit(solution)/shard_map/ppermute | solution.py:601
  28.8 2.1 %collective-permute-done.5.two.skip_two.two1 = bf16[336,128]{1,0:T(8,128)(2,1)S(1)} collective-permute-done((bf16[336,128]{1,0:T(8,128)(2,1)S(1)}, bf16[336,128]{1,0:T(8,128)(2,1)S(1)}, u32[]{:S(2)}, u32[]{:S(2)}) %collective-permute-start.5) | collective-permute-done | bytes 86048 | tf_op jit(solution)/shard_map/ppermute | solution.py:601
  31.1 1.3 collective-permute-start.7
  32.4 4.0 %collective-permute-start.6 = (bf16[720,128]{1,0:T(8,128)(2,1)S(1)}, bf16[720,128]{1,0:T(8,128)(2,1)S(1)}, u32[]{:S(2)}, u32[]{:S(2)}) collective-permute-start(bf16[720,128]{1,0:T(8,128)(2,1)S(1)} %get-tuple-element.77), channel_id=1, source_target_pairs={{0,1},{1,2},{2,3},{3,4},{4,5},{5,6},{6,7},{8,9},{9,10},{10,11},{11... | collective-permute-start | bytes 552968 | tf_op jit(solution)/shard_map/ppermute | solution.py:593
  36.4 1.0 collective-permute-done.7.below.skip_below.below1
  37.4 1.5 collective-permute-done.6.above.skip_above.above1
  38.8 2.4 %shard_map.122 = (f32[8,256,128]{2,1,0:T(8,128)S(1)}, bf16[4,128,128]{2,1,0:T(8,128)(2,1)S(1)}, f32[2,128,128]{2,1,0:T(8,128)S(1)}, f32[8,128]{1,0:T(8,128)S(1)}, bf16[3,160,1280]{2,1,0:T(8,128)(2,1)S(1)}) custom-call(bf16[4,64,128]{2,1,0:T(8,128)(2,1)S(1)} %get-tuple-element.45.own, bf16[336,128]{1,0:T(8,128)(2,1)S(1)} %collective-permute-done.4.one.skip_one.one1, ...), custom_call_target="tpu_custom_call" | custom-call | flops 536870912 | bytes 1048576 | tf_op jit(solution)/shard_map/pallas_call | solution.py:16
  41.2 1.3 collective-permute-start.9
  42.5 5.6 %collective-permute-start.8 = (f32[8,128]{1,0:T(8,128)S(1)}, f32[8,128]{1,0:T(8,128)S(1)}, u32[]{:S(2)}, u32[]{:S(2)}) collective-permute-start(f32[8,128]{1,0:T(8,128)S(1)} %get-tuple-element.50), channel_id=1, source_target_pairs={{0,16},{16,32},{32,48},{48,64},{64,80},{80,96},{96,112},{112,128},... | collective-permute-start | bytes 12296 | tf_op jit(solution)/shard_map/ppermute | solution.py:593
  48.9 20.2 %all_to_all.35.acts = f32[16,3,8,128]{3,2,1,0:T(8,128)S(1)} all-to-all(f32[16,3,8,128]{3,2,1,0:T(8,128)S(1)} %broadcast_in_dim.2), channel_id=1, replica_groups=mesh['x'=4,'z'=8,'c'=2,'gy'=8] {'c','gy'}, dimensions={0} | all-to-all | bytes 393216 | tf_op jit(solution)/shard_map/all_to_all | solution.py:683
  69.1 1.8 %shard_map.123 = (bf16[1,128,128]{2,1,0:T(8,128)(2,1)S(1)}, bf16[2,128,128]{2,1,0:T(8,128)(2,1)S(1)}, bf16[9,320,128]{2,1,0:T(8,128)(2,1)S(1)}, bf16[128,128]{1,0:T(8,128)(2,1)S(1)}) custom-call(f32[16,3,8,128]{3,2,1,0:T(8,128)S(1)} %all_to_all.35.acts, bf16[16,128]{1,0:T(8,128)(2,1)S(1)} %bitcast.82, ...), custom_call_target="tpu_custom_call" | custom-call | flops 268435456 | bytes 1048576 | tf_op jit(solution)/shard_map/pallas_call | solution.py:16
  70.9 2.9 %collective-permute-start.10 = (bf16[1,128,128]{2,1,0:T(8,128)(2,1)S(1)}, bf16[1,128,128]{2,1,0:T(8,128)(2,1)S(1)}, u32[]{:S(2)}, u32[]{:S(2)}) collective-permute-start(bf16[1,128,128]{2,1,0:T(8,128)(2,1)S(1)} %get-tuple-element.54.own), channel_id=1, source_target_pairs={{0,8},{8,0},{16,24},{24,16},{32,40},{40,32},{48,56},{56,48},{64,72... | collective-permute-start | bytes 98312 | tf_op jit(solution)/shard_map/ppermute | solution.py:601
  73.9 3.9 %collective-permute-start.11 = (bf16[1,128,128]{2,1,0:T(8,128)(2,1)S(1)}, bf16[1,128,128]{2,1,0:T(8,128)(2,1)S(1)}, u32[]{:S(2)}, u32[]{:S(2)}) collective-permute-start(bf16[1,128,128]{2,1,0:T(8,128)(2,1)S(1)} %get-tuple-element.54.own), channel_id=1, source_target_pairs={{8,16},{24,32},{40,48},{56,64},{72,80},{88,96},{104,112},{120,128}... | collective-permute-start | bytes 98312 | tf_op jit(solution)/shard_map/ppermute | solution.py:601
  77.8 1.5 collective-permute-done.11.two
  79.3 1.3 collective-permute-start.13
  80.6 4.6 %collective-permute-start.12 = (bf16[3,128,128]{2,1,0:T(8,128)(2,1)S(1)}, bf16[3,128,128]{2,1,0:T(8,128)(2,1)S(1)}, u32[]{:S(2)}, u32[]{:S(2)}) collective-permute-start(bf16[3,128,128]{2,1,0:T(8,128)(2,1)S(1)} %constant_dynamic-update-slice_fusion.18), channel_id=1, source_target_pairs={{0,1},{1,2},{2,3},{3,4},{4,5},{5,6},{6,7},{8,9},{9,10},{10,11},{11... | collective-permute-start | bytes 294920 | tf_op jit(solution)/shard_map/ppermute | solution.py:593
  86.9 3.6 %shard_map.126 = bf16[512,640]{1,0:T(8,128)(2,1)S(1)} custom-call(bf16[1,128,128]{2,1,0:T(8,128)(2,1)S(1)} %get-tuple-element.54.own, bf16[1,128,128]{2,1,0:T(8,128)(2,1)S(1)} %collective-permute-done.10.one, bf16[1,128,128]{2,1,0:T(8,128)(2,1)S(1)} %collective-permute-done.11.two, bf16[3,128,128]{2,1,0:T(8,128)(2,1)S(1)} %collective-permute-done.12.above, ...), custom_call_target="tpu_custom_call" | custom-call | flops 1073741824 | bytes 1048576 | tf_op jit(solution)/shard_map/pallas_call | solution.py:16
  90.5 29.4 %all_to_all.36 = bf16[8,64,640]{2,1,0:T(8,128)(2,1)S(1)} all-to-all(bf16[8,64,640]{2,1,0:T(8,128)(2,1)S(1)} %bitcast.70), channel_id=1, replica_groups=mesh['x'=4,'z'=8,'c'=2,'gy'=8] {'x','c'}, dimensions={0} | all-to-all | bytes 1310720 | tf_op jit(solution)/shard_map/all_to_all | solution.py:623
  120.2 20.1 %all_to_all.37 = f32[64,1,640]{2,1,0:T(1,128)S(1)} all-to-all(f32[64,1,640]{2,1,0:T(1,128)S(1)} %all_to_all.24), channel_id=1, replica_groups=mesh['x'=4,'z'=8,'c'=2,'gy'=8] {'z','gy'}, dimensions={0} | all-to-all | bytes 327680 | tf_op jit(solution)/shard_map/all_to_all | solution.py:625
  140.6 15.6 %all_to_all.38 = f32[64,1,640]{2,1,0:T(1,128)S(1)} all-to-all(f32[64,1,640]{2,1,0:T(1,128)S(1)} %all_to_all.26), channel_id=1, replica_groups=mesh['x'=4,'z'=8,'c'=2,'gy'=8] {'z','gy'}, dimensions={0} | all-to-all | bytes 327680 | tf_op jit(solution)/shard_map/all_to_all | solution.py:628
  156.2 17.0 %all_to_all.39 = bf16[8,64,640]{2,1,0:T(8,128)(2,1)S(1)} all-to-all(bf16[8,64,640]{2,1,0:T(8,128)(2,1)S(1)} %shard_map.127), channel_id=1, replica_groups=mesh['x'=4,'z'=8,'c'=2,'gy'=8] {'x','c'}, dimensions={0} | all-to-all | bytes 1310720 | tf_op jit(solution)/shard_map/all_to_all | solution.py:629
  173.2 1.4 shard_map.128
  (67 shorter events, 5.2 us)
Async XLA Ops:
  0.6 13.8 %copy-start.6 = (bf16[16,8,8,128]{3,2,1,0:T(8,128)(2,1)S(1)}, bf16[16,8,8,128]{3,2,1,0:T(8,128)(2,1)}, u32[]{:S(2)}) copy-start(bf16[16,8,8,128]{3,2,1,0:T(8,128)(2,1)} %param.14) | copy-start | bytes 786436
  0.6 17.6 %copy-start = (bf16[3,3,3,64,128]{4,3,2,1,0:T(8,128)(2,1)S(1)}, bf16[3,3,3,64,128]{4,3,2,1,0:T(8,128)(2,1)}, u32[]{:S(2)}) copy-start(bf16[3,3,3,64,128]{4,3,2,1,0:T(8,128)(2,1)} %param.13) | copy-start | bytes 1327108
  0.7 17.6 %copy-start.1 = (bf16[3,3,3,32,64]{4,3,2,1,0:T(8,128)(2,1)S(1)}, bf16[3,3,3,32,64]{4,3,2,1,0:T(8,128)(2,1)}, u32[]{:S(2)}) copy-start(bf16[3,3,3,32,64]{4,3,2,1,0:T(8,128)(2,1)} %param.12) | copy-start | bytes 331780
  0.7 17.6 %copy-start.3 = (bf16[3,3,3,16,32]{4,3,2,1,0:T(8,128)(2,1)S(1)}, bf16[3,3,3,16,32]{4,3,2,1,0:T(8,128)(2,1)}, u32[]{:S(2)}) copy-start(bf16[3,3,3,16,32]{4,3,2,1,0:T(8,128)(2,1)} %param.11) | copy-start | bytes 82948
  0.7 17.6 %copy-start.2 = (bf16[3,3,3,16,16]{4,3,2,1,0:T(8,128)(2,1)S(1)}, bf16[3,3,3,16,16]{4,3,2,1,0:T(8,128)(2,1)}, u32[]{:S(2)}) copy-start(bf16[3,3,3,16,16]{4,3,2,1,0:T(8,128)(2,1)} %param.10) | copy-start | bytes 41476
  1.6 13.1 %collective-permute-start = (bf16[1,128,128]{2,1,0:T(8,128)(2,1)S(1)}, bf16[1,128,128]{2,1,0:T(8,128)(2,1)S(1)}, u32[]{:S(2)}, u32[]{:S(2)}) collective-permute-start(bf16[1,128,128]{2,1,0:T(8,128)(2,1)S(1)} %bitcast.101), channel_id=1, source_target_pairs={{0,8},{8,0},{16,24},{24,16},{32,40},{40,32},{48,56},{56,48},{64,72... | collective-permute-start | bytes 98312 | tf_op jit(solution)/shard_map/ppermute | solution.py:601
  10.4 5.2 %collective-permute-start.1 = (bf16[1,128,128]{2,1,0:T(8,128)(2,1)S(1)}, bf16[1,128,128]{2,1,0:T(8,128)(2,1)S(1)}, u32[]{:S(2)}, u32[]{:S(2)}) collective-permute-start(bf16[1,128,128]{2,1,0:T(8,128)(2,1)S(1)} %bitcast.102), channel_id=1, source_target_pairs={{8,16},{24,32},{40,48},{56,64},{72,80},{88,96},{104,112},{120,128}... | collective-permute-start | bytes 98312 | tf_op jit(solution)/shard_map/ppermute | solution.py:601
  13.4 8.2 %copy-start.5 = (bf16[128,1,1,16]{0,3,2,1:T(8,128)(2,1)S(1)}, bf16[128,1,1,16]{0,3,2,1:T(8,128)(2,1)}, u32[]{:S(2)}) copy-start(bf16[128,1,1,16]{0,3,2,1:T(8,128)(2,1)} %param.17) | copy-start | bytes 12292
  15.6 4.1 %collective-permute-start.2 = (bf16[160,128]{1,0:T(8,128)(2,1)S(1)}, bf16[160,128]{1,0:T(8,128)(2,1)S(1)}, u32[]{:S(2)}, u32[]{:S(2)}) collective-permute-start(bf16[160,128]{1,0:T(8,128)(2,1)S(1)} %pad_maximum_fusion), channel_id=1, source_target_pairs={{0,1},{1,2},{2,3},{3,4},{4,5},{5,6},{6,7},{8,9},{9,10},{10,11},{11... | collective-permute-start | bytes 122888 | tf_op jit(solution)/shard_map/ppermute | solution.py:593
  16.9 4.7 %collective-permute-start.3 = (bf16[160,128]{1,0:T(8,128)(2,1)S(1)}, bf16[160,128]{1,0:T(8,128)(2,1)S(1)}, u32[]{:S(2)}, u32[]{:S(2)}) collective-permute-start(bf16[160,128]{1,0:T(8,128)(2,1)S(1)} %pad_maximum_fusion.1), channel_id=1, source_target_pairs={{1,0},{2,1},{3,2},{4,3},{5,4},{6,5},{7,6},{9,8},{10,9},{11,10},{12... | collective-permute-start | bytes 122888 | tf_op jit(solution)/shard_map/ppermute | solution.py:593
  22.9 5.8 %collective-permute-start.4 = (bf16[336,128]{1,0:T(8,128)(2,1)S(1)}, bf16[336,128]{1,0:T(8,128)(2,1)S(1)}, u32[]{:S(2)}, u32[]{:S(2)}) collective-permute-start(bf16[336,128]{1,0:T(8,128)(2,1)S(1)} %get-tuple-element.46), channel_id=1, source_target_pairs={{0,8},{8,0},{16,24},{24,16},{32,40},{40,32},{48,56},{56,48},{64,72... | collective-permute-start | bytes 258056 | tf_op jit(solution)/shard_map/ppermute | solution.py:601
  24.8 6.0 %collective-permute-start.5 = (bf16[336,128]{1,0:T(8,128)(2,1)S(1)}, bf16[336,128]{1,0:T(8,128)(2,1)S(1)}, u32[]{:S(2)}, u32[]{:S(2)}) collective-permute-start(bf16[336,128]{1,0:T(8,128)(2,1)S(1)} %get-tuple-element.47), channel_id=1, source_target_pairs={{8,16},{24,32},{40,48},{56,64},{72,80},{88,96},{104,112},{120,128}... | collective-permute-start | bytes 258056 | tf_op jit(solution)/shard_map/ppermute | solution.py:601
  31.1 6.3 %collective-permute-start.7 = (bf16[720,128]{1,0:T(8,128)(2,1)S(1)}, bf16[720,128]{1,0:T(8,128)(2,1)S(1)}, u32[]{:S(2)}, u32[]{:S(2)}) collective-permute-start(bf16[720,128]{1,0:T(8,128)(2,1)S(1)} %get-tuple-element.76), channel_id=1, source_target_pairs={{1,0},{2,1},{3,2},{4,3},{5,4},{6,5},{7,6},{9,8},{10,9},{11,10},{12... | collective-permute-start | bytes 552968 | tf_op jit(solution)/shard_map/ppermute | solution.py:593
  32.4 6.5 %collective-permute-start.6 = (bf16[720,128]{1,0:T(8,128)(2,1)S(1)}, bf16[720,128]{1,0:T(8,128)(2,1)S(1)}, u32[]{:S(2)}, u32[]{:S(2)}) collective-permute-start(bf16[720,128]{1,0:T(8,128)(2,1)S(1)} %get-tuple-element.77), channel_id=1, source_target_pairs={{0,1},{1,2},{2,3},{3,4},{4,5},{5,6},{6,7},{8,9},{9,10},{10,11},{11... | collective-permute-start | bytes 552968 | tf_op jit(solution)/shard_map/ppermute | solution.py:593
  38.8 30.3 %copy-start.4 = (bf16[64,2,2,32]{0,3,2,1:T(8,128)(2,1)S(1)}, bf16[64,2,2,32]{0,3,2,1:T(8,128)(2,1)}, u32[]{:S(2)}) copy-start(bf16[64,2,2,32]{0,3,2,1:T(8,128)(2,1)} %param.16) | copy-start | bytes 49156
  41.2 6.9 %collective-permute-start.9 = (f32[8,128]{1,0:T(8,128)S(1)}, f32[8,128]{1,0:T(8,128)S(1)}, u32[]{:S(2)}, u32[]{:S(2)}) collective-permute-start(f32[8,128]{1,0:T(8,128)S(1)} %get-tuple-element.50), channel_id=1, source_target_pairs={{16,0},{32,16},{48,32},{64,48},{80,64},{96,80},{112,96},{128,112},... | collective-permute-start | bytes 12296 | tf_op jit(solution)/shard_map/ppermute | solution.py:593
  42.5 6.4 %collective-permute-start.8 = (f32[8,128]{1,0:T(8,128)S(1)}, f32[8,128]{1,0:T(8,128)S(1)}, u32[]{:S(2)}, u32[]{:S(2)}) collective-permute-start(f32[8,128]{1,0:T(8,128)S(1)} %get-tuple-element.50), channel_id=1, source_target_pairs={{0,16},{16,32},{32,48},{48,64},{64,80},{80,96},{96,112},{112,128},... | collective-permute-start | bytes 12296 | tf_op jit(solution)/shard_map/ppermute | solution.py:593
  70.9 6.8 %collective-permute-start.10 = (bf16[1,128,128]{2,1,0:T(8,128)(2,1)S(1)}, bf16[1,128,128]{2,1,0:T(8,128)(2,1)S(1)}, u32[]{:S(2)}, u32[]{:S(2)}) collective-permute-start(bf16[1,128,128]{2,1,0:T(8,128)(2,1)S(1)} %get-tuple-element.54.own), channel_id=1, source_target_pairs={{0,8},{8,0},{16,24},{24,16},{32,40},{40,32},{48,56},{56,48},{64,72... | collective-permute-start | bytes 98312 | tf_op jit(solution)/shard_map/ppermute | solution.py:601
  73.9 5.5 %collective-permute-start.11 = (bf16[1,128,128]{2,1,0:T(8,128)(2,1)S(1)}, bf16[1,128,128]{2,1,0:T(8,128)(2,1)S(1)}, u32[]{:S(2)}, u32[]{:S(2)}) collective-permute-start(bf16[1,128,128]{2,1,0:T(8,128)(2,1)S(1)} %get-tuple-element.54.own), channel_id=1, source_target_pairs={{8,16},{24,32},{40,48},{56,64},{72,80},{88,96},{104,112},{120,128}... | collective-permute-start | bytes 98312 | tf_op jit(solution)/shard_map/ppermute | solution.py:601
  79.3 6.7 %collective-permute-start.13 = (bf16[3,128,128]{2,1,0:T(8,128)(2,1)S(1)}, bf16[3,128,128]{2,1,0:T(8,128)(2,1)S(1)}, u32[]{:S(2)}, u32[]{:S(2)}) collective-permute-start(bf16[3,128,128]{2,1,0:T(8,128)(2,1)S(1)} %constant_dynamic-update-slice_fusion.18), channel_id=1, source_target_pairs={{1,0},{2,1},{3,2},{4,3},{5,4},{6,5},{7,6},{9,8},{10,9},{11,10},{12... | collective-permute-start | bytes 294920 | tf_op jit(solution)/shard_map/ppermute | solution.py:593
  80.6 6.2 %collective-permute-start.12 = (bf16[3,128,128]{2,1,0:T(8,128)(2,1)S(1)}, bf16[3,128,128]{2,1,0:T(8,128)(2,1)S(1)}, u32[]{:S(2)}, u32[]{:S(2)}) collective-permute-start(bf16[3,128,128]{2,1,0:T(8,128)(2,1)S(1)} %constant_dynamic-update-slice_fusion.18), channel_id=1, source_target_pairs={{0,1},{1,2},{2,3},{3,4},{4,5},{5,6},{6,7},{8,9},{9,10},{10,11},{11... | collective-permute-start | bytes 294920 | tf_op jit(solution)/shard_map/ppermute | solution.py:593

commit v4 on v3

--- a/solution.py
+++ b/solution.py
@@ -34,6 +34,17 @@
         lax.axis_index("c"),
         row_at,
     )
+
+
+def row_edges(first, second, start, size):
+    rule = lax.axis_index("gy") % 2 == 0
+    one, two = (part[start : start + size].astype(F32) for part in (first, second))
+    return jnp.where(rule, two, one).astype(BF16), jnp.where(rule, one, two).astype(BF16)
+
+
+def half_lanes(tile, odd):
+    tile = pltpu.roll(tile.astype(F32), 64, 1) if odd else tile.astype(F32)
+    return jnp.where(lanes(tile.shape) < 64, tile, 0.0).astype(BF16)
 
 
 def lanes(shape):
@@ -176,16 +187,15 @@
         even = lax.axis_index("c") == 0
         for layer in range(10):
             if 0 < layer < 9:
-                parts = [part[layer * 16 : layer * 16 + 16] for part in (above, below)]
-                parts.insert(1, own[layer - 1])
+                high, low = row_edges(above, below, layer * 16, 16)
+                middle = own[layer - 1]
             else:
                 near, far = (two, one) if layer == 0 else (one, two)
                 at = (144, 0) if layer == 0 else (0, 144)
-                parts = [
-                    jnp.where(even, part[at[0] : at[0] + 16], part[at[1] : at[1] + 16])
-                    for part in (above, below)
-                ]
-                parts.insert(1, jnp.where(even, near[0], far[0]))
+                yes, no = (row_edges(above, below, start, 16) for start in at)
+                high, low = (jnp.where(even, yes[part], no[part]) for part in range(2))
+                middle = jnp.where(even, near[0], far[0])
+            parts = (high, middle, low)
             put_shifts(shifts, 0, layer, parts[0])
             put_shifts(shifts, 16, layer, parts[1])
             put_shifts(shifts, 144, layer, parts[2])
@@ -220,21 +230,21 @@
     ):
         flags = place_of()
         even = flags[4] == 0
+        def edge_at(place):
+            found = row_edges(above, below, place // 2 * 48, 48)
+            return [half_lanes(part, place % 2) for part in found]
+
         for layer in range(10):
             if 3 <= layer < 7:
-                at = layer * 48
                 middle = own[layer - 3]
-                edges = [part[at : at + 48] for part in (above, below)]
+                edges = edge_at(layer)
             else:
                 near, far = (two, one) if layer < 3 else (one, two)
                 at = layer % 7 * 64
                 middle = jnp.where(even, near[at : at + 64], far[at : at + 64])
-                at = layer % 7 * 48
-                at = (336 + at, at) if layer < 3 else (at, 336 + at)
-                edges = [
-                    jnp.where(even, part[at[0] : at[0] + 48], part[at[1] : at[1] + 48])
-                    for part in (above, below)
-                ]
+                at = layer % 7
+                yes, no = (edge_at(place) for place in ((7 + at, at) if layer < 3 else (at, 7 + at)))
+                edges = [jnp.where(even, yes[part], no[part]) for part in range(2)]
             put_shifts(shifts, 0, layer, edges[0])
             put_shifts(shifts, 48, layer, middle)
             put_shifts(shifts, 112, layer, edges[1])
@@ -313,17 +323,24 @@
     return jnp.concatenate(parts, axis=0)
 
 
-def deepest(columns, acts, skip_deep, halo_z, halo_y, skip, pre, weights, weights_back):
+def deepest(columns, acts, chips, skip_deep, halo_z, halo_y, skip, pre, weights, weights_back):
     def body(
-        acts, skip_own, skip_one, skip_two, skip_above, skip_below, skip, pre,
+        acts, chip_one, chip_two, skip_own, skip_one, skip_two, skip_above, skip_below, skip, pre,
         taps, taps_back, dense_out, out, shifts, delta_own, deltas,
     ):
         flags = place_of()
         core, row_at = flags[4], flags[5]
         place = lanes((64, 128)) // 16
 
+        ahead = lax.axis_index("z") % 2 == 0
+
         def cells(position, row):
-            return acts[position % 2 * columns + row, position // 2]
+            at = position % 2 * columns + row
+            if position // 2 == 1:
+                return acts[at]
+            if position // 2 == 0:
+                return jnp.where(ahead, chip_two[at], chip_one[at])
+            return jnp.where(ahead, chip_one[at], chip_two[at])
 
         for near in range(5):
             row = row_at + near - 2
@@ -349,11 +366,9 @@
             upstream = jnp.zeros((128, 128), F32)
             for layer in range(3):
                 if near != 1:
-                    edge = (skip_above, skip_below)[near // 2]
-                    at = 704 - layer * 16
-                    dense = jnp.where(
-                        core == 0, edge[at : at + 16], edge[1392 - at - 16 : 1392 - at]
-                    )
+                    yes = row_edges(skip_above, skip_below, 368 - layer * 16, 16)[near // 2]
+                    no = row_edges(skip_above, skip_below, 336 + layer * 16, 16)[near // 2]
+                    dense = jnp.where(core == 0, yes, no)
                 elif layer == 1:
                     dense = skip_own[...]
                 else:
@@ -396,7 +411,7 @@
     scratch = [((384, 128), F32)]
     return call(
         body, outs, scratch, 1 << 28,
-        acts, skip_deep, *halo_z, *halo_y, skip, pre, weights, weights_back,
+        acts, *chips, skip_deep, *halo_z, *halo_y, skip, pre, weights, weights_back,
     )
 
 
@@ -470,20 +485,24 @@
         even = flags[4] == 0
         for layer in range(6):
             block = layer // 2
-            if block == 1:
-                tiles = (above[1], own[0], below[1])
-            else:
+            high, low = row_edges(above, below, block * 128, 128)
+            middle = own[0]
+            if block != 1:
                 near, far = (two, one) if block == 0 else (one, two)
-                tiles = (
-                    jnp.where(even, above[2 - block], above[block]),
-                    jnp.where(even, near[0], far[0]),
-                    jnp.where(even, below[2 - block], below[block]),
-                )
+                middle = jnp.where(even, near[0], far[0])
+                other = row_edges(above, below, (2 - block) * 128, 128)
+                high, low = jnp.where(even, other[0], high), jnp.where(even, other[1], low)
+            tiles = (high, middle, low)
             for part, tile in enumerate(tiles):
                 tile = turned(tile.astype(F32), -32 * (layer % 2))
                 tile = jnp.where(lanes(tile.shape) < 32, tile, 0.0).astype(BF16)
                 put_shifts(moved2, part * 128, layer, tile)
         value = convolved(taps2, moved2, (0, 384), 4)
+
+        def edge_at(place):
+            found = row_edges(above1, below1, 240 + place // 2 * 32, 32)
+            return [half_lanes(part, place % 2) for part in found]
+
         picks = pair_columns(False)
         row = lax.broadcasted_iota(jnp.int32, (192, 128), 0) // 32
         inside = lanes((192, 128)) < 64
@@ -495,16 +514,14 @@
                 parts = [carried[part * 32 : part * 32 + 32] for part in (0, 1, 1, 2, 2, 3)]
                 carried = jnp.concatenate(parts, axis=0)
             if 0 < layer < 5:
-                at = 480 + layer * 32
-                parts = [above1[at : at + 32], skip1[layer - 1], below1[at : at + 32]]
+                high, low = edge_at(layer)
+                middle = skip1[layer - 1]
             else:
                 near, far = (two1, one1) if layer == 0 else (one1, two1)
-                at = (640, 480) if layer == 0 else (480, 640)
-                parts = [
-                    jnp.where(even, above1[at[0] : at[0] + 32], above1[at[1] : at[1] + 32]),
-                    jnp.where(even, near[192:320], far[192:320]),
-                    jnp.where(even, below1[at[0] : at[0] + 32], below1[at[1] : at[1] + 32]),
-                ]
+                yes, no = edge_at(5 - layer), edge_at(layer)
+                high, low = (jnp.where(even, yes[part], no[part]) for part in range(2))
+                middle = jnp.where(even, near[192:320], far[192:320])
+            parts = (high, middle, low)
             skip = jnp.concatenate(parts, axis=0).astype(F32)
             change = (skip + carried) * slope(pre1[layer + 1, 32:224])
             keep = inside
@@ -586,19 +603,67 @@
     return call(body, outs, scratch, 1 << 20, sums)
 
 
-def exchange(first, last, axis):
+def pairs(axis):
     size = lax.axis_size(axis)
-    up = [(i, i + 1) for i in range(size - 1)]
-    down = [(i + 1, i) for i in range(size - 1)]
-    return lax.ppermute(last, axis, up), lax.ppermute(first, axis, down)
-
-
-def swaps(to_one, to_two):
-    size = lax.axis_size(GZ)
-    on_chip = [(i, i ^ 1) for i in range(size)]
     between = [(i, i + 1) for i in range(1, size - 1, 2)]
-    between += [(j, i) for i, j in between]
-    return lax.ppermute(to_one, GZ, on_chip), lax.ppermute(to_two, GZ, between)
+    return [(i, i ^ 1) for i in range(size)], between + [(j, i) for i, j in between]
+
+
+def swaps(to_one, to_two, axis=GZ):
+    first, second = pairs(axis)
+    return lax.ppermute(to_one, axis, first), lax.ppermute(to_two, axis, second)
+
+
+def edge_rows(one, two, volume):
+    def body(one, two, own, to_one, to_two):
+        even = lax.axis_index("gy") % 2 == 0
+        for place in range(10):
+            block = one[0] if place == 0 else two[0] if place == 9 else own[place - 1]
+            at = place * 16
+            to_one[at : at + 16] = jnp.where(even, block[112:], block[:16])
+            to_two[at : at + 16] = jnp.where(even, block[:16], block[112:])
+
+    return call(body, [((160, 128), BF16)] * 2, [], 1 << 20, one, two, volume)
+
+
+def edge_rows_half(one, two, act, skip_half, skip_deep):
+    def body(one, two, act, skip1, skip3, to_one, to_two):
+        even = lax.axis_index("gy") % 2 == 0
+
+        def put(at, size, blocks):
+            low, high = blocks
+            packed_rows = []
+            for rows in (slice(0, size), slice(low.shape[0] - size, low.shape[0])):
+                packed_rows.append(
+                    low[rows].astype(F32) + pltpu.roll(high[rows].astype(F32), 64, 1)
+                )
+            top, bottom = packed_rows
+            to_one[at : at + size] = jnp.where(even, bottom, top).astype(BF16)
+            to_two[at : at + size] = jnp.where(even, top, bottom).astype(BF16)
+
+        def act_at(place):
+            if 3 <= place < 7:
+                return act[place - 3]
+            at = place % 7 * 64
+            return (one if place < 3 else two)[at : at + 64]
+
+        def skip_at(place):
+            if 0 < place < 5:
+                return skip1[place - 1]
+            return (one if place == 0 else two)[192:320]
+
+        for pair in range(5):
+            put(pair * 48, 48, (act_at(2 * pair), act_at(2 * pair + 1)))
+        for pair in range(3):
+            put(240 + pair * 32, 32, (skip_at(2 * pair), skip_at(2 * pair + 1)))
+        for place, rows in enumerate((one[320:], skip3[...], two[320:])):
+            at = 336 + place * 16
+            to_one[at : at + 16] = rows
+            to_two[at : at + 16] = rows
+
+    return call(
+        body, [((384, 128), BF16)] * 2, [], 1 << 20, one, two, act, skip_half, skip_deep
+    )
 
 
 def laid_out(array):
@@ -651,13 +716,7 @@
         (one, two, laid_out(skip_full), laid_out(skip_half), kernels)
     )
 
-    def flat(parts):
-        return jnp.concatenate([part.reshape(-1, 128) for part in parts], axis=0)
-
-    def edge(start):
-        return flat([part[:, start : start + 16] for part in (one, volume, two)])
-
-    halo_y = exchange(edge(0), edge(112), "gy")
+    halo_y = swaps(*edge_rows(one, two, volume), "gy")
     dims = ((8, 16, 16), (4, 16, 32), (2, 32, 64), (1, 64, 128))
     w0, w1, w2, w3, t1, t2, t3 = prepare(kernels, dims)
     pre0, act1, shifts0, to_one, to_two = forward_full(
@@ -665,30 +724,20 @@
     )
     halo_z1 = one, two = swaps(to_one, to_two)
 
-    def edge1(start, start1):
-        acts = [part[:192].reshape(3, 64, 128) for part in (one, two)]
-        acts.insert(1, act1)
-        rims = [part[192:320].reshape(1, 128, 128) for part in (one, two)]
-        rims.insert(1, skip1)
-        parts = [part[:, start : start + 48] for part in acts]
-        parts += [part[:, start1 : start1 + 32] for part in rims]
-        return flat(parts + [one[320:], skip3, two[320:]])
-
-    halo_y1 = exchange(edge1(0, 0), edge1(16, 96), "gy")
+    halo_y1 = swaps(*edge_rows_half(one, two, act1, skip1, skip3), "gy")
     pre1, act2, pre2, act3, shifts1 = forward_half(act1, halo_z1, halo_y1, w1, w2)
     columns = lax.axis_size("gy")
-    before, after = exchange(act3, act3, ("x", "z"))
-    chips = jnp.stack([before, act3, after])
-    many = (2 * columns,) + chips.shape
+    many = (2 * columns,) + act3.shape
     acts = lax.all_to_all(
-        lax.optimization_barrier(jnp.broadcast_to(chips[None], many)), ("c", "gy"), 0, 0
-    )
+        lax.optimization_barrier(jnp.broadcast_to(act3[None], many)), ("c", "gy"), 0, 0
+    )
+    chips = swaps(acts, acts, ("x", "z"))
     dense2, delta2, shifts3, delta3 = deepest(
-        columns, acts, skip3, halo_z1, halo_y1, skip2, pre2, w3, t3
+        columns, acts, chips, skip3, halo_z1, halo_y1, skip2, pre2, w3, t3
     )
     halo_z = one, two = swaps(dense2, dense2)
-    block = jnp.concatenate([one, dense2, two], axis=0)
-    halo_y = exchange(block, block, "gy")
+    block = jnp.concatenate([one, dense2, two], axis=0).reshape(384, 128)
+    halo_y = swaps(block, block, "gy")
     grad3 = grad_deepest(shifts3, delta3)
     grad2 = grad_quarter_of(act2, delta2)
     terms = back_rest(

time: 175 us -> 166 us (0.949)
  blocking collectives: 102 us -> 91.2 us
  starting transfers between devices: 44 us -> 46.7 us
    all_to_all x1, blocking collectives: 29.4 us -> 23.3 us  [summed(): pieces = lax.all_to_all(terms.reshape(first, rows, width), inner, 0, 0)]
    all_to_all x1, blocking collectives: 20.2 us -> 15.3 us  [on_device(): lax.all_to_all(lax.optimization_barrier(jnp.broadcast_to(act3[None], many...]
    ppermute x14, starting transfers between devices: 44 us -> 46.7 us  [the longest x7 32.7 us: swaps(): lax.ppermute(to_one, axis, first)]
    pallas_call x9 -> x11, Pallas kernels: 12.6 us -> 12.8 us  [call(): pl.pallas_call(body, out_shape=tuple((jax.ShapeDtypeStruct(shape, dtype)...]
  transfers between devices with their start and end apart: 14 -> 14, of which waited for: 8 -> 7; matrix products, arithmetic and copies ran while one was open for 1% -> 1% of each run, Pallas kernels for 1% -> 1%
where the time goes in v4:
time: 166 us; the launch traced here: 165 us
  blocking collectives  91.2 us (55%)
  starting transfers between devices  46.7 us (28%)
  Pallas kernels  12.8 us (8%)
  waiting for transfers between devices  9.94 us (6%)
  local copies, waits for them, and re-layouts  2.59 us (2%)
    ppermute x7, starting transfers between devices, swaps(): lax.ppermute(to_one, axis, first)  32.7 us
    all_to_all x1, blocking collectives, summed(): pieces = lax.all_to_all(terms.reshape(first, rows, width), inner, 0, 0)  23.3 us
    all_to_all x1, blocking collectives, summed(): pieces = lax.all_to_all(part, outer, 0, 0, tiled=True)  20 us
    all_to_all x1, blocking collectives, summed(): return lax.all_to_all(copies(part, first), inner, 0, 0).reshape(terms.shape)  17 us
    all_to_all x1, blocking collectives, summed(): lax.all_to_all(lax.optimization_barrier(spread), outer, 0, 0, tiled=True)  15.6 us
    all_to_all x1, blocking collectives, on_device(): lax.all_to_all(lax.optimization_barrier(jnp.broadcast_to(act3[None], many...  15.3 us
    ppermute x7, starting transfers between devices, swaps(): lax.ppermute(to_two, axis, second)  14 us
    pallas_call x11, Pallas kernels, call(): pl.pallas_call(body, out_shape=tuple((jax.ShapeDtypeStruct(shape, dtype)...  12.8 us
  transfers between devices with their start and end apart: 14, of which 7 were waited for; matrix products, arithmetic and copies ran while one was open for 1% of the time, Pallas kernels for 1%

profile of v4, /device:TPU:1, one launch (start us, length us, event | category | flops | bytes accessed | tf_op | source)
XLA Modules:
  0.0 165.3 jit_solution(12614839681090928650)
XLA Ops:
  0.7 0.9 broadcast_select_fusion
  1.6 8.8 %collective-permute-start = (bf16[1,128,128]{2,1,0:T(8,128)(2,1)S(1)}, bf16[1,128,128]{2,1,0:T(8,128)(2,1)S(1)}, u32[]{:S(2)}, u32[]{:S(2)}) collective-permute-start(bf16[1,128,128]{2,1,0:T(8,128)(2,1)S(1)} %bitcast.47), channel_id=1, source_target_pairs={{0,8},{8,0},{16,24},{24,16},{32,40},{40,32},{48,56},{56,48},{64,72... | collective-permute-start | bytes 98312 | tf_op jit(solution)/shard_map/ppermute | solution.py:614
  10.4 1.9 %collective-permute-start.1 = (bf16[1,128,128]{2,1,0:T(8,128)(2,1)S(1)}, bf16[1,128,128]{2,1,0:T(8,128)(2,1)S(1)}, u32[]{:S(2)}, u32[]{:S(2)}) collective-permute-start(bf16[1,128,128]{2,1,0:T(8,128)(2,1)S(1)} %bitcast.48), channel_id=1, source_target_pairs={{8,16},{24,32},{40,48},{56,64},{72,80},{88,96},{104,112},{120,128}... | collective-permute-start | bytes 98312 | tf_op jit(solution)/shard_map/ppermute | solution.py:614
  12.3 1.1 copy.18
  13.4 0.9 copy.22
  14.6 1.0 collective-permute-done.1.two
  15.6 1.9 %collective-permute-start.2 = (bf16[160,128]{1,0:T(8,128)(2,1)S(1)}, bf16[160,128]{1,0:T(8,128)(2,1)S(1)}, u32[]{:S(2)}, u32[]{:S(2)}) collective-permute-start(bf16[160,128]{1,0:T(8,128)(2,1)S(1)} %get-tuple-element.43), channel_id=1, source_target_pairs={{0,1},{1,0},{2,3},{3,2},{4,5},{5,4},{6,7},{7,6},{8,9},{9,8},{10,11... | collective-permute-start | bytes 122888 | tf_op jit(solution)/shard_map/ppermute | solution.py:614
  18.3 1.4 shard_map.121
  19.7 0.7 collective-permute-done.2.above
  20.4 1.2 shard_map.122
  21.6 1.9 %collective-permute-start.4 = (bf16[336,128]{1,0:T(8,128)(2,1)S(1)}, bf16[336,128]{1,0:T(8,128)(2,1)S(1)}, u32[]{:S(2)}, u32[]{:S(2)}) collective-permute-start(bf16[336,128]{1,0:T(8,128)(2,1)S(1)} %get-tuple-element.52), channel_id=1, source_target_pairs={{0,8},{8,0},{16,24},{24,16},{32,40},{40,32},{48,56},{56,48},{64,72... | collective-permute-start | bytes 258056 | tf_op jit(solution)/shard_map/ppermute | solution.py:614
  23.5 3.8 %collective-permute-start.5 = (bf16[336,128]{1,0:T(8,128)(2,1)S(1)}, bf16[336,128]{1,0:T(8,128)(2,1)S(1)}, u32[]{:S(2)}, u32[]{:S(2)}) collective-permute-start(bf16[336,128]{1,0:T(8,128)(2,1)S(1)} %get-tuple-element.53), channel_id=1, source_target_pairs={{8,16},{24,32},{40,48},{56,64},{72,80},{88,96},{104,112},{120,128}... | collective-permute-start | bytes 258056 | tf_op jit(solution)/shard_map/ppermute | solution.py:614
  27.4 2.1 %collective-permute-done.5.two.skip_two.two1 = bf16[336,128]{1,0:T(8,128)(2,1)S(1)} collective-permute-done((bf16[336,128]{1,0:T(8,128)(2,1)S(1)}, bf16[336,128]{1,0:T(8,128)(2,1)S(1)}, u32[]{:S(2)}, u32[]{:S(2)}) %collective-permute-start.5) | collective-permute-done | bytes 86048 | tf_op jit(solution)/shard_map/ppermute | solution.py:614
  29.6 5.6 %collective-permute-start.6 = (bf16[384,128]{1,0:T(8,128)(2,1)S(1)}, bf16[384,128]{1,0:T(8,128)(2,1)S(1)}, u32[]{:S(2)}, u32[]{:S(2)}) collective-permute-start(bf16[384,128]{1,0:T(8,128)(2,1)S(1)} %get-tuple-element.54), channel_id=1, source_target_pairs={{0,1},{1,0},{2,3},{3,2},{4,5},{5,4},{6,7},{7,6},{8,9},{9,8},{10,11... | collective-permute-start | bytes 294920 | tf_op jit(solution)/shard_map/ppermute | solution.py:614
  35.2 0.7 collective-permute-start.7
  35.9 1.3 collective-permute-done.6.above.skip_above.above1
  37.2 2.5 %shard_map.124 = (f32[8,256,128]{2,1,0:T(8,128)S(1)}, bf16[4,128,128]{2,1,0:T(8,128)(2,1)S(1)}, f32[2,128,128]{2,1,0:T(8,128)S(1)}, f32[8,128]{1,0:T(8,128)S(1)}, bf16[3,160,1280]{2,1,0:T(8,128)(2,1)S(1)}) custom-call(bf16[4,64,128]{2,1,0:T(8,128)(2,1)S(1)} %get-tuple-element.51.act.own, bf16[336,128]{1,0:T(8,128)(2,1)S(1)} %collective-permute-done.4.one.skip_one.one1, ...), custom_call_target="tpu_custom_call" | custom-call | flops 536870912 | bytes 1048576 | tf_op jit(solution)/shard_map/pallas_call | solution.py:16
  39.7 15.3 %all_to_all.35.acts = f32[16,8,128]{2,1,0:T(8,128)S(1)} all-to-all(f32[16,8,128]{2,1,0:T(8,128)S(1)} %broadcast_in_dim.2), channel_id=1, replica_groups=mesh['x'=4,'z'=8,'c'=2,'gy'=8] {'c','gy'}, dimensions={0} | all-to-all | bytes 131072 | tf_op jit(solution)/shard_map/all_to_all | solution.py:731
  55.7 8.4 %collective-permute-start.8 = (f32[16,8,128]{2,1,0:T(8,128)S(1)}, f32[16,8,128]{2,1,0:T(8,128)S(1)}, u32[]{:S(2)}, u32[]{:S(2)}) collective-permute-start(f32[16,8,128]{2,1,0:T(8,128)S(1)} %all_to_all.35.acts), channel_id=1, source_target_pairs={{0,16},{16,0},{32,48},{48,32},{64,80},{80,64},{96,112},{112,96},{1... | collective-permute-start | bytes 196616 | tf_op jit(solution)/shard_map/ppermute | solution.py:614
  64.1 1.6 collective-permute-done.8.chip_one
  65.8 1.8 %shard_map.125 = (bf16[1,128,128]{2,1,0:T(8,128)(2,1)S(1)}, bf16[2,128,128]{2,1,0:T(8,128)(2,1)S(1)}, bf16[9,320,128]{2,1,0:T(8,128)(2,1)S(1)}, bf16[128,128]{1,0:T(8,128)(2,1)S(1)}) custom-call(f32[16,8,128]{2,1,0:T(8,128)S(1)} %all_to_all.35.acts, f32[16,8,128]{2,1,0:T(8,128)S(1)} %collective-permute-done.8.chip_one, ...), custom_call_target="tpu_custom_call" | custom-call | flops 268435456 | bytes 1048576 | tf_op jit(solution)/shard_map/pallas_call | solution.py:16
  67.6 5.6 %collective-permute-start.11 = (bf16[1,128,128]{2,1,0:T(8,128)(2,1)S(1)}, bf16[1,128,128]{2,1,0:T(8,128)(2,1)S(1)}, u32[]{:S(2)}, u32[]{:S(2)}) collective-permute-start(bf16[1,128,128]{2,1,0:T(8,128)(2,1)S(1)} %get-tuple-element.62.own), channel_id=1, source_target_pairs={{8,16},{24,32},{40,48},{56,64},{72,80},{88,96},{104,112},{120,128}... | collective-permute-start | bytes 98312 | tf_op jit(solution)/shard_map/ppermute | solution.py:614
  73.2 1.9 %collective-permute-start.10 = (bf16[1,128,128]{2,1,0:T(8,128)(2,1)S(1)}, bf16[1,128,128]{2,1,0:T(8,128)(2,1)S(1)}, u32[]{:S(2)}, u32[]{:S(2)}) collective-permute-start(bf16[1,128,128]{2,1,0:T(8,128)(2,1)S(1)} %get-tuple-element.62.own), channel_id=1, source_target_pairs={{0,8},{8,0},{16,24},{24,16},{32,40},{40,32},{48,56},{56,48},{64,72... | collective-permute-start | bytes 98312 | tf_op jit(solution)/shard_map/ppermute | solution.py:614
  75.1 1.2 collective-permute-done.10.one
  77.0 4.1 %collective-permute-start.12 = (bf16[384,128]{1,0:T(8,128)(2,1)S(1)}, bf16[384,128]{1,0:T(8,128)(2,1)S(1)}, u32[]{:S(2)}, u32[]{:S(2)}) collective-permute-start(bf16[384,128]{1,0:T(8,128)(2,1)S(1)} %bitcast.46), channel_id=1, source_target_pairs={{0,1},{1,0},{2,3},{3,2},{4,5},{5,4},{6,7},{7,6},{8,9},{9,8},{10,11... | collective-permute-start | bytes 294920 | tf_op jit(solution)/shard_map/ppermute | solution.py:614
  81.9 2.0 %collective-permute-done.12.above = bf16[384,128]{1,0:T(8,128)(2,1)S(1)} collective-permute-done((bf16[384,128]{1,0:T(8,128)(2,1)S(1)}, bf16[384,128]{1,0:T(8,128)(2,1)S(1)}, u32[]{:S(2)}, u32[]{:S(2)}) %collective-permute-start.12) | collective-permute-done | bytes 98336 | tf_op jit(solution)/shard_map/ppermute | solution.py:614
  83.9 3.6 %shard_map.128 = bf16[512,640]{1,0:T(8,128)(2,1)S(1)} custom-call(bf16[1,128,128]{2,1,0:T(8,128)(2,1)S(1)} %get-tuple-element.62.own, bf16[1,128,128]{2,1,0:T(8,128)(2,1)S(1)} %collective-permute-done.10.one, bf16[1,128,128]{2,1,0:T(8,128)(2,1)S(1)} %collective-permute-done.11.two, bf16[384,128]{1,0:T(8,128)(2,1)S(1)} %collective-permute-done.12.above, ...), custom_call_target="tpu_custom_call" | custom-call | flops 1073741824 | bytes 1048576 | tf_op jit(solution)/shard_map/pallas_call | solution.py:16
  87.5 23.3 %all_to_all.36 = bf16[8,64,640]{2,1,0:T(8,128)(2,1)S(1)} all-to-all(bf16[8,64,640]{2,1,0:T(8,128)(2,1)S(1)} %bitcast.27), channel_id=1, replica_groups=mesh['x'=4,'z'=8,'c'=2,'gy'=8] {'x','c'}, dimensions={0} | all-to-all | bytes 1310720 | tf_op jit(solution)/shard_map/all_to_all | solution.py:688
  111.1 20.0 %all_to_all.37 = f32[64,1,640]{2,1,0:T(1,128)S(1)} all-to-all(f32[64,1,640]{2,1,0:T(1,128)S(1)} %all_to_all.24), channel_id=1, replica_groups=mesh['x'=4,'z'=8,'c'=2,'gy'=8] {'z','gy'}, dimensions={0} | all-to-all | bytes 327680 | tf_op jit(solution)/shard_map/all_to_all | solution.py:690
  131.3 15.6 %all_to_all.38 = f32[64,1,640]{2,1,0:T(1,128)S(1)} all-to-all(f32[64,1,640]{2,1,0:T(1,128)S(1)} %all_to_all.26), channel_id=1, replica_groups=mesh['x'=4,'z'=8,'c'=2,'gy'=8] {'z','gy'}, dimensions={0} | all-to-all | bytes 327680 | tf_op jit(solution)/shard_map/all_to_all | solution.py:693
  147.0 17.0 %all_to_all.39 = bf16[8,64,640]{2,1,0:T(8,128)(2,1)S(1)} all-to-all(bf16[8,64,640]{2,1,0:T(8,128)(2,1)S(1)} %shard_map.129), channel_id=1, replica_groups=mesh['x'=4,'z'=8,'c'=2,'gy'=8] {'x','c'}, dimensions={0} | all-to-all | bytes 1310720 | tf_op jit(solution)/shard_map/all_to_all | solution.py:694
  164.0 1.4 shard_map.130
  (41 shorter events, 3.7 us)
Async XLA Ops:
  0.6 13.8 %copy-start.6 = (bf16[16,8,8,128]{3,2,1,0:T(8,128)(2,1)S(1)}, bf16[16,8,8,128]{3,2,1,0:T(8,128)(2,1)}, u32[]{:S(2)}) copy-start(bf16[16,8,8,128]{3,2,1,0:T(8,128)(2,1)} %param.14) | copy-start | bytes 786436
  0.6 17.6 %copy-start = (bf16[3,3,3,64,128]{4,3,2,1,0:T(8,128)(2,1)S(1)}, bf16[3,3,3,64,128]{4,3,2,1,0:T(8,128)(2,1)}, u32[]{:S(2)}) copy-start(bf16[3,3,3,64,128]{4,3,2,1,0:T(8,128)(2,1)} %param.13) | copy-start | bytes 1327108
  0.7 17.6 %copy-start.1 = (bf16[3,3,3,32,64]{4,3,2,1,0:T(8,128)(2,1)S(1)}, bf16[3,3,3,32,64]{4,3,2,1,0:T(8,128)(2,1)}, u32[]{:S(2)}) copy-start(bf16[3,3,3,32,64]{4,3,2,1,0:T(8,128)(2,1)} %param.12) | copy-start | bytes 331780
  0.7 17.6 %copy-start.3 = (bf16[3,3,3,16,32]{4,3,2,1,0:T(8,128)(2,1)S(1)}, bf16[3,3,3,16,32]{4,3,2,1,0:T(8,128)(2,1)}, u32[]{:S(2)}) copy-start(bf16[3,3,3,16,32]{4,3,2,1,0:T(8,128)(2,1)} %param.11) | copy-start | bytes 82948
  0.7 17.6 %copy-start.2 = (bf16[3,3,3,16,16]{4,3,2,1,0:T(8,128)(2,1)S(1)}, bf16[3,3,3,16,16]{4,3,2,1,0:T(8,128)(2,1)}, u32[]{:S(2)}) copy-start(bf16[3,3,3,16,16]{4,3,2,1,0:T(8,128)(2,1)} %param.10) | copy-start | bytes 41476
  1.6 13.1 %collective-permute-start = (bf16[1,128,128]{2,1,0:T(8,128)(2,1)S(1)}, bf16[1,128,128]{2,1,0:T(8,128)(2,1)S(1)}, u32[]{:S(2)}, u32[]{:S(2)}) collective-permute-start(bf16[1,128,128]{2,1,0:T(8,128)(2,1)S(1)} %bitcast.47), channel_id=1, source_target_pairs={{0,8},{8,0},{16,24},{24,16},{32,40},{40,32},{48,56},{56,48},{64,72... | collective-permute-start | bytes 98312 | tf_op jit(solution)/shard_map/ppermute | solution.py:614
  10.4 5.2 %collective-permute-start.1 = (bf16[1,128,128]{2,1,0:T(8,128)(2,1)S(1)}, bf16[1,128,128]{2,1,0:T(8,128)(2,1)S(1)}, u32[]{:S(2)}, u32[]{:S(2)}) collective-permute-start(bf16[1,128,128]{2,1,0:T(8,128)(2,1)S(1)} %bitcast.48), channel_id=1, source_target_pairs={{8,16},{24,32},{40,48},{56,64},{72,80},{88,96},{104,112},{120,128}... | collective-permute-start | bytes 98312 | tf_op jit(solution)/shard_map/ppermute | solution.py:614
  13.4 7.0 %copy-start.5 = (bf16[128,1,1,16]{0,3,2,1:T(8,128)(2,1)S(1)}, bf16[128,1,1,16]{0,3,2,1:T(8,128)(2,1)}, u32[]{:S(2)}) copy-start(bf16[128,1,1,16]{0,3,2,1:T(8,128)(2,1)} %param.17) | copy-start | bytes 12292
  15.6 4.7 %collective-permute-start.2 = (bf16[160,128]{1,0:T(8,128)(2,1)S(1)}, bf16[160,128]{1,0:T(8,128)(2,1)S(1)}, u32[]{:S(2)}, u32[]{:S(2)}) collective-permute-start(bf16[160,128]{1,0:T(8,128)(2,1)S(1)} %get-tuple-element.43), channel_id=1, source_target_pairs={{0,1},{1,0},{2,3},{3,2},{4,5},{5,4},{6,7},{7,6},{8,9},{9,8},{10,11... | collective-permute-start | bytes 122888 | tf_op jit(solution)/shard_map/ppermute | solution.py:614
  17.6 2.8 %collective-permute-start.3 = (bf16[160,128]{1,0:T(8,128)(2,1)S(1)}, bf16[160,128]{1,0:T(8,128)(2,1)S(1)}, u32[]{:S(2)}, u32[]{:S(2)}) collective-permute-start(bf16[160,128]{1,0:T(8,128)(2,1)S(1)} %get-tuple-element.44), channel_id=1, source_target_pairs={{1,2},{3,4},{5,6},{2,1},{4,3},{6,5},{9,10},{11,12},{13,14},{10,9},... | collective-permute-start | bytes 122888 | tf_op jit(solution)/shard_map/ppermute | solution.py:614
  21.6 5.8 %collective-permute-start.4 = (bf16[336,128]{1,0:T(8,128)(2,1)S(1)}, bf16[336,128]{1,0:T(8,128)(2,1)S(1)}, u32[]{:S(2)}, u32[]{:S(2)}) collective-permute-start(bf16[336,128]{1,0:T(8,128)(2,1)S(1)} %get-tuple-element.52), channel_id=1, source_target_pairs={{0,8},{8,0},{16,24},{24,16},{32,40},{40,32},{48,56},{56,48},{64,72... | collective-permute-start | bytes 258056 | tf_op jit(solution)/shard_map/ppermute | solution.py:614
  23.5 6.0 %collective-permute-start.5 = (bf16[336,128]{1,0:T(8,128)(2,1)S(1)}, bf16[336,128]{1,0:T(8,128)(2,1)S(1)}, u32[]{:S(2)}, u32[]{:S(2)}) collective-permute-start(bf16[336,128]{1,0:T(8,128)(2,1)S(1)} %get-tuple-element.53), channel_id=1, source_target_pairs={{8,16},{24,32},{40,48},{56,64},{72,80},{88,96},{104,112},{120,128}... | collective-permute-start | bytes 258056 | tf_op jit(solution)/shard_map/ppermute | solution.py:614
  29.5 36.3 %copy-start.4 = (bf16[64,2,2,32]{0,3,2,1:T(8,128)(2,1)S(1)}, bf16[64,2,2,32]{0,3,2,1:T(8,128)(2,1)}, u32[]{:S(2)}) copy-start(bf16[64,2,2,32]{0,3,2,1:T(8,128)(2,1)} %param.16) | copy-start | bytes 49156
  29.6 7.6 %collective-permute-start.6 = (bf16[384,128]{1,0:T(8,128)(2,1)S(1)}, bf16[384,128]{1,0:T(8,128)(2,1)S(1)}, u32[]{:S(2)}, u32[]{:S(2)}) collective-permute-start(bf16[384,128]{1,0:T(8,128)(2,1)S(1)} %get-tuple-element.54), channel_id=1, source_target_pairs={{0,1},{1,0},{2,3},{3,2},{4,5},{5,4},{6,7},{7,6},{8,9},{9,8},{10,11... | collective-permute-start | bytes 294920 | tf_op jit(solution)/shard_map/ppermute | solution.py:614
  35.2 2.0 %collective-permute-start.7 = (bf16[384,128]{1,0:T(8,128)(2,1)S(1)}, bf16[384,128]{1,0:T(8,128)(2,1)S(1)}, u32[]{:S(2)}, u32[]{:S(2)}) collective-permute-start(bf16[384,128]{1,0:T(8,128)(2,1)S(1)} %get-tuple-element.55), channel_id=1, source_target_pairs={{1,2},{3,4},{5,6},{2,1},{4,3},{6,5},{9,10},{11,12},{13,14},{10,9},... | collective-permute-start | bytes 294920 | tf_op jit(solution)/shard_map/ppermute | solution.py:614
  55.0 9.1 %collective-permute-start.9 = (f32[16,8,128]{2,1,0:T(8,128)S(1)}, f32[16,8,128]{2,1,0:T(8,128)S(1)}, u32[]{:S(2)}, u32[]{:S(2)}) collective-permute-start(f32[16,8,128]{2,1,0:T(8,128)S(1)} %all_to_all.35.acts), channel_id=1, source_target_pairs={{16,32},{48,64},{80,96},{112,128},{144,160},{176,192},{208,224},{2... | collective-permute-start | bytes 196616 | tf_op jit(solution)/shard_map/ppermute | solution.py:614
  55.7 10.1 %collective-permute-start.8 = (f32[16,8,128]{2,1,0:T(8,128)S(1)}, f32[16,8,128]{2,1,0:T(8,128)S(1)}, u32[]{:S(2)}, u32[]{:S(2)}) collective-permute-start(f32[16,8,128]{2,1,0:T(8,128)S(1)} %all_to_all.35.acts), channel_id=1, source_target_pairs={{0,16},{16,0},{32,48},{48,32},{64,80},{80,64},{96,112},{112,96},{1... | collective-permute-start | bytes 196616 | tf_op jit(solution)/shard_map/ppermute | solution.py:614
  67.6 7.5 %collective-permute-start.11 = (bf16[1,128,128]{2,1,0:T(8,128)(2,1)S(1)}, bf16[1,128,128]{2,1,0:T(8,128)(2,1)S(1)}, u32[]{:S(2)}, u32[]{:S(2)}) collective-permute-start(bf16[1,128,128]{2,1,0:T(8,128)(2,1)S(1)} %get-tuple-element.62.own), channel_id=1, source_target_pairs={{8,16},{24,32},{40,48},{56,64},{72,80},{88,96},{104,112},{120,128}... | collective-permute-start | bytes 98312 | tf_op jit(solution)/shard_map/ppermute | solution.py:614
  73.2 3.1 %collective-permute-start.10 = (bf16[1,128,128]{2,1,0:T(8,128)(2,1)S(1)}, bf16[1,128,128]{2,1,0:T(8,128)(2,1)S(1)}, u32[]{:S(2)}, u32[]{:S(2)}) collective-permute-start(bf16[1,128,128]{2,1,0:T(8,128)(2,1)S(1)} %get-tuple-element.62.own), channel_id=1, source_target_pairs={{0,8},{8,0},{16,24},{24,16},{32,40},{40,32},{48,56},{56,48},{64,72... | collective-permute-start | bytes 98312 | tf_op jit(solution)/shard_map/ppermute | solution.py:614
  76.3 5.6 %collective-permute-start.13 = (bf16[384,128]{1,0:T(8,128)(2,1)S(1)}, bf16[384,128]{1,0:T(8,128)(2,1)S(1)}, u32[]{:S(2)}, u32[]{:S(2)}) collective-permute-start(bf16[384,128]{1,0:T(8,128)(2,1)S(1)} %bitcast.45), channel_id=1, source_target_pairs={{1,2},{3,4},{5,6},{2,1},{4,3},{6,5},{9,10},{11,12},{13,14},{10,9},... | collective-permute-start | bytes 294920 | tf_op jit(solution)/shard_map/ppermute | solution.py:614
  77.0 6.9 %collective-permute-start.12 = (bf16[384,128]{1,0:T(8,128)(2,1)S(1)}, bf16[384,128]{1,0:T(8,128)(2,1)S(1)}, u32[]{:S(2)}, u32[]{:S(2)}) collective-permute-start(bf16[384,128]{1,0:T(8,128)(2,1)S(1)} %bitcast.46), channel_id=1, source_target_pairs={{0,1},{1,0},{2,3},{3,2},{4,5},{5,4},{6,7},{7,6},{8,9},{9,8},{10,11... | collective-permute-start | bytes 294920 | tf_op jit(solution)/shard_map/ppermute | solution.py:614

commit v5 on v4

--- a/solution.py
+++ b/solution.py
@@ -67,16 +67,18 @@
 
 
 def convolved(weights, shifts, rows, depth):
+    tall = weights.shape[1] // 3
     total = None
+    for step in range(3):
+        window = shifts[step, rows[0] : rows[1], : (depth + 2) * 128]
+        tap = weights[step][:, : rows[1] - rows[0]]
+        term = jnp.dot(tap, window, preferred_element_type=F32)
+        total = term if total is None else total + term
+    value = None
     for down in range(3):
-        for step in range(3):
-            window = shifts[step, rows[0] : rows[1], down * 128 : (down + depth) * 128]
-            tap = weights[down * 3 + step]
-            term = jnp.dot(
-                tap[:, : rows[1] - rows[0]], window, preferred_element_type=F32
-            )
-            total = term if total is None else total + term
-    return total
+        part = total[down * tall : (down + 1) * tall, down * 128 : (down + depth) * 128]
+        value = part if value is None else value + part
+    return value
 
 
 def sigmoid(values):
@@ -148,7 +150,7 @@
                                 place == row - across, spread[at : at + chans], value
                             )
                         wide[row * chans : (row + 1) * chans, :] = value
-                    taps[down * 3 + step] = wide[:size, :].T.astype(BF16)
+                    taps[step, down * 128 : down * 128 + 128, :] = wide[:size, :].T.astype(BF16)
         for level in range(1, 4):
             rows, chans, feats = dims[level]
             if level == 2:
@@ -172,12 +174,11 @@
                             value = jnp.where(
                                 place == row + across, spread[at : at + chans], value
                             )
-                        taps[down * 3 + step, row * chans : (row + 1) * chans, :] = (
-                            value.astype(BF16)
-                        )
-
-    shapes = [(9, 128, 256), (9, 128, 128), (9, 128, 128), (9, 128, 256)]
-    shapes += [(9, 64, 192), (9, 128, 384), (9, 64, 384)]
+                        at = (down * rows + row) * chans
+                        taps[step, at : at + chans, :] = value.astype(BF16)
+
+    shapes = [(3, 384, 256), (3, 384, 128), (3, 384, 128), (3, 384, 256)]
+    shapes += [(3, 192, 192), (3, 384, 384), (3, 192, 384)]
     flat = [kernel.reshape(-1, kernel.shape[-1]) for kernel in kernels]
     return call(body, [(s, BF16) for s in shapes], [((256, 128), F32)], 1 << 27, *flat)
 
@@ -361,7 +362,8 @@
             value = None
             for tap in range(9):
                 window = shifts[tap, near * 64 : near * 64 + 192, :]
-                term = jnp.dot(taps[tap][:, :192], window, preferred_element_type=F32)
+                weight = taps[tap % 3, tap // 3 * 128 : tap // 3 * 128 + 128, :192]
+                term = jnp.dot(weight, window, preferred_element_type=F32)
                 value = term if value is None else value + term
             upstream = jnp.zeros((128, 128), F32)
             for layer in range(3):
@@ -386,9 +388,8 @@
         for down in range(3):
             for step in range(3):
                 window = near_cell(deltas[...], down - 1, step - 1)
-                term = jnp.dot(
-                    taps_back[down * 3 + step], window, preferred_element_type=F32
-                )
+                weight = taps_back[step, down * 64 : down * 64 + 64, :]
+                term = jnp.dot(weight, window, preferred_element_type=F32)
                 carried = term if carried is None else carried + term
         carried = exact_dot(turned(carried, -32), pair_columns(False))
         carried = jnp.concatenate([carried, carried], axis=0)
@@ -448,17 +449,17 @@
 
 def put_grads(tall, shifts, rows, offset, depth, delta, dims):
     count, chans, feats = dims
+    size = rows[1] - rows[0]
     for down in range(3):
+        at = (offset + down) * 128
+        window = [shifts[step, rows[0] : rows[1], at : at + depth * 128] for step in range(3)]
+        product = lax.dot_general(
+            jnp.concatenate(window, axis=0), delta, NT, preferred_element_type=F32
+        )
         for step in range(3):
-            at = (offset + down) * 128
-            product = lax.dot_general(
-                shifts[step, rows[0] : rows[1], at : at + depth * 128],
-                delta,
-                NT,
-                preferred_element_type=F32,
-            )
             tap = (down * 3 + step) * 3 * chans
-            tall[tap : tap + 3 * chans, :] = diagonal(product, count, chans, feats)
+            part = product[step * size : (step + 1) * size]
+            tall[tap : tap + 3 * chans, :] = diagonal(part, count, chans, feats)
 
 
 def grad_quarter_of(act, delta):

time: 166 us -> 167 us (level)
  no operation moved by 1% of the time
where the time goes in v5:
time: 167 us
  blocking collectives  91.2 us (55%)
  starting transfers between devices  46.9 us (28%)
  Pallas kernels  14 us (8%)
  waiting for transfers between devices  9.76 us (6%)
  local copies, waits for them, and re-layouts  2.59 us (2%)
    ppermute x7, starting transfers between devices, swaps(): lax.ppermute(to_one, axis, first)  32.9 us
    all_to_all x1, blocking collectives, summed(): pieces = lax.all_to_all(terms.reshape(first, rows, width), inner, 0, 0)  23.3 us
    all_to_all x1, blocking collectives, summed(): pieces = lax.all_to_all(part, outer, 0, 0, tiled=True)  20 us
    all_to_all x1, blocking collectives, summed(): return lax.all_to_all(copies(part, first), inner, 0, 0).reshape(terms.shape)  17 us
    all_to_all x1, blocking collectives, summed(): lax.all_to_all(lax.optimization_barrier(spread), outer, 0, 0, tiled=True)  15.6 us
    all_to_all x1, blocking collectives, on_device(): lax.all_to_all(lax.optimization_barrier(jnp.broadcast_to(act3[None], many...  15.3 us
    pallas_call x11, Pallas kernels, call(): pl.pallas_call(body, out_shape=tuple((jax.ShapeDtypeStruct(shape, dtype)...  14 us
    ppermute x7, starting transfers between devices, swaps(): lax.ppermute(to_two, axis, second)  14 us
  transfers between devices with their start and end apart: 14, of which 7 were waited for; matrix products, arithmetic and copies ran while one was open for 1% of the time, Pallas kernels for 1%

profile of v5, /device:TPU:1, one launch (start us, length us, event | category | flops | bytes accessed | tf_op | source)
XLA Modules:
  0.0 166.5 jit_solution(11564878781843689906)
XLA Ops:
  0.7 0.9 broadcast_select_fusion
  1.6 8.8 %collective-permute-start = (bf16[1,128,128]{2,1,0:T(8,128)(2,1)S(1)}, bf16[1,128,128]{2,1,0:T(8,128)(2,1)S(1)}, u32[]{:S(2)}, u32[]{:S(2)}) collective-permute-start(bf16[1,128,128]{2,1,0:T(8,128)(2,1)S(1)} %bitcast.47), channel_id=1, source_target_pairs={{0,8},{8,0},{16,24},{24,16},{32,40},{40,32},{48,56},{56,48},{64,72... | collective-permute-start | bytes 98312 | tf_op jit(solution)/shard_map/ppermute | solution.py:615
  10.4 1.9 %collective-permute-start.1 = (bf16[1,128,128]{2,1,0:T(8,128)(2,1)S(1)}, bf16[1,128,128]{2,1,0:T(8,128)(2,1)S(1)}, u32[]{:S(2)}, u32[]{:S(2)}) collective-permute-start(bf16[1,128,128]{2,1,0:T(8,128)(2,1)S(1)} %bitcast.48), channel_id=1, source_target_pairs={{8,16},{24,32},{40,48},{56,64},{72,80},{88,96},{104,112},{120,128}... | collective-permute-start | bytes 98312 | tf_op jit(solution)/shard_map/ppermute | solution.py:615
  12.3 1.1 copy.18
  13.4 0.9 copy.22
  14.6 1.0 collective-permute-done.1.two
  15.6 1.9 %collective-permute-start.2 = (bf16[160,128]{1,0:T(8,128)(2,1)S(1)}, bf16[160,128]{1,0:T(8,128)(2,1)S(1)}, u32[]{:S(2)}, u32[]{:S(2)}) collective-permute-start(bf16[160,128]{1,0:T(8,128)(2,1)S(1)} %get-tuple-element.43), channel_id=1, source_target_pairs={{0,1},{1,0},{2,3},{3,2},{4,5},{5,4},{6,7},{7,6},{8,9},{9,8},{10,11... | collective-permute-start | bytes 122888 | tf_op jit(solution)/shard_map/ppermute | solution.py:615
  18.3 1.4 shard_map.121
  19.7 0.7 collective-permute-done.2.above
  20.4 1.3 shard_map.122
  21.7 1.9 %collective-permute-start.4 = (bf16[336,128]{1,0:T(8,128)(2,1)S(1)}, bf16[336,128]{1,0:T(8,128)(2,1)S(1)}, u32[]{:S(2)}, u32[]{:S(2)}) collective-permute-start(bf16[336,128]{1,0:T(8,128)(2,1)S(1)} %get-tuple-element.52), channel_id=1, source_target_pairs={{0,8},{8,0},{16,24},{24,16},{32,40},{40,32},{48,56},{56,48},{64,72... | collective-permute-start | bytes 258056 | tf_op jit(solution)/shard_map/ppermute | solution.py:615
  23.6 3.8 %collective-permute-start.5 = (bf16[336,128]{1,0:T(8,128)(2,1)S(1)}, bf16[336,128]{1,0:T(8,128)(2,1)S(1)}, u32[]{:S(2)}, u32[]{:S(2)}) collective-permute-start(bf16[336,128]{1,0:T(8,128)(2,1)S(1)} %get-tuple-element.53), channel_id=1, source_target_pairs={{8,16},{24,32},{40,48},{56,64},{72,80},{88,96},{104,112},{120,128}... | collective-permute-start | bytes 258056 | tf_op jit(solution)/shard_map/ppermute | solution.py:615
  27.5 2.1 %collective-permute-done.5.two.skip_two.two1 = bf16[336,128]{1,0:T(8,128)(2,1)S(1)} collective-permute-done((bf16[336,128]{1,0:T(8,128)(2,1)S(1)}, bf16[336,128]{1,0:T(8,128)(2,1)S(1)}, u32[]{:S(2)}, u32[]{:S(2)}) %collective-permute-start.5) | collective-permute-done | bytes 86048 | tf_op jit(solution)/shard_map/ppermute | solution.py:615
  29.7 5.6 %collective-permute-start.6 = (bf16[384,128]{1,0:T(8,128)(2,1)S(1)}, bf16[384,128]{1,0:T(8,128)(2,1)S(1)}, u32[]{:S(2)}, u32[]{:S(2)}) collective-permute-start(bf16[384,128]{1,0:T(8,128)(2,1)S(1)} %get-tuple-element.54), channel_id=1, source_target_pairs={{0,1},{1,0},{2,3},{3,2},{4,5},{5,4},{6,7},{7,6},{8,9},{9,8},{10,11... | collective-permute-start | bytes 294920 | tf_op jit(solution)/shard_map/ppermute | solution.py:615
  35.3 0.7 collective-permute-start.7
  36.0 1.3 collective-permute-done.6.above.skip_above.above1
  37.3 3.3 %shard_map.124 = (f32[8,256,128]{2,1,0:T(8,128)S(1)}, bf16[4,128,128]{2,1,0:T(8,128)(2,1)S(1)}, f32[2,128,128]{2,1,0:T(8,128)S(1)}, f32[8,128]{1,0:T(8,128)S(1)}, bf16[3,160,1280]{2,1,0:T(8,128)(2,1)S(1)}) custom-call(bf16[4,64,128]{2,1,0:T(8,128)(2,1)S(1)} %get-tuple-element.51.act.own, bf16[336,128]{1,0:T(8,128)(2,1)S(1)} %collective-permute-done.4.one.skip_one.one1, ...), custom_call_target="tpu_custom_call" | custom-call | flops 536870912 | bytes 1048576 | tf_op jit(solution)/shard_map/pallas_call | solution.py:16
  40.6 15.3 %all_to_all.35.acts = f32[16,8,128]{2,1,0:T(8,128)S(1)} all-to-all(f32[16,8,128]{2,1,0:T(8,128)S(1)} %broadcast_in_dim.2), channel_id=1, replica_groups=mesh['x'=4,'z'=8,'c'=2,'gy'=8] {'c','gy'}, dimensions={0} | all-to-all | bytes 131072 | tf_op jit(solution)/shard_map/all_to_all | solution.py:732
  56.6 8.4 %collective-permute-start.8 = (f32[16,8,128]{2,1,0:T(8,128)S(1)}, f32[16,8,128]{2,1,0:T(8,128)S(1)}, u32[]{:S(2)}, u32[]{:S(2)}) collective-permute-start(f32[16,8,128]{2,1,0:T(8,128)S(1)} %all_to_all.35.acts), channel_id=1, source_target_pairs={{0,16},{16,0},{32,48},{48,32},{64,80},{80,64},{96,112},{112,96},{1... | collective-permute-start | bytes 196616 | tf_op jit(solution)/shard_map/ppermute | solution.py:615
  65.1 1.6 collective-permute-done.8.chip_one
  66.7 1.8 %shard_map.125 = (bf16[1,128,128]{2,1,0:T(8,128)(2,1)S(1)}, bf16[2,128,128]{2,1,0:T(8,128)(2,1)S(1)}, bf16[9,320,128]{2,1,0:T(8,128)(2,1)S(1)}, bf16[128,128]{1,0:T(8,128)(2,1)S(1)}) custom-call(f32[16,8,128]{2,1,0:T(8,128)S(1)} %all_to_all.35.acts, f32[16,8,128]{2,1,0:T(8,128)S(1)} %collective-permute-done.8.chip_one, ...), custom_call_target="tpu_custom_call" | custom-call | flops 268435456 | bytes 1048576 | tf_op jit(solution)/shard_map/pallas_call | solution.py:16
  68.5 5.6 %collective-permute-start.11 = (bf16[1,128,128]{2,1,0:T(8,128)(2,1)S(1)}, bf16[1,128,128]{2,1,0:T(8,128)(2,1)S(1)}, u32[]{:S(2)}, u32[]{:S(2)}) collective-permute-start(bf16[1,128,128]{2,1,0:T(8,128)(2,1)S(1)} %get-tuple-element.62.own), channel_id=1, source_target_pairs={{8,16},{24,32},{40,48},{56,64},{72,80},{88,96},{104,112},{120,128}... | collective-permute-start | bytes 98312 | tf_op jit(solution)/shard_map/ppermute | solution.py:615
  74.1 1.9 %collective-permute-start.10 = (bf16[1,128,128]{2,1,0:T(8,128)(2,1)S(1)}, bf16[1,128,128]{2,1,0:T(8,128)(2,1)S(1)}, u32[]{:S(2)}, u32[]{:S(2)}) collective-permute-start(bf16[1,128,128]{2,1,0:T(8,128)(2,1)S(1)} %get-tuple-element.62.own), channel_id=1, source_target_pairs={{0,8},{8,0},{16,24},{24,16},{32,40},{40,32},{48,56},{56,48},{64,72... | collective-permute-start | bytes 98312 | tf_op jit(solution)/shard_map/ppermute | solution.py:615
  76.1 1.2 collective-permute-done.10.one
  77.9 4.3 %collective-permute-start.12 = (bf16[384,128]{1,0:T(8,128)(2,1)S(1)}, bf16[384,128]{1,0:T(8,128)(2,1)S(1)}, u32[]{:S(2)}, u32[]{:S(2)}) collective-permute-start(bf16[384,128]{1,0:T(8,128)(2,1)S(1)} %bitcast.46), channel_id=1, source_target_pairs={{0,1},{1,0},{2,3},{3,2},{4,5},{5,4},{6,7},{7,6},{8,9},{9,8},{10,11... | collective-permute-start | bytes 294920 | tf_op jit(solution)/shard_map/ppermute | solution.py:615
  83.0 1.8 %collective-permute-done.12.above = bf16[384,128]{1,0:T(8,128)(2,1)S(1)} collective-permute-done((bf16[384,128]{1,0:T(8,128)(2,1)S(1)}, bf16[384,128]{1,0:T(8,128)(2,1)S(1)}, u32[]{:S(2)}, u32[]{:S(2)}) %collective-permute-start.12) | collective-permute-done | bytes 98336 | tf_op jit(solution)/shard_map/ppermute | solution.py:615
  84.8 3.9 %shard_map.128 = bf16[512,640]{1,0:T(8,128)(2,1)S(1)} custom-call(bf16[1,128,128]{2,1,0:T(8,128)(2,1)S(1)} %get-tuple-element.62.own, bf16[1,128,128]{2,1,0:T(8,128)(2,1)S(1)} %collective-permute-done.10.one, bf16[1,128,128]{2,1,0:T(8,128)(2,1)S(1)} %collective-permute-done.11.two, bf16[384,128]{1,0:T(8,128)(2,1)S(1)} %collective-permute-done.12.above, ...), custom_call_target="tpu_custom_call" | custom-call | flops 1073741824 | bytes 1048576 | tf_op jit(solution)/shard_map/pallas_call | solution.py:16
  88.7 23.3 %all_to_all.36 = bf16[8,64,640]{2,1,0:T(8,128)(2,1)S(1)} all-to-all(bf16[8,64,640]{2,1,0:T(8,128)(2,1)S(1)} %bitcast.27), channel_id=1, replica_groups=mesh['x'=4,'z'=8,'c'=2,'gy'=8] {'x','c'}, dimensions={0} | all-to-all | bytes 1310720 | tf_op jit(solution)/shard_map/all_to_all | solution.py:689
  112.3 20.0 %all_to_all.37 = f32[64,1,640]{2,1,0:T(1,128)S(1)} all-to-all(f32[64,1,640]{2,1,0:T(1,128)S(1)} %all_to_all.24), channel_id=1, replica_groups=mesh['x'=4,'z'=8,'c'=2,'gy'=8] {'z','gy'}, dimensions={0} | all-to-all | bytes 327680 | tf_op jit(solution)/shard_map/all_to_all | solution.py:691
  132.5 15.6 %all_to_all.38 = f32[64,1,640]{2,1,0:T(1,128)S(1)} all-to-all(f32[64,1,640]{2,1,0:T(1,128)S(1)} %all_to_all.26), channel_id=1, replica_groups=mesh['x'=4,'z'=8,'c'=2,'gy'=8] {'z','gy'}, dimensions={0} | all-to-all | bytes 327680 | tf_op jit(solution)/shard_map/all_to_all | solution.py:694
  148.2 17.0 %all_to_all.39 = bf16[8,64,640]{2,1,0:T(8,128)(2,1)S(1)} all-to-all(bf16[8,64,640]{2,1,0:T(8,128)(2,1)S(1)} %shard_map.129), channel_id=1, replica_groups=mesh['x'=4,'z'=8,'c'=2,'gy'=8] {'x','c'}, dimensions={0} | all-to-all | bytes 1310720 | tf_op jit(solution)/shard_map/all_to_all | solution.py:695
  165.2 1.4 shard_map.130
  (41 shorter events, 3.7 us)
Async XLA Ops:
  0.6 13.8 %copy-start.6 = (bf16[16,8,8,128]{3,2,1,0:T(8,128)(2,1)S(1)}, bf16[16,8,8,128]{3,2,1,0:T(8,128)(2,1)}, u32[]{:S(2)}) copy-start(bf16[16,8,8,128]{3,2,1,0:T(8,128)(2,1)} %param.14) | copy-start | bytes 786436
  0.6 17.6 %copy-start = (bf16[3,3,3,64,128]{4,3,2,1,0:T(8,128)(2,1)S(1)}, bf16[3,3,3,64,128]{4,3,2,1,0:T(8,128)(2,1)}, u32[]{:S(2)}) copy-start(bf16[3,3,3,64,128]{4,3,2,1,0:T(8,128)(2,1)} %param.13) | copy-start | bytes 1327108
  0.7 17.6 %copy-start.1 = (bf16[3,3,3,32,64]{4,3,2,1,0:T(8,128)(2,1)S(1)}, bf16[3,3,3,32,64]{4,3,2,1,0:T(8,128)(2,1)}, u32[]{:S(2)}) copy-start(bf16[3,3,3,32,64]{4,3,2,1,0:T(8,128)(2,1)} %param.12) | copy-start | bytes 331780
  0.7 17.6 %copy-start.3 = (bf16[3,3,3,16,32]{4,3,2,1,0:T(8,128)(2,1)S(1)}, bf16[3,3,3,16,32]{4,3,2,1,0:T(8,128)(2,1)}, u32[]{:S(2)}) copy-start(bf16[3,3,3,16,32]{4,3,2,1,0:T(8,128)(2,1)} %param.11) | copy-start | bytes 82948
  0.7 17.6 %copy-start.2 = (bf16[3,3,3,16,16]{4,3,2,1,0:T(8,128)(2,1)S(1)}, bf16[3,3,3,16,16]{4,3,2,1,0:T(8,128)(2,1)}, u32[]{:S(2)}) copy-start(bf16[3,3,3,16,16]{4,3,2,1,0:T(8,128)(2,1)} %param.10) | copy-start | bytes 41476
  1.6 13.1 %collective-permute-start = (bf16[1,128,128]{2,1,0:T(8,128)(2,1)S(1)}, bf16[1,128,128]{2,1,0:T(8,128)(2,1)S(1)}, u32[]{:S(2)}, u32[]{:S(2)}) collective-permute-start(bf16[1,128,128]{2,1,0:T(8,128)(2,1)S(1)} %bitcast.47), channel_id=1, source_target_pairs={{0,8},{8,0},{16,24},{24,16},{32,40},{40,32},{48,56},{56,48},{64,72... | collective-permute-start | bytes 98312 | tf_op jit(solution)/shard_map/ppermute | solution.py:615
  10.4 5.2 %collective-permute-start.1 = (bf16[1,128,128]{2,1,0:T(8,128)(2,1)S(1)}, bf16[1,128,128]{2,1,0:T(8,128)(2,1)S(1)}, u32[]{:S(2)}, u32[]{:S(2)}) collective-permute-start(bf16[1,128,128]{2,1,0:T(8,128)(2,1)S(1)} %bitcast.48), channel_id=1, source_target_pairs={{8,16},{24,32},{40,48},{56,64},{72,80},{88,96},{104,112},{120,128}... | collective-permute-start | bytes 98312 | tf_op jit(solution)/shard_map/ppermute | solution.py:615
  13.4 7.0 %copy-start.5 = (bf16[128,1,1,16]{0,3,2,1:T(8,128)(2,1)S(1)}, bf16[128,1,1,16]{0,3,2,1:T(8,128)(2,1)}, u32[]{:S(2)}) copy-start(bf16[128,1,1,16]{0,3,2,1:T(8,128)(2,1)} %param.17) | copy-start | bytes 12292
  15.6 4.7 %collective-permute-start.2 = (bf16[160,128]{1,0:T(8,128)(2,1)S(1)}, bf16[160,128]{1,0:T(8,128)(2,1)S(1)}, u32[]{:S(2)}, u32[]{:S(2)}) collective-permute-start(bf16[160,128]{1,0:T(8,128)(2,1)S(1)} %get-tuple-element.43), channel_id=1, source_target_pairs={{0,1},{1,0},{2,3},{3,2},{4,5},{5,4},{6,7},{7,6},{8,9},{9,8},{10,11... | collective-permute-start | bytes 122888 | tf_op jit(solution)/shard_map/ppermute | solution.py:615
  17.6 2.8 %collective-permute-start.3 = (bf16[160,128]{1,0:T(8,128)(2,1)S(1)}, bf16[160,128]{1,0:T(8,128)(2,1)S(1)}, u32[]{:S(2)}, u32[]{:S(2)}) collective-permute-start(bf16[160,128]{1,0:T(8,128)(2,1)S(1)} %get-tuple-element.44), channel_id=1, source_target_pairs={{1,2},{3,4},{5,6},{2,1},{4,3},{6,5},{9,10},{11,12},{13,14},{10,9},... | collective-permute-start | bytes 122888 | tf_op jit(solution)/shard_map/ppermute | solution.py:615
  21.7 5.8 %collective-permute-start.4 = (bf16[336,128]{1,0:T(8,128)(2,1)S(1)}, bf16[336,128]{1,0:T(8,128)(2,1)S(1)}, u32[]{:S(2)}, u32[]{:S(2)}) collective-permute-start(bf16[336,128]{1,0:T(8,128)(2,1)S(1)} %get-tuple-element.52), channel_id=1, source_target_pairs={{0,8},{8,0},{16,24},{24,16},{32,40},{40,32},{48,56},{56,48},{64,72... | collective-permute-start | bytes 258056 | tf_op jit(solution)/shard_map/ppermute | solution.py:615
  23.6 6.0 %collective-permute-start.5 = (bf16[336,128]{1,0:T(8,128)(2,1)S(1)}, bf16[336,128]{1,0:T(8,128)(2,1)S(1)}, u32[]{:S(2)}, u32[]{:S(2)}) collective-permute-start(bf16[336,128]{1,0:T(8,128)(2,1)S(1)} %get-tuple-element.53), channel_id=1, source_target_pairs={{8,16},{24,32},{40,48},{56,64},{72,80},{88,96},{104,112},{120,128}... | collective-permute-start | bytes 258056 | tf_op jit(solution)/shard_map/ppermute | solution.py:615
  29.6 37.1 %copy-start.4 = (bf16[64,2,2,32]{0,3,2,1:T(8,128)(2,1)S(1)}, bf16[64,2,2,32]{0,3,2,1:T(8,128)(2,1)}, u32[]{:S(2)}) copy-start(bf16[64,2,2,32]{0,3,2,1:T(8,128)(2,1)} %param.16) | copy-start | bytes 49156
  29.7 7.6 %collective-permute-start.6 = (bf16[384,128]{1,0:T(8,128)(2,1)S(1)}, bf16[384,128]{1,0:T(8,128)(2,1)S(1)}, u32[]{:S(2)}, u32[]{:S(2)}) collective-permute-start(bf16[384,128]{1,0:T(8,128)(2,1)S(1)} %get-tuple-element.54), channel_id=1, source_target_pairs={{0,1},{1,0},{2,3},{3,2},{4,5},{5,4},{6,7},{7,6},{8,9},{9,8},{10,11... | collective-permute-start | bytes 294920 | tf_op jit(solution)/shard_map/ppermute | solution.py:615
  35.3 2.0 %collective-permute-start.7 = (bf16[384,128]{1,0:T(8,128)(2,1)S(1)}, bf16[384,128]{1,0:T(8,128)(2,1)S(1)}, u32[]{:S(2)}, u32[]{:S(2)}) collective-permute-start(bf16[384,128]{1,0:T(8,128)(2,1)S(1)} %get-tuple-element.55), channel_id=1, source_target_pairs={{1,2},{3,4},{5,6},{2,1},{4,3},{6,5},{9,10},{11,12},{13,14},{10,9},... | collective-permute-start | bytes 294920 | tf_op jit(solution)/shard_map/ppermute | solution.py:615
  55.9 9.1 %collective-permute-start.9 = (f32[16,8,128]{2,1,0:T(8,128)S(1)}, f32[16,8,128]{2,1,0:T(8,128)S(1)}, u32[]{:S(2)}, u32[]{:S(2)}) collective-permute-start(f32[16,8,128]{2,1,0:T(8,128)S(1)} %all_to_all.35.acts), channel_id=1, source_target_pairs={{16,32},{48,64},{80,96},{112,128},{144,160},{176,192},{208,224},{2... | collective-permute-start | bytes 196616 | tf_op jit(solution)/shard_map/ppermute | solution.py:615
  56.6 10.1 %collective-permute-start.8 = (f32[16,8,128]{2,1,0:T(8,128)S(1)}, f32[16,8,128]{2,1,0:T(8,128)S(1)}, u32[]{:S(2)}, u32[]{:S(2)}) collective-permute-start(f32[16,8,128]{2,1,0:T(8,128)S(1)} %all_to_all.35.acts), channel_id=1, source_target_pairs={{0,16},{16,0},{32,48},{48,32},{64,80},{80,64},{96,112},{112,96},{1... | collective-permute-start | bytes 196616 | tf_op jit(solution)/shard_map/ppermute | solution.py:615
  68.5 7.5 %collective-permute-start.11 = (bf16[1,128,128]{2,1,0:T(8,128)(2,1)S(1)}, bf16[1,128,128]{2,1,0:T(8,128)(2,1)S(1)}, u32[]{:S(2)}, u32[]{:S(2)}) collective-permute-start(bf16[1,128,128]{2,1,0:T(8,128)(2,1)S(1)} %get-tuple-element.62.own), channel_id=1, source_target_pairs={{8,16},{24,32},{40,48},{56,64},{72,80},{88,96},{104,112},{120,128}... | collective-permute-start | bytes 98312 | tf_op jit(solution)/shard_map/ppermute | solution.py:615
  74.1 3.1 %collective-permute-start.10 = (bf16[1,128,128]{2,1,0:T(8,128)(2,1)S(1)}, bf16[1,128,128]{2,1,0:T(8,128)(2,1)S(1)}, u32[]{:S(2)}, u32[]{:S(2)}) collective-permute-start(bf16[1,128,128]{2,1,0:T(8,128)(2,1)S(1)} %get-tuple-element.62.own), channel_id=1, source_target_pairs={{0,8},{8,0},{16,24},{24,16},{32,40},{40,32},{48,56},{56,48},{64,72... | collective-permute-start | bytes 98312 | tf_op jit(solution)/shard_map/ppermute | solution.py:615
  77.2 5.8 %collective-permute-start.13 = (bf16[384,128]{1,0:T(8,128)(2,1)S(1)}, bf16[384,128]{1,0:T(8,128)(2,1)S(1)}, u32[]{:S(2)}, u32[]{:S(2)}) collective-permute-start(bf16[384,128]{1,0:T(8,128)(2,1)S(1)} %bitcast.45), channel_id=1, source_target_pairs={{1,2},{3,4},{5,6},{2,1},{4,3},{6,5},{9,10},{11,12},{13,14},{10,9},... | collective-permute-start | bytes 294920 | tf_op jit(solution)/shard_map/ppermute | solution.py:615
  77.9 6.9 %collective-permute-start.12 = (bf16[384,128]{1,0:T(8,128)(2,1)S(1)}, bf16[384,128]{1,0:T(8,128)(2,1)S(1)}, u32[]{:S(2)}, u32[]{:S(2)}) collective-permute-start(bf16[384,128]{1,0:T(8,128)(2,1)S(1)} %bitcast.46), channel_id=1, source_target_pairs={{0,1},{1,0},{2,3},{3,2},{4,5},{5,4},{6,7},{7,6},{8,9},{9,8},{10,11... | collective-permute-start | bytes 294920 | tf_op jit(solution)/shard_map/ppermute | solution.py:615

commit v6 on v4

--- a/solution.py
+++ b/solution.py
@@ -67,16 +67,15 @@
 
 
 def convolved(weights, shifts, rows, depth):
-    total = None
-    for down in range(3):
-        for step in range(3):
-            window = shifts[step, rows[0] : rows[1], down * 128 : (down + depth) * 128]
-            tap = weights[down * 3 + step]
-            term = jnp.dot(
-                tap[:, : rows[1] - rows[0]], window, preferred_element_type=F32
-            )
-            total = term if total is None else total + term
-    return total
+    windows = [
+        shifts[step, rows[0] : rows[1], down * 128 : (down + depth) * 128]
+        for down in range(3)
+        for step in range(3)
+    ]
+    size = 9 * (rows[1] - rows[0])
+    return jnp.dot(
+        weights[:, :size], jnp.concatenate(windows, axis=0), preferred_element_type=F32
+    )
 
 
 def sigmoid(values):
@@ -135,11 +134,13 @@
             spread = jnp.dot(
                 source, jnp.where(picks, 1.0, 0.0).astype(BF16), preferred_element_type=F32
             )
-            size = taps.shape[2]
+            size = taps.shape[1]
+            used = 9 * (rows + 2) * chans
+            if used < size:
+                wide[used:size, :] = jnp.zeros((size - used, 128), F32)
             place = lanes((chans, 128)) // feats
             for down in range(3):
                 for step in range(3):
-                    wide[...] = jnp.zeros_like(wide)
                     for row in range(rows + 2):
                         value = jnp.zeros((chans, 128), F32)
                         for across in range(3):
@@ -147,8 +148,9 @@
                             value = jnp.where(
                                 place == row - across, spread[at : at + chans], value
                             )
-                        wide[row * chans : (row + 1) * chans, :] = value
-                    taps[down * 3 + step] = wide[:size, :].T.astype(BF16)
+                        at = ((down * 3 + step) * (rows + 2) + row) * chans
+                        wide[at : at + chans, :] = value
+            taps[...] = wide[:size, :].T.astype(BF16)
         for level in range(1, 4):
             rows, chans, feats = dims[level]
             if level == 2:
@@ -172,14 +174,13 @@
                             value = jnp.where(
                                 place == row + across, spread[at : at + chans], value
                             )
-                        taps[down * 3 + step, row * chans : (row + 1) * chans, :] = (
-                            value.astype(BF16)
-                        )
-
-    shapes = [(9, 128, 256), (9, 128, 128), (9, 128, 128), (9, 128, 256)]
-    shapes += [(9, 64, 192), (9, 128, 384), (9, 64, 384)]
+                        at = (down * 3 + step) * size
+                        taps[row * chans : (row + 1) * chans, at : at + size] = value.astype(BF16)
+
+    shapes = [(128, 1536), (128, 896), (128, 1152), (128, 1792)]
+    shapes += [(64, 1728), (128, 3456), (64, 3456)]
     flat = [kernel.reshape(-1, kernel.shape[-1]) for kernel in kernels]
-    return call(body, [(s, BF16) for s in shapes], [((256, 128), F32)], 1 << 27, *flat)
+    return call(body, [(s, BF16) for s in shapes], [((1792, 128), F32)], 1 << 27, *flat)
 
 
 def forward_full(volume, halo_z, halo_y, weights, skip_half, skip_deep):
@@ -358,11 +359,8 @@
                     )
         place = lanes((128, 128)) // 16
         for near in range(3):
-            value = None
-            for tap in range(9):
-                window = shifts[tap, near * 64 : near * 64 + 192, :]
-                term = jnp.dot(taps[tap][:, :192], window, preferred_element_type=F32)
-                value = term if value is None else value + term
+            window = shifts[:, near * 64 : near * 64 + 192, :].reshape(1728, 128)
+            value = jnp.dot(taps[:, :1728], window, preferred_element_type=F32)
             upstream = jnp.zeros((128, 128), F32)
             for layer in range(3):
                 if near != 1:
@@ -382,14 +380,12 @@
             if near == 1:
                 delta_own[...] = jnp.where(place == 2, change, 0.0).astype(BF16)
             deltas[near * 128 : near * 128 + 128, :] = change
-        carried = None
-        for down in range(3):
-            for step in range(3):
-                window = near_cell(deltas[...], down - 1, step - 1)
-                term = jnp.dot(
-                    taps_back[down * 3 + step], window, preferred_element_type=F32
-                )
-                carried = term if carried is None else carried + term
+        windows = [
+            near_cell(deltas[...], down - 1, step - 1) for down in range(3) for step in range(3)
+        ]
+        carried = jnp.dot(
+            taps_back[...], jnp.concatenate(windows, axis=0), preferred_element_type=F32
+        )
         carried = exact_dot(turned(carried, -32), pair_columns(False))
         carried = jnp.concatenate([carried, carried], axis=0)
         dense = None
@@ -712,9 +708,10 @@
     one, two = swaps(jnp.where(even, last, first), jnp.where(even, first, last))
     skip3 = jnp.transpose(skip_eighth, (1, 2, 3, 0)).reshape(16, 128)
     skip2 = jnp.transpose(skip_quarter, (1, 2, 3, 0))
-    one, two, skip0, skip1, kernels = lax.optimization_barrier(
-        (one, two, laid_out(skip_full), laid_out(skip_half), kernels)
-    )
+    one, two, skip_full, skip_half, kernels = lax.optimization_barrier(
+        (one, two, skip_full, skip_half, kernels)
+    )
+    skip0, skip1 = laid_out(skip_full), laid_out(skip_half)
 
     halo_y = swaps(*edge_rows(one, two, volume), "gy")
     dims = ((8, 16, 16), (4, 16, 32), (2, 32, 64), (1, 64, 128))

time: 166 us -> 166 us (level)
  blocking collectives: 91.2 us -> 92.9 us
    ppermute x7, waiting for transfers between devices: 3.13 us -> 6.47 us  [swaps(): lax.ppermute(to_two, axis, second)]
    ppermute x7, starting transfers between devices: 32.7 us -> 29.5 us  [swaps(): lax.ppermute(to_one, axis, first)]
    ppermute x7, waiting for transfers between devices: 6.81 us -> 4.13 us  [swaps(): lax.ppermute(to_one, axis, first)]
    ppermute x7, starting transfers between devices: 14 us -> 16.6 us  [swaps(): lax.ppermute(to_two, axis, second)]
    all_to_all x1, blocking collectives: 23.3 us -> 25.5 us  [summed(): pieces = lax.all_to_all(terms.reshape(first, rows, width), inner, 0, 0)]
where the time goes in v6:
time: 166 us; the launch traced here: 165 us
  blocking collectives  92.9 us (56%)
  starting transfers between devices  46.1 us (28%)
  Pallas kernels  11.7 us (7%)
  waiting for transfers between devices  10.6 us (6%)
  local copies, waits for them, and re-layouts  1.68 us (1%)
    ppermute x7, starting transfers between devices, swaps(): lax.ppermute(to_one, axis, first)  29.5 us
    all_to_all x1, blocking collectives, summed(): pieces = lax.all_to_all(terms.reshape(first, rows, width), inner, 0, 0)  25.5 us
    all_to_all x1, blocking collectives, summed(): pieces = lax.all_to_all(part, outer, 0, 0, tiled=True)  19.2 us
    all_to_all x1, blocking collectives, summed(): return lax.all_to_all(copies(part, first), inner, 0, 0).reshape(terms.shape)  17 us
    ppermute x7, starting transfers between devices, swaps(): lax.ppermute(to_two, axis, second)  16.6 us
    all_to_all x1, blocking collectives, on_device(): lax.all_to_all(lax.optimization_barrier(jnp.broadcast_to(act3[None], many...  15.7 us
    all_to_all x1, blocking collectives, summed(): lax.all_to_all(lax.optimization_barrier(spread), outer, 0, 0, tiled=True)  15.6 us
    pallas_call x11, Pallas kernels, call(): pl.pallas_call(body, out_shape=tuple((jax.ShapeDtypeStruct(shape, dtype)...  11.7 us
  transfers between devices with their start and end apart: 14, of which 7 were waited for; matrix products, arithmetic and copies ran while one was open for 1% of the time, Pallas kernels for 1%

profile of v6, /device:TPU:1, one launch (start us, length us, event | category | flops | bytes accessed | tf_op | source)
XLA Modules:
  0.0 165.1 jit_solution(12877934105175110025)
XLA Ops:
  0.7 0.9 broadcast_select_fusion
  1.6 8.8 %collective-permute-start = (bf16[1,128,128]{2,1,0:T(8,128)(2,1)S(1)}, bf16[1,128,128]{2,1,0:T(8,128)(2,1)S(1)}, u32[]{:S(2)}, u32[]{:S(2)}) collective-permute-start(bf16[1,128,128]{2,1,0:T(8,128)(2,1)S(1)} %bitcast.47), channel_id=1, source_target_pairs={{0,8},{8,0},{16,24},{24,16},{32,40},{40,32},{48,56},{56,48},{64,72... | collective-permute-start | bytes 98312 | tf_op jit(solution)/shard_map/ppermute | solution.py:610
  10.4 1.9 %collective-permute-start.1 = (bf16[1,128,128]{2,1,0:T(8,128)(2,1)S(1)}, bf16[1,128,128]{2,1,0:T(8,128)(2,1)S(1)}, u32[]{:S(2)}, u32[]{:S(2)}) collective-permute-start(bf16[1,128,128]{2,1,0:T(8,128)(2,1)S(1)} %bitcast.48), channel_id=1, source_target_pairs={{8,16},{24,32},{40,48},{56,64},{72,80},{88,96},{104,112},{120,128}... | collective-permute-start | bytes 98312 | tf_op jit(solution)/shard_map/ppermute | solution.py:610
  12.3 1.1 copy.18
  13.5 2.2 %collective-permute-done.1.two = bf16[1,128,128]{2,1,0:T(8,128)(2,1)S(1)} collective-permute-done((bf16[1,128,128]{2,1,0:T(8,128)(2,1)S(1)}, bf16[1,128,128]{2,1,0:T(8,128)(2,1)S(1)}, u32[]{:S(2)}, u32[]{:S(2)}) %collective-permute-start.1) | collective-permute-done | bytes 32800 | tf_op jit(solution)/shard_map/ppermute | solution.py:610
  15.7 1.9 %collective-permute-start.2 = (bf16[160,128]{1,0:T(8,128)(2,1)S(1)}, bf16[160,128]{1,0:T(8,128)(2,1)S(1)}, u32[]{:S(2)}, u32[]{:S(2)}) collective-permute-start(bf16[160,128]{1,0:T(8,128)(2,1)S(1)} %get-tuple-element.43), channel_id=1, source_target_pairs={{0,1},{1,0},{2,3},{3,2},{4,5},{5,4},{6,7},{7,6},{8,9},{9,8},{10,11... | collective-permute-start | bytes 122888 | tf_op jit(solution)/shard_map/ppermute | solution.py:610
  18.4 1.3 shard_map.121
  19.7 0.7 collective-permute-done.2.above
  20.4 0.9 shard_map.122
  21.4 1.9 %collective-permute-start.4 = (bf16[336,128]{1,0:T(8,128)(2,1)S(1)}, bf16[336,128]{1,0:T(8,128)(2,1)S(1)}, u32[]{:S(2)}, u32[]{:S(2)}) collective-permute-start(bf16[336,128]{1,0:T(8,128)(2,1)S(1)} %get-tuple-element.52), channel_id=1, source_target_pairs={{0,8},{8,0},{16,24},{24,16},{32,40},{40,32},{48,56},{56,48},{64,72... | collective-permute-start | bytes 258056 | tf_op jit(solution)/shard_map/ppermute | solution.py:610
  23.3 3.1 %collective-permute-start.5 = (bf16[336,128]{1,0:T(8,128)(2,1)S(1)}, bf16[336,128]{1,0:T(8,128)(2,1)S(1)}, u32[]{:S(2)}, u32[]{:S(2)}) collective-permute-start(bf16[336,128]{1,0:T(8,128)(2,1)S(1)} %get-tuple-element.53), channel_id=1, source_target_pairs={{8,16},{24,32},{40,48},{56,64},{72,80},{88,96},{104,112},{120,128}... | collective-permute-start | bytes 258056 | tf_op jit(solution)/shard_map/ppermute | solution.py:610
  26.4 2.7 %collective-permute-done.5.two.skip_two.two1 = bf16[336,128]{1,0:T(8,128)(2,1)S(1)} collective-permute-done((bf16[336,128]{1,0:T(8,128)(2,1)S(1)}, bf16[336,128]{1,0:T(8,128)(2,1)S(1)}, u32[]{:S(2)}, u32[]{:S(2)}) %collective-permute-start.5) | collective-permute-done | bytes 86048 | tf_op jit(solution)/shard_map/ppermute | solution.py:610
  29.2 5.3 %collective-permute-start.6 = (bf16[384,128]{1,0:T(8,128)(2,1)S(1)}, bf16[384,128]{1,0:T(8,128)(2,1)S(1)}, u32[]{:S(2)}, u32[]{:S(2)}) collective-permute-start(bf16[384,128]{1,0:T(8,128)(2,1)S(1)} %get-tuple-element.54), channel_id=1, source_target_pairs={{0,1},{1,0},{2,3},{3,2},{4,5},{5,4},{6,7},{7,6},{8,9},{9,8},{10,11... | collective-permute-start | bytes 294920 | tf_op jit(solution)/shard_map/ppermute | solution.py:610
  34.5 0.7 collective-permute-start.7
  35.2 1.3 collective-permute-done.6.above.skip_above.above1
  36.5 2.0 %shard_map.124 = (f32[8,256,128]{2,1,0:T(8,128)S(1)}, bf16[4,128,128]{2,1,0:T(8,128)(2,1)S(1)}, f32[2,128,128]{2,1,0:T(8,128)S(1)}, f32[8,128]{1,0:T(8,128)S(1)}, bf16[3,160,1280]{2,1,0:T(8,128)(2,1)S(1)}) custom-call(bf16[4,64,128]{2,1,0:T(8,128)(2,1)S(1)} %get-tuple-element.51.act.own, bf16[336,128]{1,0:T(8,128)(2,1)S(1)} %collective-permute-done.4.one.skip_one.one1, ...), custom_call_target="tpu_custom_call" | custom-call | flops 536870912 | bytes 1048576 | tf_op jit(solution)/shard_map/pallas_call | solution.py:16
  38.5 15.7 %all_to_all.35.acts = f32[16,8,128]{2,1,0:T(8,128)S(1)} all-to-all(f32[16,8,128]{2,1,0:T(8,128)S(1)} %broadcast_in_dim.2), channel_id=1, replica_groups=mesh['x'=4,'z'=8,'c'=2,'gy'=8] {'c','gy'}, dimensions={0} | all-to-all | bytes 131072 | tf_op jit(solution)/shard_map/all_to_all | solution.py:728
  54.2 5.3 %collective-permute-start.8 = (f32[16,8,128]{2,1,0:T(8,128)S(1)}, f32[16,8,128]{2,1,0:T(8,128)S(1)}, u32[]{:S(2)}, u32[]{:S(2)}) collective-permute-start(f32[16,8,128]{2,1,0:T(8,128)S(1)} %all_to_all.35.acts), channel_id=1, source_target_pairs={{0,16},{16,0},{32,48},{48,32},{64,80},{80,64},{96,112},{112,96},{1... | collective-permute-start | bytes 196616 | tf_op jit(solution)/shard_map/ppermute | solution.py:610
  60.2 1.0 collective-permute-done.8.chip_one
  61.1 1.7 %shard_map.125 = (bf16[1,128,128]{2,1,0:T(8,128)(2,1)S(1)}, bf16[2,128,128]{2,1,0:T(8,128)(2,1)S(1)}, bf16[9,320,128]{2,1,0:T(8,128)(2,1)S(1)}, bf16[128,128]{1,0:T(8,128)(2,1)S(1)}) custom-call(f32[16,8,128]{2,1,0:T(8,128)S(1)} %all_to_all.35.acts, f32[16,8,128]{2,1,0:T(8,128)S(1)} %collective-permute-done.8.chip_one, ...), custom_call_target="tpu_custom_call" | custom-call | flops 268435456 | bytes 1048576 | tf_op jit(solution)/shard_map/pallas_call | solution.py:16
  62.8 3.7 %collective-permute-start.10 = (bf16[1,128,128]{2,1,0:T(8,128)(2,1)S(1)}, bf16[1,128,128]{2,1,0:T(8,128)(2,1)S(1)}, u32[]{:S(2)}, u32[]{:S(2)}) collective-permute-start(bf16[1,128,128]{2,1,0:T(8,128)(2,1)S(1)} %get-tuple-element.62.own), channel_id=1, source_target_pairs={{0,8},{8,0},{16,24},{24,16},{32,40},{40,32},{48,56},{56,48},{64,72... | collective-permute-start | bytes 98312 | tf_op jit(solution)/shard_map/ppermute | solution.py:610
  66.5 9.0 %collective-permute-start.11 = (bf16[1,128,128]{2,1,0:T(8,128)(2,1)S(1)}, bf16[1,128,128]{2,1,0:T(8,128)(2,1)S(1)}, u32[]{:S(2)}, u32[]{:S(2)}) collective-permute-start(bf16[1,128,128]{2,1,0:T(8,128)(2,1)S(1)} %get-tuple-element.62.own), channel_id=1, source_target_pairs={{8,16},{24,32},{40,48},{56,64},{72,80},{88,96},{104,112},{120,128}... | collective-permute-start | bytes 98312 | tf_op jit(solution)/shard_map/ppermute | solution.py:610
  75.5 1.6 collective-permute-done.11.two
  77.1 2.6 %collective-permute-start.12 = (bf16[384,128]{1,0:T(8,128)(2,1)S(1)}, bf16[384,128]{1,0:T(8,128)(2,1)S(1)}, u32[]{:S(2)}, u32[]{:S(2)}) collective-permute-start(bf16[384,128]{1,0:T(8,128)(2,1)S(1)} %bitcast.45), channel_id=1, source_target_pairs={{0,1},{1,0},{2,3},{3,2},{4,5},{5,4},{6,7},{7,6},{8,9},{9,8},{10,11... | collective-permute-start | bytes 294920 | tf_op jit(solution)/shard_map/ppermute | solution.py:610
  79.7 0.7 collective-permute-start.13
  81.3 1.1 collective-permute-done.12.above
  82.5 3.5 %shard_map.128 = bf16[512,640]{1,0:T(8,128)(2,1)S(1)} custom-call(bf16[1,128,128]{2,1,0:T(8,128)(2,1)S(1)} %get-tuple-element.62.own, bf16[1,128,128]{2,1,0:T(8,128)(2,1)S(1)} %collective-permute-done.10.one, bf16[1,128,128]{2,1,0:T(8,128)(2,1)S(1)} %collective-permute-done.11.two, bf16[384,128]{1,0:T(8,128)(2,1)S(1)} %collective-permute-done.12.above, ...), custom_call_target="tpu_custom_call" | custom-call | flops 1073741824 | bytes 1048576 | tf_op jit(solution)/shard_map/pallas_call | solution.py:16
  85.9 25.5 %all_to_all.36 = bf16[8,64,640]{2,1,0:T(8,128)(2,1)S(1)} all-to-all(bf16[8,64,640]{2,1,0:T(8,128)(2,1)S(1)} %bitcast.27), channel_id=1, replica_groups=mesh['x'=4,'z'=8,'c'=2,'gy'=8] {'x','c'}, dimensions={0} | all-to-all | bytes 1310720 | tf_op jit(solution)/shard_map/all_to_all | solution.py:684
  111.6 19.2 %all_to_all.37 = f32[64,1,640]{2,1,0:T(1,128)S(1)} all-to-all(f32[64,1,640]{2,1,0:T(1,128)S(1)} %all_to_all.24), channel_id=1, replica_groups=mesh['x'=4,'z'=8,'c'=2,'gy'=8] {'z','gy'}, dimensions={0} | all-to-all | bytes 327680 | tf_op jit(solution)/shard_map/all_to_all | solution.py:686
  131.0 15.6 %all_to_all.38 = f32[64,1,640]{2,1,0:T(1,128)S(1)} all-to-all(f32[64,1,640]{2,1,0:T(1,128)S(1)} %all_to_all.26), channel_id=1, replica_groups=mesh['x'=4,'z'=8,'c'=2,'gy'=8] {'z','gy'}, dimensions={0} | all-to-all | bytes 327680 | tf_op jit(solution)/shard_map/all_to_all | solution.py:689
  146.7 17.0 %all_to_all.39 = bf16[8,64,640]{2,1,0:T(8,128)(2,1)S(1)} all-to-all(bf16[8,64,640]{2,1,0:T(8,128)(2,1)S(1)} %shard_map.129), channel_id=1, replica_groups=mesh['x'=4,'z'=8,'c'=2,'gy'=8] {'x','c'}, dimensions={0} | all-to-all | bytes 1310720 | tf_op jit(solution)/shard_map/all_to_all | solution.py:690
  163.7 1.4 shard_map.130
  (43 shorter events, 3.1 us)
Async XLA Ops:
  0.6 17.7 %copy-start.2 = (bf16[3,3,3,16,16]{4,3,2,1,0:T(8,128)(2,1)S(1)}, bf16[3,3,3,16,16]{4,3,2,1,0:T(8,128)(2,1)}, u32[]{:S(2)}) copy-start(bf16[3,3,3,16,16]{4,3,2,1,0:T(8,128)(2,1)} %param.10) | copy-start | bytes 41476
  0.6 17.7 %copy-start.3 = (bf16[3,3,3,16,32]{4,3,2,1,0:T(8,128)(2,1)S(1)}, bf16[3,3,3,16,32]{4,3,2,1,0:T(8,128)(2,1)}, u32[]{:S(2)}) copy-start(bf16[3,3,3,16,32]{4,3,2,1,0:T(8,128)(2,1)} %param.11) | copy-start | bytes 82948
  0.7 17.7 %copy-start.1 = (bf16[3,3,3,32,64]{4,3,2,1,0:T(8,128)(2,1)S(1)}, bf16[3,3,3,32,64]{4,3,2,1,0:T(8,128)(2,1)}, u32[]{:S(2)}) copy-start(bf16[3,3,3,32,64]{4,3,2,1,0:T(8,128)(2,1)} %param.12) | copy-start | bytes 331780
  0.7 17.7 %copy-start = (bf16[3,3,3,64,128]{4,3,2,1,0:T(8,128)(2,1)S(1)}, bf16[3,3,3,64,128]{4,3,2,1,0:T(8,128)(2,1)}, u32[]{:S(2)}) copy-start(bf16[3,3,3,64,128]{4,3,2,1,0:T(8,128)(2,1)} %param.13) | copy-start | bytes 1327108
  0.7 17.6 %copy-start.7 = (bf16[32,4,4,64]{3,2,1,0:T(4,128)(2,1)S(1)}, bf16[32,4,4,64]{3,2,1,0:T(4,128)(2,1)}, u32[]{:S(2)}) copy-start(bf16[32,4,4,64]{3,2,1,0:T(4,128)(2,1)} %param.15) | copy-start | bytes 196612
  1.6 18.8 %copy-start.5 = (bf16[128,1,1,16]{0,3,2,1:T(8,128)(2,1)S(1)}, bf16[128,1,1,16]{0,3,2,1:T(8,128)(2,1)}, u32[]{:S(2)}) copy-start(bf16[128,1,1,16]{0,3,2,1:T(8,128)(2,1)} %param.17) | copy-start | bytes 12292
  1.6 11.9 %collective-permute-start = (bf16[1,128,128]{2,1,0:T(8,128)(2,1)S(1)}, bf16[1,128,128]{2,1,0:T(8,128)(2,1)S(1)}, u32[]{:S(2)}, u32[]{:S(2)}) collective-permute-start(bf16[1,128,128]{2,1,0:T(8,128)(2,1)S(1)} %bitcast.47), channel_id=1, source_target_pairs={{0,8},{8,0},{16,24},{24,16},{32,40},{40,32},{48,56},{56,48},{64,72... | collective-permute-start | bytes 98312 | tf_op jit(solution)/shard_map/ppermute | solution.py:610
  10.4 5.2 %collective-permute-start.1 = (bf16[1,128,128]{2,1,0:T(8,128)(2,1)S(1)}, bf16[1,128,128]{2,1,0:T(8,128)(2,1)S(1)}, u32[]{:S(2)}, u32[]{:S(2)}) collective-permute-start(bf16[1,128,128]{2,1,0:T(8,128)(2,1)S(1)} %bitcast.48), channel_id=1, source_target_pairs={{8,16},{24,32},{40,48},{56,64},{72,80},{88,96},{104,112},{120,128}... | collective-permute-start | bytes 98312 | tf_op jit(solution)/shard_map/ppermute | solution.py:610
  15.7 4.7 %collective-permute-start.2 = (bf16[160,128]{1,0:T(8,128)(2,1)S(1)}, bf16[160,128]{1,0:T(8,128)(2,1)S(1)}, u32[]{:S(2)}, u32[]{:S(2)}) collective-permute-start(bf16[160,128]{1,0:T(8,128)(2,1)S(1)} %get-tuple-element.43), channel_id=1, source_target_pairs={{0,1},{1,0},{2,3},{3,2},{4,5},{5,4},{6,7},{7,6},{8,9},{9,8},{10,11... | collective-permute-start | bytes 122888 | tf_op jit(solution)/shard_map/ppermute | solution.py:610
  17.6 2.8 %collective-permute-start.3 = (bf16[160,128]{1,0:T(8,128)(2,1)S(1)}, bf16[160,128]{1,0:T(8,128)(2,1)S(1)}, u32[]{:S(2)}, u32[]{:S(2)}) collective-permute-start(bf16[160,128]{1,0:T(8,128)(2,1)S(1)} %get-tuple-element.44), channel_id=1, source_target_pairs={{1,2},{3,4},{5,6},{2,1},{4,3},{6,5},{9,10},{11,12},{13,14},{10,9},... | collective-permute-start | bytes 122888 | tf_op jit(solution)/shard_map/ppermute | solution.py:610
  21.4 5.0 %collective-permute-start.4 = (bf16[336,128]{1,0:T(8,128)(2,1)S(1)}, bf16[336,128]{1,0:T(8,128)(2,1)S(1)}, u32[]{:S(2)}, u32[]{:S(2)}) collective-permute-start(bf16[336,128]{1,0:T(8,128)(2,1)S(1)} %get-tuple-element.52), channel_id=1, source_target_pairs={{0,8},{8,0},{16,24},{24,16},{32,40},{40,32},{48,56},{56,48},{64,72... | collective-permute-start | bytes 258056 | tf_op jit(solution)/shard_map/ppermute | solution.py:610
  23.3 5.8 %collective-permute-start.5 = (bf16[336,128]{1,0:T(8,128)(2,1)S(1)}, bf16[336,128]{1,0:T(8,128)(2,1)S(1)}, u32[]{:S(2)}, u32[]{:S(2)}) collective-permute-start(bf16[336,128]{1,0:T(8,128)(2,1)S(1)} %get-tuple-element.53), channel_id=1, source_target_pairs={{8,16},{24,32},{40,48},{56,64},{72,80},{88,96},{104,112},{120,128}... | collective-permute-start | bytes 258056 | tf_op jit(solution)/shard_map/ppermute | solution.py:610
  29.1 32.0 %copy-start.4 = (bf16[64,2,2,32]{0,3,2,1:T(8,128)(2,1)S(1)}, bf16[64,2,2,32]{0,3,2,1:T(8,128)(2,1)}, u32[]{:S(2)}) copy-start(bf16[64,2,2,32]{0,3,2,1:T(8,128)(2,1)} %param.16) | copy-start | bytes 49156
  29.2 7.3 %collective-permute-start.6 = (bf16[384,128]{1,0:T(8,128)(2,1)S(1)}, bf16[384,128]{1,0:T(8,128)(2,1)S(1)}, u32[]{:S(2)}, u32[]{:S(2)}) collective-permute-start(bf16[384,128]{1,0:T(8,128)(2,1)S(1)} %get-tuple-element.54), channel_id=1, source_target_pairs={{0,1},{1,0},{2,3},{3,2},{4,5},{5,4},{6,7},{7,6},{8,9},{9,8},{10,11... | collective-permute-start | bytes 294920 | tf_op jit(solution)/shard_map/ppermute | solution.py:610
  34.5 2.0 %collective-permute-start.7 = (bf16[384,128]{1,0:T(8,128)(2,1)S(1)}, bf16[384,128]{1,0:T(8,128)(2,1)S(1)}, u32[]{:S(2)}, u32[]{:S(2)}) collective-permute-start(bf16[384,128]{1,0:T(8,128)(2,1)S(1)} %get-tuple-element.55), channel_id=1, source_target_pairs={{1,2},{3,4},{5,6},{2,1},{4,3},{6,5},{9,10},{11,12},{13,14},{10,9},... | collective-permute-start | bytes 294920 | tf_op jit(solution)/shard_map/ppermute | solution.py:610
  38.5 41.9 %copy-start.6 = (bf16[16,8,8,128]{3,2,1,0:T(8,128)(2,1)S(1)}, bf16[16,8,8,128]{3,2,1,0:T(8,128)(2,1)}, u32[]{:S(2)}) copy-start(bf16[16,8,8,128]{3,2,1,0:T(8,128)(2,1)} %param.14) | copy-start | bytes 786436
  54.2 7.0 %collective-permute-start.8 = (f32[16,8,128]{2,1,0:T(8,128)S(1)}, f32[16,8,128]{2,1,0:T(8,128)S(1)}, u32[]{:S(2)}, u32[]{:S(2)}) collective-permute-start(f32[16,8,128]{2,1,0:T(8,128)S(1)} %all_to_all.35.acts), channel_id=1, source_target_pairs={{0,16},{16,0},{32,48},{48,32},{64,80},{80,64},{96,112},{112,96},{1... | collective-permute-start | bytes 196616 | tf_op jit(solution)/shard_map/ppermute | solution.py:610
  59.5 1.6 collective-permute-start.9
  62.8 12.7 %collective-permute-start.10 = (bf16[1,128,128]{2,1,0:T(8,128)(2,1)S(1)}, bf16[1,128,128]{2,1,0:T(8,128)(2,1)S(1)}, u32[]{:S(2)}, u32[]{:S(2)}) collective-permute-start(bf16[1,128,128]{2,1,0:T(8,128)(2,1)S(1)} %get-tuple-element.62.own), channel_id=1, source_target_pairs={{0,8},{8,0},{16,24},{24,16},{32,40},{40,32},{48,56},{56,48},{64,72... | collective-permute-start | bytes 98312 | tf_op jit(solution)/shard_map/ppermute | solution.py:610
  66.5 10.6 %collective-permute-start.11 = (bf16[1,128,128]{2,1,0:T(8,128)(2,1)S(1)}, bf16[1,128,128]{2,1,0:T(8,128)(2,1)S(1)}, u32[]{:S(2)}, u32[]{:S(2)}) collective-permute-start(bf16[1,128,128]{2,1,0:T(8,128)(2,1)S(1)} %get-tuple-element.62.own), channel_id=1, source_target_pairs={{8,16},{24,32},{40,48},{56,64},{72,80},{88,96},{104,112},{120,128}... | collective-permute-start | bytes 98312 | tf_op jit(solution)/shard_map/ppermute | solution.py:610
  77.1 5.4 %collective-permute-start.12 = (bf16[384,128]{1,0:T(8,128)(2,1)S(1)}, bf16[384,128]{1,0:T(8,128)(2,1)S(1)}, u32[]{:S(2)}, u32[]{:S(2)}) collective-permute-start(bf16[384,128]{1,0:T(8,128)(2,1)S(1)} %bitcast.45), channel_id=1, source_target_pairs={{0,1},{1,0},{2,3},{3,2},{4,5},{5,4},{6,7},{7,6},{8,9},{9,8},{10,11... | collective-permute-start | bytes 294920 | tf_op jit(solution)/shard_map/ppermute | solution.py:610
  79.7 2.8 %collective-permute-start.13 = (bf16[384,128]{1,0:T(8,128)(2,1)S(1)}, bf16[384,128]{1,0:T(8,128)(2,1)S(1)}, u32[]{:S(2)}, u32[]{:S(2)}) collective-permute-start(bf16[384,128]{1,0:T(8,128)(2,1)S(1)} %bitcast.46), channel_id=1, source_target_pairs={{1,2},{3,4},{5,6},{2,1},{4,3},{6,5},{9,10},{11,12},{13,14},{10,9},... | collective-permute-start | bytes 294920 | tf_op jit(solution)/shard_map/ppermute | solution.py:610

commit v7 on v6

--- a/solution.py
+++ b/solution.py
@@ -565,11 +565,17 @@
     )[0]
 
 
-def unpack(sums):
-    def body(sums, full, half, quarter, eighth, whole, tall):
-        for part in range(5):
-            block = sums[:, part * 128 : part * 128 + 128]
-            whole[part * 512 : part * 512 + 512, :] = block.astype(F32)
+def unpack(mine, other):
+    def body(mine, other, full, half, quarter, eighth, whole, tall):
+        even = lax.axis_index("c") == 0
+        count, size = mine.shape[0], mine.shape[1]
+        for at in range(count):
+            own, partner = mine[at].astype(F32), other[at].astype(F32)
+            for core in range(2):
+                chunk = jnp.where(even, *((own, partner) if core == 0 else (partner, own)))
+                for part in range(5):
+                    row = part * 512 + (2 * at + core) * size
+                    whole[row : row + size, :] = chunk[:, part * 128 : part * 128 + 128]
 
         def spread(out, source, chans):
             for down in range(3):
@@ -596,7 +602,7 @@
 
     outs = [((432, 16), F32), ((432, 32), F32), ((864, 64), F32), ((1728, 128), F32)]
     scratch = [((2560, 128), F32), ((864, 128), F32)]
-    return call(body, outs, scratch, 1 << 20, sums)
+    return call(body, outs, scratch, 1 << 20, mine, other)
 
 
 def pairs(axis):
@@ -687,7 +693,8 @@
     done = jnp.sum(pieces.reshape(second, -1, width), axis=0)
     spread = jnp.broadcast_to(done[None], (second,) + done.shape).reshape(rows, width)
     part = lax.all_to_all(lax.optimization_barrier(spread), outer, 0, 0, tiled=True)
-    return lax.all_to_all(copies(part, first), inner, 0, 0).reshape(terms.shape)
+    mine = lax.all_to_all(copies(part, lax.axis_size("x")), "x", 0, 0)
+    return mine, lax.ppermute(mine, "c", [(0, 1), (1, 0)])
 
 
 def on_device(
@@ -741,7 +748,7 @@
         dense2, halo_z, halo_y, skip1, halo_z1, halo_y1, pre1, skip0, pre0,
         t2, t1, shifts1, shifts0, grad3, grad2,
     )
-    outs = unpack(summed(terms))
+    outs = unpack(*summed(terms))
     return tuple(out.reshape(kernel.shape) for out, kernel in zip(outs, kernels))
 
 

time: 166 us -> 165 us (level)
  blocking collectives: 92.9 us -> 84.1 us
  starting transfers between devices: 46.1 us -> 52.8 us
    all_to_all x1, blocking collectives: 17 us -> 8.25 us  [summed(): mine = lax.all_to_all(copies(part, lax.axis_size('x')), 'x', 0, 0)]
    ppermute x0 -> x1, starting transfers between devices: none -> 6.71 us  [summed(): return (mine, lax.ppermute(mine, 'c', [(0, 1), (1, 0)]))]
  transfers between devices with their start and end apart: 14 -> 15, of which waited for: 7 -> 8; matrix products, arithmetic and copies ran while one was open for 1% -> 1% of each run, Pallas kernels for 1% -> 1%
where the time goes in v7:
time: 165 us; the launch traced here: 164 us
  blocking collectives  84.1 us (51%)
  starting transfers between devices  52.8 us (32%)
  waiting for transfers between devices  11.8 us (7%)
  Pallas kernels  11.7 us (7%)
  local copies, waits for them, and re-layouts  1.68 us (1%)
    ppermute x7, starting transfers between devices, swaps(): lax.ppermute(to_one, axis, first)  29.5 us
    all_to_all x1, blocking collectives, summed(): pieces = lax.all_to_all(terms.reshape(first, rows, width), inner, 0, 0)  25.5 us
    all_to_all x1, blocking collectives, summed(): pieces = lax.all_to_all(part, outer, 0, 0, tiled=True)  19.2 us
    ppermute x7, starting transfers between devices, swaps(): lax.ppermute(to_two, axis, second)  16.6 us
    all_to_all x1, blocking collectives, on_device(): lax.all_to_all(lax.optimization_barrier(jnp.broadcast_to(act3[None], many...  15.7 us
    all_to_all x1, blocking collectives, summed(): lax.all_to_all(lax.optimization_barrier(spread), outer, 0, 0, tiled=True)  15.6 us
    pallas_call x11, Pallas kernels, call(): pl.pallas_call(body, out_shape=tuple((jax.ShapeDtypeStruct(shape, dtype)...  11.7 us
    all_to_all x1, blocking collectives, summed(): mine = lax.all_to_all(copies(part, lax.axis_size('x')), 'x', 0, 0)  8.25 us
  transfers between devices with their start and end apart: 15, of which 8 were waited for; matrix products, arithmetic and copies ran while one was open for 1% of the time, Pallas kernels for 1%

profile of v7, /device:TPU:1, one launch (start us, length us, event | category | flops | bytes accessed | tf_op | source)
XLA Modules:
  0.0 164.3 jit_solution(5128940949527085531)
XLA Ops:
  0.7 0.9 broadcast_select_fusion
  1.6 8.8 %collective-permute-start = (bf16[1,128,128]{2,1,0:T(8,128)(2,1)S(1)}, bf16[1,128,128]{2,1,0:T(8,128)(2,1)S(1)}, u32[]{:S(2)}, u32[]{:S(2)}) collective-permute-start(bf16[1,128,128]{2,1,0:T(8,128)(2,1)S(1)} %bitcast.45), channel_id=1, source_target_pairs={{0,8},{8,0},{16,24},{24,16},{32,40},{40,32},{48,56},{56,48},{64,72... | collective-permute-start | bytes 98312 | tf_op jit(solution)/shard_map/ppermute | solution.py:616
  10.4 1.9 %collective-permute-start.1 = (bf16[1,128,128]{2,1,0:T(8,128)(2,1)S(1)}, bf16[1,128,128]{2,1,0:T(8,128)(2,1)S(1)}, u32[]{:S(2)}, u32[]{:S(2)}) collective-permute-start(bf16[1,128,128]{2,1,0:T(8,128)(2,1)S(1)} %bitcast.46), channel_id=1, source_target_pairs={{8,16},{24,32},{40,48},{56,64},{72,80},{88,96},{104,112},{120,128}... | collective-permute-start | bytes 98312 | tf_op jit(solution)/shard_map/ppermute | solution.py:616
  12.3 1.1 copy.18
  13.5 2.2 %collective-permute-done.1.two = bf16[1,128,128]{2,1,0:T(8,128)(2,1)S(1)} collective-permute-done((bf16[1,128,128]{2,1,0:T(8,128)(2,1)S(1)}, bf16[1,128,128]{2,1,0:T(8,128)(2,1)S(1)}, u32[]{:S(2)}, u32[]{:S(2)}) %collective-permute-start.1) | collective-permute-done | bytes 32800 | tf_op jit(solution)/shard_map/ppermute | solution.py:616
  15.7 1.9 %collective-permute-start.2 = (bf16[160,128]{1,0:T(8,128)(2,1)S(1)}, bf16[160,128]{1,0:T(8,128)(2,1)S(1)}, u32[]{:S(2)}, u32[]{:S(2)}) collective-permute-start(bf16[160,128]{1,0:T(8,128)(2,1)S(1)} %get-tuple-element.43), channel_id=1, source_target_pairs={{0,1},{1,0},{2,3},{3,2},{4,5},{5,4},{6,7},{7,6},{8,9},{9,8},{10,11... | collective-permute-start | bytes 122888 | tf_op jit(solution)/shard_map/ppermute | solution.py:616
  18.4 1.3 shard_map.121
  19.7 0.7 collective-permute-done.2.above
  20.4 0.9 shard_map.122
  21.4 1.9 %collective-permute-start.4 = (bf16[336,128]{1,0:T(8,128)(2,1)S(1)}, bf16[336,128]{1,0:T(8,128)(2,1)S(1)}, u32[]{:S(2)}, u32[]{:S(2)}) collective-permute-start(bf16[336,128]{1,0:T(8,128)(2,1)S(1)} %get-tuple-element.52), channel_id=1, source_target_pairs={{0,8},{8,0},{16,24},{24,16},{32,40},{40,32},{48,56},{56,48},{64,72... | collective-permute-start | bytes 258056 | tf_op jit(solution)/shard_map/ppermute | solution.py:616
  23.3 3.1 %collective-permute-start.5 = (bf16[336,128]{1,0:T(8,128)(2,1)S(1)}, bf16[336,128]{1,0:T(8,128)(2,1)S(1)}, u32[]{:S(2)}, u32[]{:S(2)}) collective-permute-start(bf16[336,128]{1,0:T(8,128)(2,1)S(1)} %get-tuple-element.53), channel_id=1, source_target_pairs={{8,16},{24,32},{40,48},{56,64},{72,80},{88,96},{104,112},{120,128}... | collective-permute-start | bytes 258056 | tf_op jit(solution)/shard_map/ppermute | solution.py:616
  26.4 2.7 %collective-permute-done.5.two.skip_two.two1 = bf16[336,128]{1,0:T(8,128)(2,1)S(1)} collective-permute-done((bf16[336,128]{1,0:T(8,128)(2,1)S(1)}, bf16[336,128]{1,0:T(8,128)(2,1)S(1)}, u32[]{:S(2)}, u32[]{:S(2)}) %collective-permute-start.5) | collective-permute-done | bytes 86048 | tf_op jit(solution)/shard_map/ppermute | solution.py:616
  29.2 5.3 %collective-permute-start.6 = (bf16[384,128]{1,0:T(8,128)(2,1)S(1)}, bf16[384,128]{1,0:T(8,128)(2,1)S(1)}, u32[]{:S(2)}, u32[]{:S(2)}) collective-permute-start(bf16[384,128]{1,0:T(8,128)(2,1)S(1)} %get-tuple-element.54), channel_id=1, source_target_pairs={{0,1},{1,0},{2,3},{3,2},{4,5},{5,4},{6,7},{7,6},{8,9},{9,8},{10,11... | collective-permute-start | bytes 294920 | tf_op jit(solution)/shard_map/ppermute | solution.py:616
  35.2 1.3 collective-permute-done.6.above.skip_above.above1
  36.5 2.0 %shard_map.124 = (f32[8,256,128]{2,1,0:T(8,128)S(1)}, bf16[4,128,128]{2,1,0:T(8,128)(2,1)S(1)}, f32[2,128,128]{2,1,0:T(8,128)S(1)}, f32[8,128]{1,0:T(8,128)S(1)}, bf16[3,160,1280]{2,1,0:T(8,128)(2,1)S(1)}) custom-call(bf16[4,64,128]{2,1,0:T(8,128)(2,1)S(1)} %get-tuple-element.51.act.own, bf16[336,128]{1,0:T(8,128)(2,1)S(1)} %collective-permute-done.4.one.skip_one.one1, ...), custom_call_target="tpu_custom_call" | custom-call | flops 536870912 | bytes 1048576 | tf_op jit(solution)/shard_map/pallas_call | solution.py:16
  38.5 15.7 %all_to_all.35.acts = f32[16,8,128]{2,1,0:T(8,128)S(1)} all-to-all(f32[16,8,128]{2,1,0:T(8,128)S(1)} %broadcast_in_dim.2), channel_id=1, replica_groups=mesh['x'=4,'z'=8,'c'=2,'gy'=8] {'c','gy'}, dimensions={0} | all-to-all | bytes 131072 | tf_op jit(solution)/shard_map/all_to_all | solution.py:735
  54.2 5.3 %collective-permute-start.8 = (f32[16,8,128]{2,1,0:T(8,128)S(1)}, f32[16,8,128]{2,1,0:T(8,128)S(1)}, u32[]{:S(2)}, u32[]{:S(2)}) collective-permute-start(f32[16,8,128]{2,1,0:T(8,128)S(1)} %all_to_all.35.acts), channel_id=1, source_target_pairs={{0,16},{16,0},{32,48},{48,32},{64,80},{80,64},{96,112},{112,96},{1... | collective-permute-start | bytes 196616 | tf_op jit(solution)/shard_map/ppermute | solution.py:616
  60.2 1.0 collective-permute-done.8.chip_one
  61.1 1.7 %shard_map.125 = (bf16[1,128,128]{2,1,0:T(8,128)(2,1)S(1)}, bf16[2,128,128]{2,1,0:T(8,128)(2,1)S(1)}, bf16[9,320,128]{2,1,0:T(8,128)(2,1)S(1)}, bf16[128,128]{1,0:T(8,128)(2,1)S(1)}) custom-call(f32[16,8,128]{2,1,0:T(8,128)S(1)} %all_to_all.35.acts, f32[16,8,128]{2,1,0:T(8,128)S(1)} %collective-permute-done.8.chip_one, ...), custom_call_target="tpu_custom_call" | custom-call | flops 268435456 | bytes 1048576 | tf_op jit(solution)/shard_map/pallas_call | solution.py:16
  62.8 3.7 %collective-permute-start.10 = (bf16[1,128,128]{2,1,0:T(8,128)(2,1)S(1)}, bf16[1,128,128]{2,1,0:T(8,128)(2,1)S(1)}, u32[]{:S(2)}, u32[]{:S(2)}) collective-permute-start(bf16[1,128,128]{2,1,0:T(8,128)(2,1)S(1)} %get-tuple-element.62.own), channel_id=1, source_target_pairs={{0,8},{8,0},{16,24},{24,16},{32,40},{40,32},{48,56},{56,48},{64,72... | collective-permute-start | bytes 98312 | tf_op jit(solution)/shard_map/ppermute | solution.py:616
  66.5 9.0 %collective-permute-start.11 = (bf16[1,128,128]{2,1,0:T(8,128)(2,1)S(1)}, bf16[1,128,128]{2,1,0:T(8,128)(2,1)S(1)}, u32[]{:S(2)}, u32[]{:S(2)}) collective-permute-start(bf16[1,128,128]{2,1,0:T(8,128)(2,1)S(1)} %get-tuple-element.62.own), channel_id=1, source_target_pairs={{8,16},{24,32},{40,48},{56,64},{72,80},{88,96},{104,112},{120,128}... | collective-permute-start | bytes 98312 | tf_op jit(solution)/shard_map/ppermute | solution.py:616
  75.5 1.6 collective-permute-done.11.two
  77.1 2.6 %collective-permute-start.12 = (bf16[384,128]{1,0:T(8,128)(2,1)S(1)}, bf16[384,128]{1,0:T(8,128)(2,1)S(1)}, u32[]{:S(2)}, u32[]{:S(2)}) collective-permute-start(bf16[384,128]{1,0:T(8,128)(2,1)S(1)} %bitcast.43), channel_id=1, source_target_pairs={{0,1},{1,0},{2,3},{3,2},{4,5},{5,4},{6,7},{7,6},{8,9},{9,8},{10,11... | collective-permute-start | bytes 294920 | tf_op jit(solution)/shard_map/ppermute | solution.py:616
  81.3 1.1 collective-permute-done.12.above
  82.5 3.5 %shard_map.128 = bf16[512,640]{1,0:T(8,128)(2,1)S(1)} custom-call(bf16[1,128,128]{2,1,0:T(8,128)(2,1)S(1)} %get-tuple-element.62.own, bf16[1,128,128]{2,1,0:T(8,128)(2,1)S(1)} %collective-permute-done.10.one, bf16[1,128,128]{2,1,0:T(8,128)(2,1)S(1)} %collective-permute-done.11.two, bf16[384,128]{1,0:T(8,128)(2,1)S(1)} %collective-permute-done.12.above, ...), custom_call_target="tpu_custom_call" | custom-call | flops 1073741824 | bytes 1048576 | tf_op jit(solution)/shard_map/pallas_call | solution.py:16
  85.9 25.5 %all_to_all.36 = bf16[8,64,640]{2,1,0:T(8,128)(2,1)S(1)} all-to-all(bf16[8,64,640]{2,1,0:T(8,128)(2,1)S(1)} %bitcast.25), channel_id=1, replica_groups=mesh['x'=4,'z'=8,'c'=2,'gy'=8] {'x','c'}, dimensions={0} | all-to-all | bytes 1310720 | tf_op jit(solution)/shard_map/all_to_all | solution.py:690
  111.6 19.2 %all_to_all.37 = f32[64,1,640]{2,1,0:T(1,128)S(1)} all-to-all(f32[64,1,640]{2,1,0:T(1,128)S(1)} %all_to_all.24), channel_id=1, replica_groups=mesh['x'=4,'z'=8,'c'=2,'gy'=8] {'z','gy'}, dimensions={0} | all-to-all | bytes 327680 | tf_op jit(solution)/shard_map/all_to_all | solution.py:692
  131.0 15.6 %all_to_all.38 = f32[64,1,640]{2,1,0:T(1,128)S(1)} all-to-all(f32[64,1,640]{2,1,0:T(1,128)S(1)} %all_to_all.26), channel_id=1, replica_groups=mesh['x'=4,'z'=8,'c'=2,'gy'=8] {'z','gy'}, dimensions={0} | all-to-all | bytes 327680 | tf_op jit(solution)/shard_map/all_to_all | solution.py:695
  146.7 8.3 %all_to_all.39.mine = bf16[4,64,640]{2,1,0:T(8,128)(2,1)S(1)} all-to-all(bf16[4,64,640]{2,1,0:T(8,128)(2,1)S(1)} %shard_map.129), channel_id=1, replica_groups=mesh['x'=4,'z'=8,'c'=2,'gy'=8] {'x'}, dimensions={0} | all-to-all | bytes 655360 | tf_op jit(solution)/shard_map/all_to_all | solution.py:696
  154.9 6.7 %collective-permute-start.14 = (bf16[4,64,640]{2,1,0:T(8,128)(2,1)S(1)}, bf16[4,64,640]{2,1,0:T(8,128)(2,1)S(1)}, u32[]{:S(2)}, u32[]{:S(2)}) collective-permute-start(bf16[4,64,640]{2,1,0:T(8,128)(2,1)S(1)} %all_to_all.39.mine), channel_id=1, source_target_pairs={{0,8},{8,0},{1,9},{9,1},{2,10},{10,2},{3,11},{11,3},{4,12},{12,4},... | collective-permute-start | bytes 983048 | tf_op jit(solution)/shard_map/ppermute | solution.py:697
  161.7 1.2 collective-permute-done.14.other
  162.9 1.4 shard_map.130
  (45 shorter events, 4.4 us)
Async XLA Ops:
  0.6 17.7 %copy-start.2 = (bf16[3,3,3,16,16]{4,3,2,1,0:T(8,128)(2,1)S(1)}, bf16[3,3,3,16,16]{4,3,2,1,0:T(8,128)(2,1)}, u32[]{:S(2)}) copy-start(bf16[3,3,3,16,16]{4,3,2,1,0:T(8,128)(2,1)} %param.10) | copy-start | bytes 41476
  0.6 17.7 %copy-start.3 = (bf16[3,3,3,16,32]{4,3,2,1,0:T(8,128)(2,1)S(1)}, bf16[3,3,3,16,32]{4,3,2,1,0:T(8,128)(2,1)}, u32[]{:S(2)}) copy-start(bf16[3,3,3,16,32]{4,3,2,1,0:T(8,128)(2,1)} %param.11) | copy-start | bytes 82948
  0.7 17.7 %copy-start.1 = (bf16[3,3,3,32,64]{4,3,2,1,0:T(8,128)(2,1)S(1)}, bf16[3,3,3,32,64]{4,3,2,1,0:T(8,128)(2,1)}, u32[]{:S(2)}) copy-start(bf16[3,3,3,32,64]{4,3,2,1,0:T(8,128)(2,1)} %param.12) | copy-start | bytes 331780
  0.7 17.7 %copy-start = (bf16[3,3,3,64,128]{4,3,2,1,0:T(8,128)(2,1)S(1)}, bf16[3,3,3,64,128]{4,3,2,1,0:T(8,128)(2,1)}, u32[]{:S(2)}) copy-start(bf16[3,3,3,64,128]{4,3,2,1,0:T(8,128)(2,1)} %param.13) | copy-start | bytes 1327108
  0.7 17.6 %copy-start.7 = (bf16[32,4,4,64]{3,2,1,0:T(4,128)(2,1)S(1)}, bf16[32,4,4,64]{3,2,1,0:T(4,128)(2,1)}, u32[]{:S(2)}) copy-start(bf16[32,4,4,64]{3,2,1,0:T(4,128)(2,1)} %param.15) | copy-start | bytes 196612
  1.6 18.8 %copy-start.5 = (bf16[128,1,1,16]{0,3,2,1:T(8,128)(2,1)S(1)}, bf16[128,1,1,16]{0,3,2,1:T(8,128)(2,1)}, u32[]{:S(2)}) copy-start(bf16[128,1,1,16]{0,3,2,1:T(8,128)(2,1)} %param.17) | copy-start | bytes 12292
  1.6 11.9 %collective-permute-start = (bf16[1,128,128]{2,1,0:T(8,128)(2,1)S(1)}, bf16[1,128,128]{2,1,0:T(8,128)(2,1)S(1)}, u32[]{:S(2)}, u32[]{:S(2)}) collective-permute-start(bf16[1,128,128]{2,1,0:T(8,128)(2,1)S(1)} %bitcast.45), channel_id=1, source_target_pairs={{0,8},{8,0},{16,24},{24,16},{32,40},{40,32},{48,56},{56,48},{64,72... | collective-permute-start | bytes 98312 | tf_op jit(solution)/shard_map/ppermute | solution.py:616
  10.4 5.2 %collective-permute-start.1 = (bf16[1,128,128]{2,1,0:T(8,128)(2,1)S(1)}, bf16[1,128,128]{2,1,0:T(8,128)(2,1)S(1)}, u32[]{:S(2)}, u32[]{:S(2)}) collective-permute-start(bf16[1,128,128]{2,1,0:T(8,128)(2,1)S(1)} %bitcast.46), channel_id=1, source_target_pairs={{8,16},{24,32},{40,48},{56,64},{72,80},{88,96},{104,112},{120,128}... | collective-permute-start | bytes 98312 | tf_op jit(solution)/shard_map/ppermute | solution.py:616
  15.7 4.7 %collective-permute-start.2 = (bf16[160,128]{1,0:T(8,128)(2,1)S(1)}, bf16[160,128]{1,0:T(8,128)(2,1)S(1)}, u32[]{:S(2)}, u32[]{:S(2)}) collective-permute-start(bf16[160,128]{1,0:T(8,128)(2,1)S(1)} %get-tuple-element.43), channel_id=1, source_target_pairs={{0,1},{1,0},{2,3},{3,2},{4,5},{5,4},{6,7},{7,6},{8,9},{9,8},{10,11... | collective-permute-start | bytes 122888 | tf_op jit(solution)/shard_map/ppermute | solution.py:616
  17.6 2.8 %collective-permute-start.3 = (bf16[160,128]{1,0:T(8,128)(2,1)S(1)}, bf16[160,128]{1,0:T(8,128)(2,1)S(1)}, u32[]{:S(2)}, u32[]{:S(2)}) collective-permute-start(bf16[160,128]{1,0:T(8,128)(2,1)S(1)} %get-tuple-element.44), channel_id=1, source_target_pairs={{1,2},{3,4},{5,6},{2,1},{4,3},{6,5},{9,10},{11,12},{13,14},{10,9},... | collective-permute-start | bytes 122888 | tf_op jit(solution)/shard_map/ppermute | solution.py:616
  21.4 5.0 %collective-permute-start.4 = (bf16[336,128]{1,0:T(8,128)(2,1)S(1)}, bf16[336,128]{1,0:T(8,128)(2,1)S(1)}, u32[]{:S(2)}, u32[]{:S(2)}) collective-permute-start(bf16[336,128]{1,0:T(8,128)(2,1)S(1)} %get-tuple-element.52), channel_id=1, source_target_pairs={{0,8},{8,0},{16,24},{24,16},{32,40},{40,32},{48,56},{56,48},{64,72... | collective-permute-start | bytes 258056 | tf_op jit(solution)/shard_map/ppermute | solution.py:616
  23.3 5.8 %collective-permute-start.5 = (bf16[336,128]{1,0:T(8,128)(2,1)S(1)}, bf16[336,128]{1,0:T(8,128)(2,1)S(1)}, u32[]{:S(2)}, u32[]{:S(2)}) collective-permute-start(bf16[336,128]{1,0:T(8,128)(2,1)S(1)} %get-tuple-element.53), channel_id=1, source_target_pairs={{8,16},{24,32},{40,48},{56,64},{72,80},{88,96},{104,112},{120,128}... | collective-permute-start | bytes 258056 | tf_op jit(solution)/shard_map/ppermute | solution.py:616
  29.1 32.0 %copy-start.4 = (bf16[64,2,2,32]{0,3,2,1:T(8,128)(2,1)S(1)}, bf16[64,2,2,32]{0,3,2,1:T(8,128)(2,1)}, u32[]{:S(2)}) copy-start(bf16[64,2,2,32]{0,3,2,1:T(8,128)(2,1)} %param.16) | copy-start | bytes 49156
  29.2 7.3 %collective-permute-start.6 = (bf16[384,128]{1,0:T(8,128)(2,1)S(1)}, bf16[384,128]{1,0:T(8,128)(2,1)S(1)}, u32[]{:S(2)}, u32[]{:S(2)}) collective-permute-start(bf16[384,128]{1,0:T(8,128)(2,1)S(1)} %get-tuple-element.54), channel_id=1, source_target_pairs={{0,1},{1,0},{2,3},{3,2},{4,5},{5,4},{6,7},{7,6},{8,9},{9,8},{10,11... | collective-permute-start | bytes 294920 | tf_op jit(solution)/shard_map/ppermute | solution.py:616
  34.5 2.0 %collective-permute-start.7 = (bf16[384,128]{1,0:T(8,128)(2,1)S(1)}, bf16[384,128]{1,0:T(8,128)(2,1)S(1)}, u32[]{:S(2)}, u32[]{:S(2)}) collective-permute-start(bf16[384,128]{1,0:T(8,128)(2,1)S(1)} %get-tuple-element.55), channel_id=1, source_target_pairs={{1,2},{3,4},{5,6},{2,1},{4,3},{6,5},{9,10},{11,12},{13,14},{10,9},... | collective-permute-start | bytes 294920 | tf_op jit(solution)/shard_map/ppermute | solution.py:616
  38.5 41.9 %copy-start.6 = (bf16[16,8,8,128]{3,2,1,0:T(8,128)(2,1)S(1)}, bf16[16,8,8,128]{3,2,1,0:T(8,128)(2,1)}, u32[]{:S(2)}) copy-start(bf16[16,8,8,128]{3,2,1,0:T(8,128)(2,1)} %param.14) | copy-start | bytes 786436
  54.2 7.0 %collective-permute-start.8 = (f32[16,8,128]{2,1,0:T(8,128)S(1)}, f32[16,8,128]{2,1,0:T(8,128)S(1)}, u32[]{:S(2)}, u32[]{:S(2)}) collective-permute-start(f32[16,8,128]{2,1,0:T(8,128)S(1)} %all_to_all.35.acts), channel_id=1, source_target_pairs={{0,16},{16,0},{32,48},{48,32},{64,80},{80,64},{96,112},{112,96},{1... | collective-permute-start | bytes 196616 | tf_op jit(solution)/shard_map/ppermute | solution.py:616
  59.5 1.6 %collective-permute-start.9 = (f32[16,8,128]{2,1,0:T(8,128)S(1)}, f32[16,8,128]{2,1,0:T(8,128)S(1)}, u32[]{:S(2)}, u32[]{:S(2)}) collective-permute-start(f32[16,8,128]{2,1,0:T(8,128)S(1)} %all_to_all.35.acts), channel_id=1, source_target_pairs={{16,32},{48,64},{80,96},{112,128},{144,160},{176,192},{208,224},{2... | collective-permute-start | bytes 196616 | tf_op jit(solution)/shard_map/ppermute | solution.py:616
  62.8 12.7 %collective-permute-start.10 = (bf16[1,128,128]{2,1,0:T(8,128)(2,1)S(1)}, bf16[1,128,128]{2,1,0:T(8,128)(2,1)S(1)}, u32[]{:S(2)}, u32[]{:S(2)}) collective-permute-start(bf16[1,128,128]{2,1,0:T(8,128)(2,1)S(1)} %get-tuple-element.62.own), channel_id=1, source_target_pairs={{0,8},{8,0},{16,24},{24,16},{32,40},{40,32},{48,56},{56,48},{64,72... | collective-permute-start | bytes 98312 | tf_op jit(solution)/shard_map/ppermute | solution.py:616
  66.5 10.6 %collective-permute-start.11 = (bf16[1,128,128]{2,1,0:T(8,128)(2,1)S(1)}, bf16[1,128,128]{2,1,0:T(8,128)(2,1)S(1)}, u32[]{:S(2)}, u32[]{:S(2)}) collective-permute-start(bf16[1,128,128]{2,1,0:T(8,128)(2,1)S(1)} %get-tuple-element.62.own), channel_id=1, source_target_pairs={{8,16},{24,32},{40,48},{56,64},{72,80},{88,96},{104,112},{120,128}... | collective-permute-start | bytes 98312 | tf_op jit(solution)/shard_map/ppermute | solution.py:616
  77.1 5.4 %collective-permute-start.12 = (bf16[384,128]{1,0:T(8,128)(2,1)S(1)}, bf16[384,128]{1,0:T(8,128)(2,1)S(1)}, u32[]{:S(2)}, u32[]{:S(2)}) collective-permute-start(bf16[384,128]{1,0:T(8,128)(2,1)S(1)} %bitcast.43), channel_id=1, source_target_pairs={{0,1},{1,0},{2,3},{3,2},{4,5},{5,4},{6,7},{7,6},{8,9},{9,8},{10,11... | collective-permute-start | bytes 294920 | tf_op jit(solution)/shard_map/ppermute | solution.py:616
  79.7 2.8 %collective-permute-start.13 = (bf16[384,128]{1,0:T(8,128)(2,1)S(1)}, bf16[384,128]{1,0:T(8,128)(2,1)S(1)}, u32[]{:S(2)}, u32[]{:S(2)}) collective-permute-start(bf16[384,128]{1,0:T(8,128)(2,1)S(1)} %bitcast.44), channel_id=1, source_target_pairs={{1,2},{3,4},{5,6},{2,1},{4,3},{6,5},{9,10},{11,12},{13,14},{10,9},... | collective-permute-start | bytes 294920 | tf_op jit(solution)/shard_map/ppermute | solution.py:616
  154.9 8.0 %collective-permute-start.14 = (bf16[4,64,640]{2,1,0:T(8,128)(2,1)S(1)}, bf16[4,64,640]{2,1,0:T(8,128)(2,1)S(1)}, u32[]{:S(2)}, u32[]{:S(2)}) collective-permute-start(bf16[4,64,640]{2,1,0:T(8,128)(2,1)S(1)} %all_to_all.39.mine), channel_id=1, source_target_pairs={{0,8},{8,0},{1,9},{9,1},{2,10},{10,2},{3,11},{11,3},{4,12},{12,4},... | collective-permute-start | bytes 983048 | tf_op jit(solution)/shard_map/ppermute | solution.py:697

commit v8 on v7

--- a/solution.py
+++ b/solution.py
@@ -481,16 +481,17 @@
         even = flags[4] == 0
         for layer in range(6):
             block = layer // 2
-            high, low = row_edges(above, below, block * 128, 128)
+            high, low = row_edges(above, below, block // 2 * 128, 128)
             middle = own[0]
             if block != 1:
                 near, far = (two, one) if block == 0 else (one, two)
                 middle = jnp.where(even, near[0], far[0])
-                other = row_edges(above, below, (2 - block) * 128, 128)
+                other = row_edges(above, below, (2 - block) // 2 * 128, 128)
                 high, low = jnp.where(even, other[0], high), jnp.where(even, other[1], low)
             tiles = (high, middle, low)
             for part, tile in enumerate(tiles):
-                tile = turned(tile.astype(F32), -32 * (layer % 2))
+                start = 64 if block == 1 and part != 1 else 0
+                tile = turned(tile.astype(F32), -start - 32 * (layer % 2))
                 tile = jnp.where(lanes(tile.shape) < 32, tile, 0.0).astype(BF16)
                 put_shifts(moved2, part * 128, layer, tile)
         value = convolved(taps2, moved2, (0, 384), 4)
@@ -668,6 +669,15 @@
     )
 
 
+def side_by_side(one, own, two):
+    def body(one, own, two, out):
+        moved = pltpu.roll(own[0].astype(F32), 64, 1)
+        out[:128] = (one[0].astype(F32) + moved).astype(BF16)
+        out[128:] = two[0]
+
+    return call(body, [((256, 128), BF16)], [], 1 << 20, one, own, two)[0]
+
+
 def laid_out(array):
     chans, depth, height, width = array.shape
     rows = jnp.transpose(array, (1, 2, 0, 3)).reshape(depth, height * chans, width)
@@ -740,7 +750,7 @@
         columns, acts, chips, skip3, halo_z1, halo_y1, skip2, pre2, w3, t3
     )
     halo_z = one, two = swaps(dense2, dense2)
-    block = jnp.concatenate([one, dense2, two], axis=0).reshape(384, 128)
+    block = side_by_side(one, dense2, two)
     halo_y = swaps(block, block, "gy")
     grad3 = grad_deepest(shifts3, delta3)
     grad2 = grad_quarter_of(act2, delta2)

time: 165 us -> 165 us (level)
    pallas_call x11 -> x12, Pallas kernels: 11.7 us -> 11.8 us  [call(): pl.pallas_call(body, out_shape=tuple((jax.ShapeDtypeStruct(shape, dtype)...]
where the time goes in v8:
time: 165 us; the launch traced here: 164 us
  blocking collectives  84.1 us (51%)
  starting transfers between devices  52.8 us (32%)
  Pallas kernels  11.8 us (7%)
  waiting for transfers between devices  11.5 us (7%)
  local copies, waits for them, and re-layouts  1.68 us (1%)
    ppermute x7, starting transfers between devices, swaps(): lax.ppermute(to_one, axis, first)  29.5 us
    all_to_all x1, blocking collectives, summed(): pieces = lax.all_to_all(terms.reshape(first, rows, width), inner, 0, 0)  25.4 us
    all_to_all x1, blocking collectives, summed(): pieces = lax.all_to_all(part, outer, 0, 0, tiled=True)  19.2 us
    ppermute x7, starting transfers between devices, swaps(): lax.ppermute(to_two, axis, second)  16.6 us
    all_to_all x1, blocking collectives, on_device(): lax.all_to_all(lax.optimization_barrier(jnp.broadcast_to(act3[None], many...  15.7 us
    all_to_all x1, blocking collectives, summed(): lax.all_to_all(lax.optimization_barrier(spread), outer, 0, 0, tiled=True)  15.6 us
    pallas_call x12, Pallas kernels, call(): pl.pallas_call(body, out_shape=tuple((jax.ShapeDtypeStruct(shape, dtype)...  11.8 us
    all_to_all x1, blocking collectives, summed(): mine = lax.all_to_all(copies(part, lax.axis_size('x')), 'x', 0, 0)  8.25 us
  transfers between devices with their start and end apart: 15, of which 8 were waited for; matrix products, arithmetic and copies ran while one was open for 1% of the time, Pallas kernels for 1%

profile of v8, /device:TPU:1, one launch (start us, length us, event | category | flops | bytes accessed | tf_op | source)
XLA Modules:
  0.0 164.0 jit_solution(2322309755105491652)
XLA Ops:
  0.7 0.9 broadcast_select_fusion
  1.6 8.8 %collective-permute-start = (bf16[1,128,128]{2,1,0:T(8,128)(2,1)S(1)}, bf16[1,128,128]{2,1,0:T(8,128)(2,1)S(1)}, u32[]{:S(2)}, u32[]{:S(2)}) collective-permute-start(bf16[1,128,128]{2,1,0:T(8,128)(2,1)S(1)} %bitcast.42), channel_id=1, source_target_pairs={{0,8},{8,0},{16,24},{24,16},{32,40},{40,32},{48,56},{56,48},{64,72... | collective-permute-start | bytes 98312 | tf_op jit(solution)/shard_map/ppermute | solution.py:617
  10.4 1.9 %collective-permute-start.1 = (bf16[1,128,128]{2,1,0:T(8,128)(2,1)S(1)}, bf16[1,128,128]{2,1,0:T(8,128)(2,1)S(1)}, u32[]{:S(2)}, u32[]{:S(2)}) collective-permute-start(bf16[1,128,128]{2,1,0:T(8,128)(2,1)S(1)} %bitcast.43), channel_id=1, source_target_pairs={{8,16},{24,32},{40,48},{56,64},{72,80},{88,96},{104,112},{120,128}... | collective-permute-start | bytes 98312 | tf_op jit(solution)/shard_map/ppermute | solution.py:617
  12.3 1.1 copy.18
  13.5 2.2 %collective-permute-done.1.two = bf16[1,128,128]{2,1,0:T(8,128)(2,1)S(1)} collective-permute-done((bf16[1,128,128]{2,1,0:T(8,128)(2,1)S(1)}, bf16[1,128,128]{2,1,0:T(8,128)(2,1)S(1)}, u32[]{:S(2)}, u32[]{:S(2)}) %collective-permute-start.1) | collective-permute-done | bytes 32800 | tf_op jit(solution)/shard_map/ppermute | solution.py:617
  15.7 1.9 %collective-permute-start.2 = (bf16[160,128]{1,0:T(8,128)(2,1)S(1)}, bf16[160,128]{1,0:T(8,128)(2,1)S(1)}, u32[]{:S(2)}, u32[]{:S(2)}) collective-permute-start(bf16[160,128]{1,0:T(8,128)(2,1)S(1)} %get-tuple-element.43), channel_id=1, source_target_pairs={{0,1},{1,0},{2,3},{3,2},{4,5},{5,4},{6,7},{7,6},{8,9},{9,8},{10,11... | collective-permute-start | bytes 122888 | tf_op jit(solution)/shard_map/ppermute | solution.py:617
  18.4 1.3 shard_map.121
  19.7 0.7 collective-permute-done.2.above
  20.4 0.9 shard_map.122
  21.4 1.9 %collective-permute-start.4 = (bf16[336,128]{1,0:T(8,128)(2,1)S(1)}, bf16[336,128]{1,0:T(8,128)(2,1)S(1)}, u32[]{:S(2)}, u32[]{:S(2)}) collective-permute-start(bf16[336,128]{1,0:T(8,128)(2,1)S(1)} %get-tuple-element.52), channel_id=1, source_target_pairs={{0,8},{8,0},{16,24},{24,16},{32,40},{40,32},{48,56},{56,48},{64,72... | collective-permute-start | bytes 258056 | tf_op jit(solution)/shard_map/ppermute | solution.py:617
  23.3 3.1 %collective-permute-start.5 = (bf16[336,128]{1,0:T(8,128)(2,1)S(1)}, bf16[336,128]{1,0:T(8,128)(2,1)S(1)}, u32[]{:S(2)}, u32[]{:S(2)}) collective-permute-start(bf16[336,128]{1,0:T(8,128)(2,1)S(1)} %get-tuple-element.53), channel_id=1, source_target_pairs={{8,16},{24,32},{40,48},{56,64},{72,80},{88,96},{104,112},{120,128}... | collective-permute-start | bytes 258056 | tf_op jit(solution)/shard_map/ppermute | solution.py:617
  26.4 2.7 %collective-permute-done.5.two.skip_two.two1 = bf16[336,128]{1,0:T(8,128)(2,1)S(1)} collective-permute-done((bf16[336,128]{1,0:T(8,128)(2,1)S(1)}, bf16[336,128]{1,0:T(8,128)(2,1)S(1)}, u32[]{:S(2)}, u32[]{:S(2)}) %collective-permute-start.5) | collective-permute-done | bytes 86048 | tf_op jit(solution)/shard_map/ppermute | solution.py:617
  29.2 5.3 %collective-permute-start.6 = (bf16[384,128]{1,0:T(8,128)(2,1)S(1)}, bf16[384,128]{1,0:T(8,128)(2,1)S(1)}, u32[]{:S(2)}, u32[]{:S(2)}) collective-permute-start(bf16[384,128]{1,0:T(8,128)(2,1)S(1)} %get-tuple-element.54), channel_id=1, source_target_pairs={{0,1},{1,0},{2,3},{3,2},{4,5},{5,4},{6,7},{7,6},{8,9},{9,8},{10,11... | collective-permute-start | bytes 294920 | tf_op jit(solution)/shard_map/ppermute | solution.py:617
  35.2 1.3 collective-permute-done.6.above.skip_above.above1
  36.5 2.0 %shard_map.124 = (f32[8,256,128]{2,1,0:T(8,128)S(1)}, bf16[4,128,128]{2,1,0:T(8,128)(2,1)S(1)}, f32[2,128,128]{2,1,0:T(8,128)S(1)}, f32[8,128]{1,0:T(8,128)S(1)}, bf16[3,160,1280]{2,1,0:T(8,128)(2,1)S(1)}) custom-call(bf16[4,64,128]{2,1,0:T(8,128)(2,1)S(1)} %get-tuple-element.51.act.own, bf16[336,128]{1,0:T(8,128)(2,1)S(1)} %collective-permute-done.4.one.skip_one.one1, ...), custom_call_target="tpu_custom_call" | custom-call | flops 536870912 | bytes 1048576 | tf_op jit(solution)/shard_map/pallas_call | solution.py:16
  38.5 15.7 %all_to_all.35.acts = f32[16,8,128]{2,1,0:T(8,128)S(1)} all-to-all(f32[16,8,128]{2,1,0:T(8,128)S(1)} %broadcast_in_dim.2), channel_id=1, replica_groups=mesh['x'=4,'z'=8,'c'=2,'gy'=8] {'c','gy'}, dimensions={0} | all-to-all | bytes 131072 | tf_op jit(solution)/shard_map/all_to_all | solution.py:745
  54.2 5.3 %collective-permute-start.8 = (f32[16,8,128]{2,1,0:T(8,128)S(1)}, f32[16,8,128]{2,1,0:T(8,128)S(1)}, u32[]{:S(2)}, u32[]{:S(2)}) collective-permute-start(f32[16,8,128]{2,1,0:T(8,128)S(1)} %all_to_all.35.acts), channel_id=1, source_target_pairs={{0,16},{16,0},{32,48},{48,32},{64,80},{80,64},{96,112},{112,96},{1... | collective-permute-start | bytes 196616 | tf_op jit(solution)/shard_map/ppermute | solution.py:617
  60.2 1.0 collective-permute-done.8.chip_one
  61.1 1.7 %shard_map.125 = (bf16[1,128,128]{2,1,0:T(8,128)(2,1)S(1)}, bf16[2,128,128]{2,1,0:T(8,128)(2,1)S(1)}, bf16[9,320,128]{2,1,0:T(8,128)(2,1)S(1)}, bf16[128,128]{1,0:T(8,128)(2,1)S(1)}) custom-call(f32[16,8,128]{2,1,0:T(8,128)S(1)} %all_to_all.35.acts, f32[16,8,128]{2,1,0:T(8,128)S(1)} %collective-permute-done.8.chip_one, ...), custom_call_target="tpu_custom_call" | custom-call | flops 268435456 | bytes 1048576 | tf_op jit(solution)/shard_map/pallas_call | solution.py:16
  62.8 3.7 %collective-permute-start.10 = (bf16[1,128,128]{2,1,0:T(8,128)(2,1)S(1)}, bf16[1,128,128]{2,1,0:T(8,128)(2,1)S(1)}, u32[]{:S(2)}, u32[]{:S(2)}) collective-permute-start(bf16[1,128,128]{2,1,0:T(8,128)(2,1)S(1)} %get-tuple-element.62.own), channel_id=1, source_target_pairs={{0,8},{8,0},{16,24},{24,16},{32,40},{40,32},{48,56},{56,48},{64,72... | collective-permute-start | bytes 98312 | tf_op jit(solution)/shard_map/ppermute | solution.py:617
  66.5 9.0 %collective-permute-start.11 = (bf16[1,128,128]{2,1,0:T(8,128)(2,1)S(1)}, bf16[1,128,128]{2,1,0:T(8,128)(2,1)S(1)}, u32[]{:S(2)}, u32[]{:S(2)}) collective-permute-start(bf16[1,128,128]{2,1,0:T(8,128)(2,1)S(1)} %get-tuple-element.62.own), channel_id=1, source_target_pairs={{8,16},{24,32},{40,48},{56,64},{72,80},{88,96},{104,112},{120,128}... | collective-permute-start | bytes 98312 | tf_op jit(solution)/shard_map/ppermute | solution.py:617
  75.5 1.6 collective-permute-done.11.two
  77.2 2.6 %collective-permute-start.12 = (bf16[256,128]{1,0:T(8,128)(2,1)S(1)}, bf16[256,128]{1,0:T(8,128)(2,1)S(1)}, u32[]{:S(2)}, u32[]{:S(2)}) collective-permute-start(bf16[256,128]{1,0:T(8,128)(2,1)S(1)} %shard_map.126), channel_id=1, source_target_pairs={{0,1},{1,0},{2,3},{3,2},{4,5},{5,4},{6,7},{7,6},{8,9},{9,8},{10,11... | collective-permute-start | bytes 196616 | tf_op jit(solution)/shard_map/ppermute | solution.py:617
  81.4 0.8 collective-permute-done.12.above
  82.2 3.5 %shard_map.129 = bf16[512,640]{1,0:T(8,128)(2,1)S(1)} custom-call(bf16[1,128,128]{2,1,0:T(8,128)(2,1)S(1)} %get-tuple-element.62.own, bf16[1,128,128]{2,1,0:T(8,128)(2,1)S(1)} %collective-permute-done.10.one, bf16[1,128,128]{2,1,0:T(8,128)(2,1)S(1)} %collective-permute-done.11.two, bf16[256,128]{1,0:T(8,128)(2,1)S(1)} %collective-permute-done.12.above, ...), custom_call_target="tpu_custom_call" | custom-call | flops 1073741824 | bytes 1048576 | tf_op jit(solution)/shard_map/pallas_call | solution.py:16
  85.7 25.4 %all_to_all.36 = bf16[8,64,640]{2,1,0:T(8,128)(2,1)S(1)} all-to-all(bf16[8,64,640]{2,1,0:T(8,128)(2,1)S(1)} %bitcast.24), channel_id=1, replica_groups=mesh['x'=4,'z'=8,'c'=2,'gy'=8] {'x','c'}, dimensions={0} | all-to-all | bytes 1310720 | tf_op jit(solution)/shard_map/all_to_all | solution.py:700
  111.3 19.2 %all_to_all.37 = f32[64,1,640]{2,1,0:T(1,128)S(1)} all-to-all(f32[64,1,640]{2,1,0:T(1,128)S(1)} %all_to_all.24), channel_id=1, replica_groups=mesh['x'=4,'z'=8,'c'=2,'gy'=8] {'z','gy'}, dimensions={0} | all-to-all | bytes 327680 | tf_op jit(solution)/shard_map/all_to_all | solution.py:702
  130.8 15.6 %all_to_all.38 = f32[64,1,640]{2,1,0:T(1,128)S(1)} all-to-all(f32[64,1,640]{2,1,0:T(1,128)S(1)} %all_to_all.26), channel_id=1, replica_groups=mesh['x'=4,'z'=8,'c'=2,'gy'=8] {'z','gy'}, dimensions={0} | all-to-all | bytes 327680 | tf_op jit(solution)/shard_map/all_to_all | solution.py:705
  146.4 8.3 %all_to_all.39.mine = bf16[4,64,640]{2,1,0:T(8,128)(2,1)S(1)} all-to-all(bf16[4,64,640]{2,1,0:T(8,128)(2,1)S(1)} %shard_map.130), channel_id=1, replica_groups=mesh['x'=4,'z'=8,'c'=2,'gy'=8] {'x'}, dimensions={0} | all-to-all | bytes 655360 | tf_op jit(solution)/shard_map/all_to_all | solution.py:706
  154.7 6.7 %collective-permute-start.14 = (bf16[4,64,640]{2,1,0:T(8,128)(2,1)S(1)}, bf16[4,64,640]{2,1,0:T(8,128)(2,1)S(1)}, u32[]{:S(2)}, u32[]{:S(2)}) collective-permute-start(bf16[4,64,640]{2,1,0:T(8,128)(2,1)S(1)} %all_to_all.39.mine), channel_id=1, source_target_pairs={{0,8},{8,0},{1,9},{9,1},{2,10},{10,2},{3,11},{11,3},{4,12},{12,4},... | collective-permute-start | bytes 983048 | tf_op jit(solution)/shard_map/ppermute | solution.py:707
  161.4 1.2 collective-permute-done.14.other
  162.6 1.4 shard_map.131
  (45 shorter events, 4.4 us)
Async XLA Ops:
  0.6 17.7 %copy-start.2 = (bf16[3,3,3,16,16]{4,3,2,1,0:T(8,128)(2,1)S(1)}, bf16[3,3,3,16,16]{4,3,2,1,0:T(8,128)(2,1)}, u32[]{:S(2)}) copy-start(bf16[3,3,3,16,16]{4,3,2,1,0:T(8,128)(2,1)} %param.10) | copy-start | bytes 41476
  0.6 17.7 %copy-start.3 = (bf16[3,3,3,16,32]{4,3,2,1,0:T(8,128)(2,1)S(1)}, bf16[3,3,3,16,32]{4,3,2,1,0:T(8,128)(2,1)}, u32[]{:S(2)}) copy-start(bf16[3,3,3,16,32]{4,3,2,1,0:T(8,128)(2,1)} %param.11) | copy-start | bytes 82948
  0.7 17.7 %copy-start.1 = (bf16[3,3,3,32,64]{4,3,2,1,0:T(8,128)(2,1)S(1)}, bf16[3,3,3,32,64]{4,3,2,1,0:T(8,128)(2,1)}, u32[]{:S(2)}) copy-start(bf16[3,3,3,32,64]{4,3,2,1,0:T(8,128)(2,1)} %param.12) | copy-start | bytes 331780
  0.7 17.7 %copy-start = (bf16[3,3,3,64,128]{4,3,2,1,0:T(8,128)(2,1)S(1)}, bf16[3,3,3,64,128]{4,3,2,1,0:T(8,128)(2,1)}, u32[]{:S(2)}) copy-start(bf16[3,3,3,64,128]{4,3,2,1,0:T(8,128)(2,1)} %param.13) | copy-start | bytes 1327108
  0.7 17.6 %copy-start.7 = (bf16[32,4,4,64]{3,2,1,0:T(4,128)(2,1)S(1)}, bf16[32,4,4,64]{3,2,1,0:T(4,128)(2,1)}, u32[]{:S(2)}) copy-start(bf16[32,4,4,64]{3,2,1,0:T(4,128)(2,1)} %param.15) | copy-start | bytes 196612
  1.6 18.8 %copy-start.5 = (bf16[128,1,1,16]{0,3,2,1:T(8,128)(2,1)S(1)}, bf16[128,1,1,16]{0,3,2,1:T(8,128)(2,1)}, u32[]{:S(2)}) copy-start(bf16[128,1,1,16]{0,3,2,1:T(8,128)(2,1)} %param.17) | copy-start | bytes 12292
  1.6 11.9 %collective-permute-start = (bf16[1,128,128]{2,1,0:T(8,128)(2,1)S(1)}, bf16[1,128,128]{2,1,0:T(8,128)(2,1)S(1)}, u32[]{:S(2)}, u32[]{:S(2)}) collective-permute-start(bf16[1,128,128]{2,1,0:T(8,128)(2,1)S(1)} %bitcast.42), channel_id=1, source_target_pairs={{0,8},{8,0},{16,24},{24,16},{32,40},{40,32},{48,56},{56,48},{64,72... | collective-permute-start | bytes 98312 | tf_op jit(solution)/shard_map/ppermute | solution.py:617
  10.4 5.2 %collective-permute-start.1 = (bf16[1,128,128]{2,1,0:T(8,128)(2,1)S(1)}, bf16[1,128,128]{2,1,0:T(8,128)(2,1)S(1)}, u32[]{:S(2)}, u32[]{:S(2)}) collective-permute-start(bf16[1,128,128]{2,1,0:T(8,128)(2,1)S(1)} %bitcast.43), channel_id=1, source_target_pairs={{8,16},{24,32},{40,48},{56,64},{72,80},{88,96},{104,112},{120,128}... | collective-permute-start | bytes 98312 | tf_op jit(solution)/shard_map/ppermute | solution.py:617
  15.7 4.7 %collective-permute-start.2 = (bf16[160,128]{1,0:T(8,128)(2,1)S(1)}, bf16[160,128]{1,0:T(8,128)(2,1)S(1)}, u32[]{:S(2)}, u32[]{:S(2)}) collective-permute-start(bf16[160,128]{1,0:T(8,128)(2,1)S(1)} %get-tuple-element.43), channel_id=1, source_target_pairs={{0,1},{1,0},{2,3},{3,2},{4,5},{5,4},{6,7},{7,6},{8,9},{9,8},{10,11... | collective-permute-start | bytes 122888 | tf_op jit(solution)/shard_map/ppermute | solution.py:617
  17.6 2.8 %collective-permute-start.3 = (bf16[160,128]{1,0:T(8,128)(2,1)S(1)}, bf16[160,128]{1,0:T(8,128)(2,1)S(1)}, u32[]{:S(2)}, u32[]{:S(2)}) collective-permute-start(bf16[160,128]{1,0:T(8,128)(2,1)S(1)} %get-tuple-element.44), channel_id=1, source_target_pairs={{1,2},{3,4},{5,6},{2,1},{4,3},{6,5},{9,10},{11,12},{13,14},{10,9},... | collective-permute-start | bytes 122888 | tf_op jit(solution)/shard_map/ppermute | solution.py:617
  21.4 5.0 %collective-permute-start.4 = (bf16[336,128]{1,0:T(8,128)(2,1)S(1)}, bf16[336,128]{1,0:T(8,128)(2,1)S(1)}, u32[]{:S(2)}, u32[]{:S(2)}) collective-permute-start(bf16[336,128]{1,0:T(8,128)(2,1)S(1)} %get-tuple-element.52), channel_id=1, source_target_pairs={{0,8},{8,0},{16,24},{24,16},{32,40},{40,32},{48,56},{56,48},{64,72... | collective-permute-start | bytes 258056 | tf_op jit(solution)/shard_map/ppermute | solution.py:617
  23.3 5.8 %collective-permute-start.5 = (bf16[336,128]{1,0:T(8,128)(2,1)S(1)}, bf16[336,128]{1,0:T(8,128)(2,1)S(1)}, u32[]{:S(2)}, u32[]{:S(2)}) collective-permute-start(bf16[336,128]{1,0:T(8,128)(2,1)S(1)} %get-tuple-element.53), channel_id=1, source_target_pairs={{8,16},{24,32},{40,48},{56,64},{72,80},{88,96},{104,112},{120,128}... | collective-permute-start | bytes 258056 | tf_op jit(solution)/shard_map/ppermute | solution.py:617
  29.1 32.0 %copy-start.4 = (bf16[64,2,2,32]{0,3,2,1:T(8,128)(2,1)S(1)}, bf16[64,2,2,32]{0,3,2,1:T(8,128)(2,1)}, u32[]{:S(2)}) copy-start(bf16[64,2,2,32]{0,3,2,1:T(8,128)(2,1)} %param.16) | copy-start | bytes 49156
  29.2 7.3 %collective-permute-start.6 = (bf16[384,128]{1,0:T(8,128)(2,1)S(1)}, bf16[384,128]{1,0:T(8,128)(2,1)S(1)}, u32[]{:S(2)}, u32[]{:S(2)}) collective-permute-start(bf16[384,128]{1,0:T(8,128)(2,1)S(1)} %get-tuple-element.54), channel_id=1, source_target_pairs={{0,1},{1,0},{2,3},{3,2},{4,5},{5,4},{6,7},{7,6},{8,9},{9,8},{10,11... | collective-permute-start | bytes 294920 | tf_op jit(solution)/shard_map/ppermute | solution.py:617
  34.5 2.0 %collective-permute-start.7 = (bf16[384,128]{1,0:T(8,128)(2,1)S(1)}, bf16[384,128]{1,0:T(8,128)(2,1)S(1)}, u32[]{:S(2)}, u32[]{:S(2)}) collective-permute-start(bf16[384,128]{1,0:T(8,128)(2,1)S(1)} %get-tuple-element.55), channel_id=1, source_target_pairs={{1,2},{3,4},{5,6},{2,1},{4,3},{6,5},{9,10},{11,12},{13,14},{10,9},... | collective-permute-start | bytes 294920 | tf_op jit(solution)/shard_map/ppermute | solution.py:617
  38.5 41.9 %copy-start.6 = (bf16[16,8,8,128]{3,2,1,0:T(8,128)(2,1)S(1)}, bf16[16,8,8,128]{3,2,1,0:T(8,128)(2,1)}, u32[]{:S(2)}) copy-start(bf16[16,8,8,128]{3,2,1,0:T(8,128)(2,1)} %param.14) | copy-start | bytes 786436
  54.2 7.0 %collective-permute-start.8 = (f32[16,8,128]{2,1,0:T(8,128)S(1)}, f32[16,8,128]{2,1,0:T(8,128)S(1)}, u32[]{:S(2)}, u32[]{:S(2)}) collective-permute-start(f32[16,8,128]{2,1,0:T(8,128)S(1)} %all_to_all.35.acts), channel_id=1, source_target_pairs={{0,16},{16,0},{32,48},{48,32},{64,80},{80,64},{96,112},{112,96},{1... | collective-permute-start | bytes 196616 | tf_op jit(solution)/shard_map/ppermute | solution.py:617
  59.5 1.6 %collective-permute-start.9 = (f32[16,8,128]{2,1,0:T(8,128)S(1)}, f32[16,8,128]{2,1,0:T(8,128)S(1)}, u32[]{:S(2)}, u32[]{:S(2)}) collective-permute-start(f32[16,8,128]{2,1,0:T(8,128)S(1)} %all_to_all.35.acts), channel_id=1, source_target_pairs={{16,32},{48,64},{80,96},{112,128},{144,160},{176,192},{208,224},{2... | collective-permute-start | bytes 196616 | tf_op jit(solution)/shard_map/ppermute | solution.py:617
  62.8 12.7 %collective-permute-start.10 = (bf16[1,128,128]{2,1,0:T(8,128)(2,1)S(1)}, bf16[1,128,128]{2,1,0:T(8,128)(2,1)S(1)}, u32[]{:S(2)}, u32[]{:S(2)}) collective-permute-start(bf16[1,128,128]{2,1,0:T(8,128)(2,1)S(1)} %get-tuple-element.62.own), channel_id=1, source_target_pairs={{0,8},{8,0},{16,24},{24,16},{32,40},{40,32},{48,56},{56,48},{64,72... | collective-permute-start | bytes 98312 | tf_op jit(solution)/shard_map/ppermute | solution.py:617
  66.5 10.6 %collective-permute-start.11 = (bf16[1,128,128]{2,1,0:T(8,128)(2,1)S(1)}, bf16[1,128,128]{2,1,0:T(8,128)(2,1)S(1)}, u32[]{:S(2)}, u32[]{:S(2)}) collective-permute-start(bf16[1,128,128]{2,1,0:T(8,128)(2,1)S(1)} %get-tuple-element.62.own), channel_id=1, source_target_pairs={{8,16},{24,32},{40,48},{56,64},{72,80},{88,96},{104,112},{120,128}... | collective-permute-start | bytes 98312 | tf_op jit(solution)/shard_map/ppermute | solution.py:617
  77.2 5.0 %collective-permute-start.12 = (bf16[256,128]{1,0:T(8,128)(2,1)S(1)}, bf16[256,128]{1,0:T(8,128)(2,1)S(1)}, u32[]{:S(2)}, u32[]{:S(2)}) collective-permute-start(bf16[256,128]{1,0:T(8,128)(2,1)S(1)} %shard_map.126), channel_id=1, source_target_pairs={{0,1},{1,0},{2,3},{3,2},{4,5},{5,4},{6,7},{7,6},{8,9},{9,8},{10,11... | collective-permute-start | bytes 196616 | tf_op jit(solution)/shard_map/ppermute | solution.py:617
  79.7 2.4 %collective-permute-start.13 = (bf16[256,128]{1,0:T(8,128)(2,1)S(1)}, bf16[256,128]{1,0:T(8,128)(2,1)S(1)}, u32[]{:S(2)}, u32[]{:S(2)}) collective-permute-start(bf16[256,128]{1,0:T(8,128)(2,1)S(1)} %shard_map.126), channel_id=1, source_target_pairs={{1,2},{3,4},{5,6},{2,1},{4,3},{6,5},{9,10},{11,12},{13,14},{10,9},... | collective-permute-start | bytes 196616 | tf_op jit(solution)/shard_map/ppermute | solution.py:617
  154.7 8.0 %collective-permute-start.14 = (bf16[4,64,640]{2,1,0:T(8,128)(2,1)S(1)}, bf16[4,64,640]{2,1,0:T(8,128)(2,1)S(1)}, u32[]{:S(2)}, u32[]{:S(2)}) collective-permute-start(bf16[4,64,640]{2,1,0:T(8,128)(2,1)S(1)} %all_to_all.39.mine), channel_id=1, source_target_pairs={{0,8},{8,0},{1,9},{9,1},{2,10},{10,2},{3,11},{11,3},{4,12},{12,4},... | collective-permute-start | bytes 983048 | tf_op jit(solution)/shard_map/ppermute | solution.py:707
